TPU v7x, 32 devices: a whole 2x2x4 slice. The times are simulated.
32 devices in a mesh: stream: 8 (over z, y), span: 4 (over x, core).
Axes of the slice: x: 2, y: 2, z: 4, core: 2. Of those that a mesh axis runs over, the one named last changes fastest.
Arguments:
- rhs: float32 [32, 4, 64, 4096], P('stream', None, None, 'span'), may hold values from -0.15625 to 0.15625
- lagged: float32 [32, 4, 64, 4096], P('stream', None, None, 'span'), may hold values from -6 to 6
- face_types: int32 [3, 32, 4096], P(None, 'stream', 'span'), may hold values from 0 to 5
- stream_scale: float32 [32, 4096], P('stream', 'span'), may hold values from 1 to 4
- span_scale: float32 [2, 32, 4096], P(None, 'stream', 'span'), may hold values from 0.004 to 0.016
- absorb: float32 [32, 4096], P('stream', 'span'), may hold values from 0.002 to 0.008
- up_blocks: float32 [6, 64, 64], replicated, may hold values from -1 to 0.03
- down_blocks: float32 [6, 64, 64], replicated, may hold values from -1 to 0.03
- diag_inverse: float32 [64, 64], replicated, may hold values from -0.012 to 1
Outputs:
- increment: float32 [32, 4, 64, 4096], P('stream', None, None, 'span')
All inputs are finite; a program needn't handle non-finite values.
Results may differ from a plain program's by a relative error of at most 0.00023.
Values sent between devices are 32-bit elements; how exact they have to be, the bound alone decides.
No kernel may reach another device: no remote copies, remote signals or barrier semaphores. Data moves between devices by JAX's collectives and lax.ppermute only.
A program may use at most 64 MiB of HBM per device.

v0:
```python
import jax
import jax.numpy as jnp
from jax import lax
from jax.sharding import PartitionSpec as P

precise = lax.Precision.HIGHEST


def padded_2(block, sides, width):
    for axis, dim in sides:
        count = lax.axis_size(axis)
        forward = [(i, i + 1) for i in range(count - 1)]
        backward = [(target, source) for source, target in forward]
        low = lax.ppermute(
            lax.slice_in_dim(block, block.shape[dim] - width, None, axis=dim), axis, forward
        )
        high = lax.ppermute(lax.slice_in_dim(block, 0, width, axis=dim), axis, backward)
        block = jnp.concatenate([low, block, high], axis=dim)
    return block


def passed_along(block, axis, distance):
    devices = range(lax.axis_size(axis))
    route = [(i - distance, i) for i in devices if i - distance in devices]
    return lax.ppermute(block, axis, route)


def typed_product(blocks_table, type_ids, state_in):
    products = jnp.einsum("tpq,rqw->trpw", blocks_table, state_in, precision=precise)
    kinds = jnp.arange(blocks_table.shape[0], dtype=jnp.int32)
    selector = (type_ids[None, :] == kinds[:, None]).astype(jnp.float32)
    return jnp.sum(products * selector[:, None, None, :], axis=0)


def inverse_product(diag_inverse, balance, denom_row):
    return jnp.einsum("pq,rqw->rpw", diag_inverse, balance, precision=precise) / denom_row


def span_block(padded, face_types, span_scale, up_blocks, offset, breadth):
    lower_side = lax.dynamic_slice_in_dim(padded, offset, breadth, 3)
    upper_side = lax.dynamic_slice_in_dim(padded, offset + 2, breadth, 3)
    lower_types = face_types[1]
    upper_types = face_types[2]
    lower_scale = span_scale[0]
    upper_scale = span_scale[1]
    results = []
    for row_index in range(padded.shape[0]):
        lower_term = lower_scale[row_index] * typed_product(
            up_blocks, lower_types[row_index], lower_side[row_index]
        )
        upper_term = upper_scale[row_index] * typed_product(
            up_blocks, upper_types[row_index], upper_side[row_index]
        )
        results.append(lower_term + upper_term)
    return jnp.stack(results)


def per_device(
    rhs, lagged, face_types, stream_scale, span_scale, absorb, up_blocks, down_blocks, diag_inverse
):
    height = rhs.shape[0]
    columns = rhs.shape[3]
    padded = padded_2(lagged, (("span", 3),), 1)
    denominator = stream_scale + span_scale[0] + span_scale[1] + absorb
    blocks = 4
    breadth = columns // blocks
    length = lax.axis_size("stream")
    position = lax.axis_index("stream")
    whole_span = span_block(padded, face_types, span_scale, up_blocks, 0, columns)

    def span_part(offset):
        return lax.dynamic_slice_in_dim(whole_span, offset, breadth, 3)

    def forward_block(forward_part, inflow, offset):
        rhs_block = lax.dynamic_slice_in_dim(rhs, offset, breadth, 3)
        type_block = lax.dynamic_slice_in_dim(face_types[0], offset, breadth, 1)
        scale_block = lax.dynamic_slice_in_dim(stream_scale, offset, breadth, 1)
        denom_block = lax.dynamic_slice_in_dim(denominator, offset, breadth, 1)
        span_terms = span_part(offset)
        previous = inflow
        results = []
        for row_index in range(height):
            balance = (
                rhs_block[row_index]
                - span_terms[row_index]
                - scale_block[row_index] * typed_product(up_blocks, type_block[row_index], previous)
            )
            previous = inverse_product(diag_inverse, balance, denom_block[row_index])
            results.append(previous)
        forward_part = lax.dynamic_update_slice_in_dim(forward_part, jnp.stack(results), offset, 3)
        return (forward_part, previous)

    def forward_step(wave_step, state):
        forward_part, inflow = state
        block_index = wave_step - position
        active = (block_index >= 0) & (block_index < blocks)
        offset = jnp.clip(block_index, 0, blocks - 1) * breadth

        def forward_working(forward_part, inflow):
            return forward_block(forward_part, inflow, offset)

        def forward_waiting(forward_part, inflow):
            return (forward_part, jnp.zeros_like(inflow))

        forward_part, outflow = lax.cond(
            active, forward_working, forward_waiting, forward_part, inflow
        )
        inflow = passed_along(outflow, "stream", 1)
        return (forward_part, inflow)

    front_zero = jnp.zeros((rhs.shape[1], rhs.shape[2], breadth), jnp.float32)
    forward_part, unused = lax.fori_loop(
        0, length + blocks - 1, forward_step, (jnp.zeros_like(rhs), front_zero)
    )

    def backward_block(increment, inflow, offset):
        part_block = lax.dynamic_slice_in_dim(forward_part, offset, breadth, 3)
        type_block = lax.dynamic_slice_in_dim(face_types[0], offset, breadth, 1)
        scale_block = lax.dynamic_slice_in_dim(stream_scale, offset, breadth, 1)
        denom_block = lax.dynamic_slice_in_dim(denominator, offset, breadth, 1)
        carried = inflow
        results = []
        for row_index in reversed(range(height)):
            solved = part_block[row_index] - inverse_product(
                diag_inverse, carried, denom_block[row_index]
            )
            carried = scale_block[row_index] * typed_product(
                down_blocks, type_block[row_index], solved
            )
            results.append(solved)
        ordered = results[::-1]
        increment = lax.dynamic_update_slice_in_dim(increment, jnp.stack(ordered), offset, 3)
        return (increment, carried)

    def backward_step(wave_step, state):
        increment, inflow = state
        block_index = wave_step - (length - 1 - position)
        active = (block_index >= 0) & (block_index < blocks)
        offset = jnp.clip(block_index, 0, blocks - 1) * breadth

        def backward_working(increment, inflow):
            return backward_block(increment, inflow, offset)

        def backward_waiting(increment, inflow):
            return (increment, jnp.zeros_like(inflow))

        increment, outflow = lax.cond(active, backward_working, backward_waiting, increment, inflow)
        inflow = passed_along(outflow, "stream", -1)
        return (increment, inflow)

    increment, unused_two = lax.fori_loop(
        0, length + blocks - 1, backward_step, (jnp.zeros_like(rhs), front_zero)
    )
    return increment


def solution(mesh):
    return jax.shard_map(
        per_device,
        mesh=mesh,
        in_specs=(
            P("stream", None, None, "span"),
            P("stream", None, None, "span"),
            P(None, "stream", "span"),
            P("stream", "span"),
            P(None, "stream", "span"),
            P("stream", "span"),
            P(),
            P(),
            P(),
        ),
        out_specs=P("stream", None, None, "span"),
        check_vma=False,
    )
```

profile of v0, /device:TPU:0, one launch (start us, length us, event | category | flops | bytes accessed | tf_op | source)
XLA Modules:
  0.0 556.8 jit_solution(18102902180588325186)
XLA Ops:
  14.3 7.0 %fusion.86 = f32[4,64,1024]{2,1,0:T(8,128)S(1)} fusion(f32[6,1024]{1,0:T(8,128)S(1)} %fusion.114, f32[4,4,64,1025]{3,2,1,0:T(8,128)} %constant_dynamic-update-slice_fusion, f32[6,64,64]{2,1,0:T(8,128)S(1)} %copy-done.1), kind=kOutput, calls=%fused_computation.134 | convolution fusion | flops 1210843136 | bytes 2220032 | tf_op jit(solution)/shard_map/tpq,rqw->trpw/dot_general | solution.py:29
  21.3 7.1 %fusion.88 = f32[4,64,1024]{2,1,0:T(8,128)S(1)} fusion(f32[6,1024]{1,0:T(8,128)S(1)} %fusion.112, f32[4,4,64,1025]{3,2,1,0:T(8,128)} %constant_dynamic-update-slice_fusion, f32[6,64,64]{2,1,0:T(8,128)S(1)} %copy-done.1), kind=kOutput, calls=%fused_computation.138 | convolution fusion | flops 1210843136 | bytes 2220032 | tf_op jit(solution)/shard_map/tpq,rqw->trpw/dot_general | solution.py:29
  28.4 7.0 %fusion.82 = f32[4,64,1024]{2,1,0:T(8,128)S(1)} fusion(f32[6,1024]{1,0:T(8,128)S(1)} %fusion.118, f32[4,4,64,1025]{3,2,1,0:T(8,128)} %constant_dynamic-update-slice_fusion, f32[6,64,64]{2,1,0:T(8,128)S(1)} %copy-done.1), kind=kOutput, calls=%fused_computation.126 | convolution fusion | flops 1210843136 | bytes 2220032 | tf_op jit(solution)/shard_map/tpq,rqw->trpw/dot_general | solution.py:29
  35.4 7.0 %fusion.84 = f32[4,64,1024]{2,1,0:T(8,128)S(1)} fusion(f32[6,1024]{1,0:T(8,128)S(1)} %fusion.116, f32[4,4,64,1025]{3,2,1,0:T(8,128)} %constant_dynamic-update-slice_fusion, f32[6,64,64]{2,1,0:T(8,128)S(1)} %copy-done.1), kind=kOutput, calls=%fused_computation.130 | convolution fusion | flops 1210843136 | bytes 2220032 | tf_op jit(solution)/shard_map/tpq,rqw->trpw/dot_general | solution.py:29
  60.5 5.9 %fusion.85 = f32[4,64,1024]{2,1,0:T(8,128)S(1)} fusion(f32[6,1024]{1,0:T(8,128)S(1)} %fusion.115, f32[4,4,64,1024]{3,2,1,0:T(8,128)S(1)} %copy-done, f32[4,4,64,1]{3,2,1,0:T(8,128)S(1)} %collective-permute-done.2, f32[6,64,64]{2,1,0:T(8,128)S(1)} %copy-done.1), kind=kOutput, calls=%fused_computation.132 | convolution fusion | flops 1211105280 | bytes 5369856 | tf_op jit(solution)/shard_map/tpq,rqw->trpw/dot_general | solution.py:29
  71.9 214.5 %while.38 = (s32[]{:T(128)}, f32[4,4,64,1024]{3,2,1,0:T(8,128)}, f32[4,64,256]{2,1,0:T(8,128)S(1)}, s32[]{:T(128)}, f32[4,4,64,1024]{3,2,1,0:T(8,128)}, /*index=...) while((s32[]{:T(128)}, f32[4,4,64,1024]{3,2,1,0:T(8,128)}, ...), condition=%wide.region_15.16_spmd, body=%wide.region_8.15_spmd.sunk | while | flops 1414017024 | bytes 10015197 | solution.py:112
  71.9 14.4 %conditional.4 = (f32[4,4,64,1024]{3,2,1,0:T(8,128)}, f32[4,64,256]{2,1,0:T(8,128)}) conditional(s32[]{:T(128)} %convert_element_type.162, f32[4,4,64,1024]{3,2,1,0:T(8,128)} %get-tuple-element.802, (s32[]{:T(128)}, f32[4,4,64,1024]{3,2,1,0:T(8,128)}, f32[4,4,64,1024]{3,2,1,0:T(8,128)}, f32[4,1024]{1,0:T(4,128)S(1)}, f32[4,64,256]{2,1,0:T(8,128)S(1)}, ...), branch_computations={%region_9.9_spmd, %region_10.14_spmd} | conditional | flops 1414017024 | bytes 8966330 | solution.py:105
  92.7 14.4 %conditional.4 = (f32[4,4,64,1024]{3,2,1,0:T(8,128)}, f32[4,64,256]{2,1,0:T(8,128)}) conditional(s32[]{:T(128)} %convert_element_type.162, f32[4,4,64,1024]{3,2,1,0:T(8,128)} %get-tuple-element.802, (s32[]{:T(128)}, f32[4,4,64,1024]{3,2,1,0:T(8,128)}, f32[4,4,64,1024]{3,2,1,0:T(8,128)}, f32[4,1024]{1,0:T(4,128)S(1)}, f32[4,64,256]{2,1,0:T(8,128)S(1)}, ...), branch_computations={%region_9.9_spmd, %region_10.14_spmd} | conditional | flops 1414017024 | bytes 8966330 | solution.py:105
  111.4 6.3 %collective-permute-done = f32[4,64,256]{2,1,0:T(8,128)S(1)} collective-permute-done((f32[4,64,256]{2,1,0:T(8,128)}, f32[4,64,256]{2,1,0:T(8,128)S(1)}, u32[]{:S(2)}, u32[]{:S(2)}) %collective-permute-start) | collective-permute-done | bytes 262176 | tf_op jit(solution)/shard_map/while/body/eval_jaxpr/ppermute | solution.py:25
  117.7 14.4 %conditional.4 = (f32[4,4,64,1024]{3,2,1,0:T(8,128)}, f32[4,64,256]{2,1,0:T(8,128)}) conditional(s32[]{:T(128)} %convert_element_type.162, f32[4,4,64,1024]{3,2,1,0:T(8,128)} %get-tuple-element.802, (s32[]{:T(128)}, f32[4,4,64,1024]{3,2,1,0:T(8,128)}, f32[4,4,64,1024]{3,2,1,0:T(8,128)}, f32[4,1024]{1,0:T(4,128)S(1)}, f32[4,64,256]{2,1,0:T(8,128)S(1)}, ...), branch_computations={%region_9.9_spmd, %region_10.14_spmd} | conditional | flops 1414017024 | bytes 8966330 | solution.py:105
  136.4 6.5 %collective-permute-done = f32[4,64,256]{2,1,0:T(8,128)S(1)} collective-permute-done((f32[4,64,256]{2,1,0:T(8,128)}, f32[4,64,256]{2,1,0:T(8,128)S(1)}, u32[]{:S(2)}, u32[]{:S(2)}) %collective-permute-start) | collective-permute-done | bytes 262176 | tf_op jit(solution)/shard_map/while/body/eval_jaxpr/ppermute | solution.py:25
  143.0 14.4 %conditional.4 = (f32[4,4,64,1024]{3,2,1,0:T(8,128)}, f32[4,64,256]{2,1,0:T(8,128)}) conditional(s32[]{:T(128)} %convert_element_type.162, f32[4,4,64,1024]{3,2,1,0:T(8,128)} %get-tuple-element.802, (s32[]{:T(128)}, f32[4,4,64,1024]{3,2,1,0:T(8,128)}, f32[4,4,64,1024]{3,2,1,0:T(8,128)}, f32[4,1024]{1,0:T(4,128)S(1)}, f32[4,64,256]{2,1,0:T(8,128)S(1)}, ...), branch_computations={%region_9.9_spmd, %region_10.14_spmd} | conditional | flops 1414017024 | bytes 8966330 | solution.py:105
  168.1 17.9 %collective-permute-start = (f32[4,64,256]{2,1,0:T(8,128)}, f32[4,64,256]{2,1,0:T(8,128)S(1)}, u32[]{:S(2)}, u32[]{:S(2)}) collective-permute-start(f32[4,64,256]{2,1,0:T(8,128)} %get-tuple-element.766), channel_id=1, source_target_pairs={{0,4},{4,8},{8,12},{12,16},{16,20},{20,24},{24,28},{1,5},{5,9},{9,... | collective-permute-start | bytes 786440 | tf_op jit(solution)/shard_map/while/body/eval_jaxpr/ppermute | solution.py:25
  201.6 18.9 %collective-permute-start = (f32[4,64,256]{2,1,0:T(8,128)}, f32[4,64,256]{2,1,0:T(8,128)S(1)}, u32[]{:S(2)}, u32[]{:S(2)}) collective-permute-start(f32[4,64,256]{2,1,0:T(8,128)} %get-tuple-element.766), channel_id=1, source_target_pairs={{0,4},{4,8},{8,12},{12,16},{16,20},{20,24},{24,28},{1,5},{5,9},{9,... | collective-permute-start | bytes 786440 | tf_op jit(solution)/shard_map/while/body/eval_jaxpr/ppermute | solution.py:25
  235.5 15.0 %collective-permute-start = (f32[4,64,256]{2,1,0:T(8,128)}, f32[4,64,256]{2,1,0:T(8,128)S(1)}, u32[]{:S(2)}, u32[]{:S(2)}) collective-permute-start(f32[4,64,256]{2,1,0:T(8,128)} %get-tuple-element.766), channel_id=1, source_target_pairs={{0,4},{4,8},{8,12},{12,16},{16,20},{20,24},{24,28},{1,5},{5,9},{9,... | collective-permute-start | bytes 786440 | tf_op jit(solution)/shard_map/while/body/eval_jaxpr/ppermute | solution.py:25
  265.4 16.7 %collective-permute-start = (f32[4,64,256]{2,1,0:T(8,128)}, f32[4,64,256]{2,1,0:T(8,128)S(1)}, u32[]{:S(2)}, u32[]{:S(2)}) collective-permute-start(f32[4,64,256]{2,1,0:T(8,128)} %get-tuple-element.766), channel_id=1, source_target_pairs={{0,4},{4,8},{8,12},{12,16},{16,20},{20,24},{24,28},{1,5},{5,9},{9,... | collective-permute-start | bytes 786440 | tf_op jit(solution)/shard_map/while/body/eval_jaxpr/ppermute | solution.py:25
  288.9 267.5 %while.39 = (s32[]{:T(128)}, f32[4,4,64,1024]{3,2,1,0:T(8,128)}, f32[4,64,256]{2,1,0:T(8,128)S(1)}, s32[]{:T(128)}, f32[4,4,64,1024]{3,2,1,0:T(8,128)}, /*index=...) while((s32[]{:T(128)}, f32[4,4,64,1024]{3,2,1,0:T(8,128)}, ...), condition=%wide.region_23.24_spmd, body=%wide.region_16.23_spmd.sunk | while | flops 1413754880 | bytes 9490893 | solution.py:151
  290.5 8.2 %collective-permute-done.1 = f32[4,64,256]{2,1,0:T(8,128)S(1)} collective-permute-done((f32[4,64,256]{2,1,0:T(8,128)S(1)}, f32[4,64,256]{2,1,0:T(8,128)S(1)}, u32[]{:S(2)}, u32[]{:S(2)}) %collective-permute-start.1) | collective-permute-done | bytes 262176 | tf_op jit(solution)/shard_map/while/body/eval_jaxpr/ppermute | solution.py:25
  300.1 22.6 %collective-permute-done.1 = f32[4,64,256]{2,1,0:T(8,128)S(1)} collective-permute-done((f32[4,64,256]{2,1,0:T(8,128)S(1)}, f32[4,64,256]{2,1,0:T(8,128)S(1)}, u32[]{:S(2)}, u32[]{:S(2)}) %collective-permute-start.1) | collective-permute-done | bytes 262176 | tf_op jit(solution)/shard_map/while/body/eval_jaxpr/ppermute | solution.py:25
  324.1 7.0 %collective-permute-done.1 = f32[4,64,256]{2,1,0:T(8,128)S(1)} collective-permute-done((f32[4,64,256]{2,1,0:T(8,128)S(1)}, f32[4,64,256]{2,1,0:T(8,128)S(1)}, u32[]{:S(2)}, u32[]{:S(2)}) %collective-permute-start.1) | collective-permute-done | bytes 262176 | tf_op jit(solution)/shard_map/while/body/eval_jaxpr/ppermute | solution.py:25
  332.4 24.4 %collective-permute-done.1 = f32[4,64,256]{2,1,0:T(8,128)S(1)} collective-permute-done((f32[4,64,256]{2,1,0:T(8,128)S(1)}, f32[4,64,256]{2,1,0:T(8,128)S(1)}, u32[]{:S(2)}, u32[]{:S(2)}) %collective-permute-start.1) | collective-permute-done | bytes 262176 | tf_op jit(solution)/shard_map/while/body/eval_jaxpr/ppermute | solution.py:25
  358.2 8.7 %collective-permute-done.1 = f32[4,64,256]{2,1,0:T(8,128)S(1)} collective-permute-done((f32[4,64,256]{2,1,0:T(8,128)S(1)}, f32[4,64,256]{2,1,0:T(8,128)S(1)}, u32[]{:S(2)}, u32[]{:S(2)}) %collective-permute-start.1) | collective-permute-done | bytes 262176 | tf_op jit(solution)/shard_map/while/body/eval_jaxpr/ppermute | solution.py:25
  368.2 8.9 %collective-permute-done.1 = f32[4,64,256]{2,1,0:T(8,128)S(1)} collective-permute-done((f32[4,64,256]{2,1,0:T(8,128)S(1)}, f32[4,64,256]{2,1,0:T(8,128)S(1)}, u32[]{:S(2)}, u32[]{:S(2)}) %collective-permute-start.1) | collective-permute-done | bytes 262176 | tf_op jit(solution)/shard_map/while/body/eval_jaxpr/ppermute | solution.py:25
  378.4 92.8 %collective-permute-done.1 = f32[4,64,256]{2,1,0:T(8,128)S(1)} collective-permute-done((f32[4,64,256]{2,1,0:T(8,128)S(1)}, f32[4,64,256]{2,1,0:T(8,128)S(1)}, u32[]{:S(2)}, u32[]{:S(2)}) %collective-permute-start.1) | collective-permute-done | bytes 262176 | tf_op jit(solution)/shard_map/while/body/eval_jaxpr/ppermute | solution.py:25
  471.2 12.3 %conditional.5 = (f32[4,4,64,1024]{3,2,1,0:T(8,128)}, f32[4,64,256]{2,1,0:T(8,128)S(1)}) conditional(s32[]{:T(128)} %convert_element_type.163, f32[4,4,64,1024]{3,2,1,0:T(8,128)} %get-tuple-element.843, (s32[]{:T(128)}, f32[4,4,64,1024]{3,2,1,0:T(8,128)}, f32[4,1024]{1,0:T(4,128)S(1)}, f32[4,64,256]{2,1,0:T(8,128)S(1)}, f32[64,64]{1,0:T(8,128)S(1)}, ...), branch_computations={%region_17.17_spmd, %region_18.22_spmd} | conditional | flops 1413754880 | bytes 8442042 | solution.py:147
  484.9 7.9 %collective-permute-done.1 = f32[4,64,256]{2,1,0:T(8,128)S(1)} collective-permute-done((f32[4,64,256]{2,1,0:T(8,128)S(1)}, f32[4,64,256]{2,1,0:T(8,128)S(1)}, u32[]{:S(2)}, u32[]{:S(2)}) %collective-permute-start.1) | collective-permute-done | bytes 262176 | tf_op jit(solution)/shard_map/while/body/eval_jaxpr/ppermute | solution.py:25
  492.8 12.3 %conditional.5 = (f32[4,4,64,1024]{3,2,1,0:T(8,128)}, f32[4,64,256]{2,1,0:T(8,128)S(1)}) conditional(s32[]{:T(128)} %convert_element_type.163, f32[4,4,64,1024]{3,2,1,0:T(8,128)} %get-tuple-element.843, (s32[]{:T(128)}, f32[4,4,64,1024]{3,2,1,0:T(8,128)}, f32[4,1024]{1,0:T(4,128)S(1)}, f32[4,64,256]{2,1,0:T(8,128)S(1)}, f32[64,64]{1,0:T(8,128)S(1)}, ...), branch_computations={%region_17.17_spmd, %region_18.22_spmd} | conditional | flops 1413754880 | bytes 8442042 | solution.py:147
  506.5 7.8 %collective-permute-done.1 = f32[4,64,256]{2,1,0:T(8,128)S(1)} collective-permute-done((f32[4,64,256]{2,1,0:T(8,128)S(1)}, f32[4,64,256]{2,1,0:T(8,128)S(1)}, u32[]{:S(2)}, u32[]{:S(2)}) %collective-permute-start.1) | collective-permute-done | bytes 262176 | tf_op jit(solution)/shard_map/while/body/eval_jaxpr/ppermute | solution.py:25
  514.3 12.3 %conditional.5 = (f32[4,4,64,1024]{3,2,1,0:T(8,128)}, f32[4,64,256]{2,1,0:T(8,128)S(1)}) conditional(s32[]{:T(128)} %convert_element_type.163, f32[4,4,64,1024]{3,2,1,0:T(8,128)} %get-tuple-element.843, (s32[]{:T(128)}, f32[4,4,64,1024]{3,2,1,0:T(8,128)}, f32[4,1024]{1,0:T(4,128)S(1)}, f32[4,64,256]{2,1,0:T(8,128)S(1)}, f32[64,64]{1,0:T(8,128)S(1)}, ...), branch_computations={%region_17.17_spmd, %region_18.22_spmd} | conditional | flops 1413754880 | bytes 8442042 | solution.py:147
  527.9 7.9 %collective-permute-done.1 = f32[4,64,256]{2,1,0:T(8,128)S(1)} collective-permute-done((f32[4,64,256]{2,1,0:T(8,128)S(1)}, f32[4,64,256]{2,1,0:T(8,128)S(1)}, u32[]{:S(2)}, u32[]{:S(2)}) %collective-permute-start.1) | collective-permute-done | bytes 262176 | tf_op jit(solution)/shard_map/while/body/eval_jaxpr/ppermute | solution.py:25
  535.8 12.3 %conditional.5 = (f32[4,4,64,1024]{3,2,1,0:T(8,128)}, f32[4,64,256]{2,1,0:T(8,128)S(1)}) conditional(s32[]{:T(128)} %convert_element_type.163, f32[4,4,64,1024]{3,2,1,0:T(8,128)} %get-tuple-element.843, (s32[]{:T(128)}, f32[4,4,64,1024]{3,2,1,0:T(8,128)}, f32[4,1024]{1,0:T(4,128)S(1)}, f32[4,64,256]{2,1,0:T(8,128)S(1)}, f32[64,64]{1,0:T(8,128)S(1)}, ...), branch_computations={%region_17.17_spmd, %region_18.22_spmd} | conditional | flops 1413754880 | bytes 8442042 | solution.py:147
  549.4 7.0 %collective-permute-done.1 = f32[4,64,256]{2,1,0:T(8,128)S(1)} collective-permute-done((f32[4,64,256]{2,1,0:T(8,128)S(1)}, f32[4,64,256]{2,1,0:T(8,128)S(1)}, u32[]{:S(2)}, u32[]{:S(2)}) %collective-permute-start.1) | collective-permute-done | bytes 262176 | tf_op jit(solution)/shard_map/while/body/eval_jaxpr/ppermute | solution.py:25
  (227 shorter events, 241.1 us)
Async XLA Ops:
  1.4 12.0 %collective-permute-start.3 = (f32[4,4,64,1]{3,2,1,0:T(8,128)S(1)}, f32[4,4,64,1]{3,2,1,0:T(8,128)S(1)}, u32[]{:S(2)}, u32[]{:S(2)}) collective-permute-start(f32[4,4,64,1]{3,2,1,0:T(8,128)S(1)} %get-tuple-element.622), channel_id=1, source_target_pairs={{1,0},{2,1},{3,2},{5,4},{6,5},{7,6},{9,8},{10,9},{11,10},{13,12},{... | collective-permute-start | bytes 12296 | tf_op jit(solution)/shard_map/ppermute | solution.py:17
  2.7 39.7 %collective-permute-start.2 = (f32[4,4,64,1]{3,2,1,0:T(8,128)S(1)}, f32[4,4,64,1]{3,2,1,0:T(8,128)S(1)}, u32[]{:S(2)}, u32[]{:S(2)}) collective-permute-start(f32[4,4,64,1]{3,2,1,0:T(8,128)S(1)} %get-tuple-element.621), channel_id=1, source_target_pairs={{0,1},{1,2},{2,3},{4,5},{5,6},{6,7},{8,9},{9,10},{10,11},{12,13},{... | collective-permute-start | bytes 12296 | tf_op jit(solution)/shard_map/ppermute | solution.py:14
  8.5 5.8 %copy-start.1 = (f32[6,64,64]{2,1,0:T(8,128)S(1)}, f32[6,64,64]{2,1,0:T(8,128)}, u32[]{:S(2)}) copy-start(f32[6,64,64]{2,1,0:T(8,128)} %param.23) | copy-start | bytes 294916
  21.3 21.2 %copy-start = (f32[4,4,64,1024]{3,2,1,0:T(8,128)S(1)}, f32[4,4,64,1024]{3,2,1,0:T(8,128)}, u32[]{:S(2)}) copy-start(f32[4,4,64,1024]{3,2,1,0:T(8,128)} %param.18) | copy-start | bytes 12582916
  69.4 2.5 copy-start.2
  69.4 2.5 copy-start.3
  69.4 2.5 copy-start.5
  86.3 6.4 %collective-permute-start = (f32[4,64,256]{2,1,0:T(8,128)}, f32[4,64,256]{2,1,0:T(8,128)S(1)}, u32[]{:S(2)}, u32[]{:S(2)}) collective-permute-start(f32[4,64,256]{2,1,0:T(8,128)} %get-tuple-element.766), channel_id=1, source_target_pairs={{0,4},{4,8},{8,12},{12,16},{16,20},{20,24},{24,28},{1,5},{5,9},{9,... | collective-permute-start | bytes 786440 | tf_op jit(solution)/shard_map/while/body/eval_jaxpr/ppermute | solution.py:25
  107.1 10.6 %collective-permute-start = (f32[4,64,256]{2,1,0:T(8,128)}, f32[4,64,256]{2,1,0:T(8,128)S(1)}, u32[]{:S(2)}, u32[]{:S(2)}) collective-permute-start(f32[4,64,256]{2,1,0:T(8,128)} %get-tuple-element.766), channel_id=1, source_target_pairs={{0,4},{4,8},{8,12},{12,16},{16,20},{20,24},{24,28},{1,5},{5,9},{9,... | collective-permute-start | bytes 786440 | tf_op jit(solution)/shard_map/while/body/eval_jaxpr/ppermute | solution.py:25
  132.1 10.9 %collective-permute-start = (f32[4,64,256]{2,1,0:T(8,128)}, f32[4,64,256]{2,1,0:T(8,128)S(1)}, u32[]{:S(2)}, u32[]{:S(2)}) collective-permute-start(f32[4,64,256]{2,1,0:T(8,128)} %get-tuple-element.766), channel_id=1, source_target_pairs={{0,4},{4,8},{8,12},{12,16},{16,20},{20,24},{24,28},{1,5},{5,9},{9,... | collective-permute-start | bytes 786440 | tf_op jit(solution)/shard_map/while/body/eval_jaxpr/ppermute | solution.py:25
  157.4 10.0 %collective-permute-start = (f32[4,64,256]{2,1,0:T(8,128)}, f32[4,64,256]{2,1,0:T(8,128)S(1)}, u32[]{:S(2)}, u32[]{:S(2)}) collective-permute-start(f32[4,64,256]{2,1,0:T(8,128)} %get-tuple-element.766), channel_id=1, source_target_pairs={{0,4},{4,8},{8,12},{12,16},{16,20},{20,24},{24,28},{1,5},{5,9},{9,... | collective-permute-start | bytes 786440 | tf_op jit(solution)/shard_map/while/body/eval_jaxpr/ppermute | solution.py:25
  168.1 22.9 %collective-permute-start = (f32[4,64,256]{2,1,0:T(8,128)}, f32[4,64,256]{2,1,0:T(8,128)S(1)}, u32[]{:S(2)}, u32[]{:S(2)}) collective-permute-start(f32[4,64,256]{2,1,0:T(8,128)} %get-tuple-element.766), channel_id=1, source_target_pairs={{0,4},{4,8},{8,12},{12,16},{16,20},{20,24},{24,28},{1,5},{5,9},{9,... | collective-permute-start | bytes 786440 | tf_op jit(solution)/shard_map/while/body/eval_jaxpr/ppermute | solution.py:25
  191.7 9.2 %collective-permute-start = (f32[4,64,256]{2,1,0:T(8,128)}, f32[4,64,256]{2,1,0:T(8,128)S(1)}, u32[]{:S(2)}, u32[]{:S(2)}) collective-permute-start(f32[4,64,256]{2,1,0:T(8,128)} %get-tuple-element.766), channel_id=1, source_target_pairs={{0,4},{4,8},{8,12},{12,16},{16,20},{20,24},{24,28},{1,5},{5,9},{9,... | collective-permute-start | bytes 786440 | tf_op jit(solution)/shard_map/while/body/eval_jaxpr/ppermute | solution.py:25
  201.6 23.1 %collective-permute-start = (f32[4,64,256]{2,1,0:T(8,128)}, f32[4,64,256]{2,1,0:T(8,128)S(1)}, u32[]{:S(2)}, u32[]{:S(2)}) collective-permute-start(f32[4,64,256]{2,1,0:T(8,128)} %get-tuple-element.766), channel_id=1, source_target_pairs={{0,4},{4,8},{8,12},{12,16},{16,20},{20,24},{24,28},{1,5},{5,9},{9,... | collective-permute-start | bytes 786440 | tf_op jit(solution)/shard_map/while/body/eval_jaxpr/ppermute | solution.py:25
  225.4 9.4 %collective-permute-start = (f32[4,64,256]{2,1,0:T(8,128)}, f32[4,64,256]{2,1,0:T(8,128)S(1)}, u32[]{:S(2)}, u32[]{:S(2)}) collective-permute-start(f32[4,64,256]{2,1,0:T(8,128)} %get-tuple-element.766), channel_id=1, source_target_pairs={{0,4},{4,8},{8,12},{12,16},{16,20},{20,24},{24,28},{1,5},{5,9},{9,... | collective-permute-start | bytes 786440 | tf_op jit(solution)/shard_map/while/body/eval_jaxpr/ppermute | solution.py:25
  235.5 19.2 %collective-permute-start = (f32[4,64,256]{2,1,0:T(8,128)}, f32[4,64,256]{2,1,0:T(8,128)S(1)}, u32[]{:S(2)}, u32[]{:S(2)}) collective-permute-start(f32[4,64,256]{2,1,0:T(8,128)} %get-tuple-element.766), channel_id=1, source_target_pairs={{0,4},{4,8},{8,12},{12,16},{16,20},{20,24},{24,28},{1,5},{5,9},{9,... | collective-permute-start | bytes 786440 | tf_op jit(solution)/shard_map/while/body/eval_jaxpr/ppermute | solution.py:25
  255.3 9.4 %collective-permute-start = (f32[4,64,256]{2,1,0:T(8,128)}, f32[4,64,256]{2,1,0:T(8,128)S(1)}, u32[]{:S(2)}, u32[]{:S(2)}) collective-permute-start(f32[4,64,256]{2,1,0:T(8,128)} %get-tuple-element.766), channel_id=1, source_target_pairs={{0,4},{4,8},{8,12},{12,16},{16,20},{20,24},{24,28},{1,5},{5,9},{9,... | collective-permute-start | bytes 786440 | tf_op jit(solution)/shard_map/while/body/eval_jaxpr/ppermute | solution.py:25
  265.4 20.9 %collective-permute-start = (f32[4,64,256]{2,1,0:T(8,128)}, f32[4,64,256]{2,1,0:T(8,128)S(1)}, u32[]{:S(2)}, u32[]{:S(2)}) collective-permute-start(f32[4,64,256]{2,1,0:T(8,128)} %get-tuple-element.766), channel_id=1, source_target_pairs={{0,4},{4,8},{8,12},{12,16},{16,20},{20,24},{24,28},{1,5},{5,9},{9,... | collective-permute-start | bytes 786440 | tf_op jit(solution)/shard_map/while/body/eval_jaxpr/ppermute | solution.py:25
  286.3 2.6 copy-start.4
  289.2 9.5 %collective-permute-start.1 = (f32[4,64,256]{2,1,0:T(8,128)S(1)}, f32[4,64,256]{2,1,0:T(8,128)S(1)}, u32[]{:S(2)}, u32[]{:S(2)}) collective-permute-start(f32[4,64,256]{2,1,0:T(8,128)S(1)} %get-tuple-element.778), channel_id=1, source_target_pairs={{4,0},{8,4},{12,8},{16,12},{20,16},{24,20},{28,24},{5,1},{9,5},{13... | collective-permute-start | bytes 786440 | tf_op jit(solution)/shard_map/while/body/eval_jaxpr/ppermute | solution.py:25
  298.8 23.9 %collective-permute-start.1 = (f32[4,64,256]{2,1,0:T(8,128)S(1)}, f32[4,64,256]{2,1,0:T(8,128)S(1)}, u32[]{:S(2)}, u32[]{:S(2)}) collective-permute-start(f32[4,64,256]{2,1,0:T(8,128)S(1)} %get-tuple-element.778), channel_id=1, source_target_pairs={{4,0},{8,4},{12,8},{16,12},{20,16},{24,20},{28,24},{5,1},{9,5},{13... | collective-permute-start | bytes 786440 | tf_op jit(solution)/shard_map/while/body/eval_jaxpr/ppermute | solution.py:25
  322.8 8.3 %collective-permute-start.1 = (f32[4,64,256]{2,1,0:T(8,128)S(1)}, f32[4,64,256]{2,1,0:T(8,128)S(1)}, u32[]{:S(2)}, u32[]{:S(2)}) collective-permute-start(f32[4,64,256]{2,1,0:T(8,128)S(1)} %get-tuple-element.778), channel_id=1, source_target_pairs={{4,0},{8,4},{12,8},{16,12},{20,16},{24,20},{28,24},{5,1},{9,5},{13... | collective-permute-start | bytes 786440 | tf_op jit(solution)/shard_map/while/body/eval_jaxpr/ppermute | solution.py:25
  331.1 25.7 %collective-permute-start.1 = (f32[4,64,256]{2,1,0:T(8,128)S(1)}, f32[4,64,256]{2,1,0:T(8,128)S(1)}, u32[]{:S(2)}, u32[]{:S(2)}) collective-permute-start(f32[4,64,256]{2,1,0:T(8,128)S(1)} %get-tuple-element.778), channel_id=1, source_target_pairs={{4,0},{8,4},{12,8},{16,12},{20,16},{24,20},{28,24},{5,1},{9,5},{13... | collective-permute-start | bytes 786440 | tf_op jit(solution)/shard_map/while/body/eval_jaxpr/ppermute | solution.py:25
  356.9 10.0 %collective-permute-start.1 = (f32[4,64,256]{2,1,0:T(8,128)S(1)}, f32[4,64,256]{2,1,0:T(8,128)S(1)}, u32[]{:S(2)}, u32[]{:S(2)}) collective-permute-start(f32[4,64,256]{2,1,0:T(8,128)S(1)} %get-tuple-element.778), channel_id=1, source_target_pairs={{4,0},{8,4},{12,8},{16,12},{20,16},{24,20},{28,24},{5,1},{9,5},{13... | collective-permute-start | bytes 786440 | tf_op jit(solution)/shard_map/while/body/eval_jaxpr/ppermute | solution.py:25
  366.9 10.2 %collective-permute-start.1 = (f32[4,64,256]{2,1,0:T(8,128)S(1)}, f32[4,64,256]{2,1,0:T(8,128)S(1)}, u32[]{:S(2)}, u32[]{:S(2)}) collective-permute-start(f32[4,64,256]{2,1,0:T(8,128)S(1)} %get-tuple-element.778), channel_id=1, source_target_pairs={{4,0},{8,4},{12,8},{16,12},{20,16},{24,20},{28,24},{5,1},{9,5},{13... | collective-permute-start | bytes 786440 | tf_op jit(solution)/shard_map/while/body/eval_jaxpr/ppermute | solution.py:25
  377.1 94.1 %collective-permute-start.1 = (f32[4,64,256]{2,1,0:T(8,128)S(1)}, f32[4,64,256]{2,1,0:T(8,128)S(1)}, u32[]{:S(2)}, u32[]{:S(2)}) collective-permute-start(f32[4,64,256]{2,1,0:T(8,128)S(1)} %get-tuple-element.778), channel_id=1, source_target_pairs={{4,0},{8,4},{12,8},{16,12},{20,16},{24,20},{28,24},{5,1},{9,5},{13... | collective-permute-start | bytes 786440 | tf_op jit(solution)/shard_map/while/body/eval_jaxpr/ppermute | solution.py:25
  483.6 9.2 %collective-permute-start.1 = (f32[4,64,256]{2,1,0:T(8,128)S(1)}, f32[4,64,256]{2,1,0:T(8,128)S(1)}, u32[]{:S(2)}, u32[]{:S(2)}) collective-permute-start(f32[4,64,256]{2,1,0:T(8,128)S(1)} %get-tuple-element.778), channel_id=1, source_target_pairs={{4,0},{8,4},{12,8},{16,12},{20,16},{24,20},{28,24},{5,1},{9,5},{13... | collective-permute-start | bytes 786440 | tf_op jit(solution)/shard_map/while/body/eval_jaxpr/ppermute | solution.py:25
  505.1 9.1 %collective-permute-start.1 = (f32[4,64,256]{2,1,0:T(8,128)S(1)}, f32[4,64,256]{2,1,0:T(8,128)S(1)}, u32[]{:S(2)}, u32[]{:S(2)}) collective-permute-start(f32[4,64,256]{2,1,0:T(8,128)S(1)} %get-tuple-element.778), channel_id=1, source_target_pairs={{4,0},{8,4},{12,8},{16,12},{20,16},{24,20},{28,24},{5,1},{9,5},{13... | collective-permute-start | bytes 786440 | tf_op jit(solution)/shard_map/while/body/eval_jaxpr/ppermute | solution.py:25
  526.6 9.2 %collective-permute-start.1 = (f32[4,64,256]{2,1,0:T(8,128)S(1)}, f32[4,64,256]{2,1,0:T(8,128)S(1)}, u32[]{:S(2)}, u32[]{:S(2)}) collective-permute-start(f32[4,64,256]{2,1,0:T(8,128)S(1)} %get-tuple-element.778), channel_id=1, source_target_pairs={{4,0},{8,4},{12,8},{16,12},{20,16},{24,20},{28,24},{5,1},{9,5},{13... | collective-permute-start | bytes 786440 | tf_op jit(solution)/shard_map/while/body/eval_jaxpr/ppermute | solution.py:25
  548.1 8.3 %collective-permute-start.1 = (f32[4,64,256]{2,1,0:T(8,128)S(1)}, f32[4,64,256]{2,1,0:T(8,128)S(1)}, u32[]{:S(2)}, u32[]{:S(2)}) collective-permute-start(f32[4,64,256]{2,1,0:T(8,128)S(1)} %get-tuple-element.778), channel_id=1, source_target_pairs={{4,0},{8,4},{12,8},{16,12},{20,16},{24,20},{28,24},{5,1},{9,5},{13... | collective-permute-start | bytes 786440 | tf_op jit(solution)/shard_map/while/body/eval_jaxpr/ppermute | solution.py:25
where the time goes:
time: 567 us; the launch traced here: 557 us
  waiting for transfers between devices  257 us (45%)
  matrix products  143 us (25%)
  starting transfers between devices  117 us (21%)
  local copies, waits for them, and re-layouts  20.5 us (4%)
  other arithmetic  17.3 us (3%)
    ppermute x22, waiting for transfers between devices, passed_along(): return lax.ppermute(block, axis, route)  257 us
    ppermute x22, starting transfers between devices, passed_along(): return lax.ppermute(block, axis, route)  112 us
    dot_general x40, matrix products, typed_product(): jnp.einsum('tpq,rqw->trpw', blocks_table, state_in, precision=precise)  96.3 us
    dot_general x32, matrix products, inverse_product(): jnp.einsum('pq,rqw->rpw', diag_inverse, balance, precision=precise)  47 us
  transfers between devices with their start and end apart: 24, of which 22 were waited for; matrix products, arithmetic and copies ran while one was open for 7% of the time, Pallas kernels for 0%

commit v1 on v0

v1 whole, which is shorter than its diff:
```python
import functools

import jax
import jax.numpy as jnp
from jax import lax
from jax.experimental import pallas as pl
from jax.experimental.pallas import tpu as pltpu
from jax.sharding import PartitionSpec as P

KINDS = 6
MEMBERS = 4
F32 = jnp.float32
BF16 = jnp.bfloat16
VMEM_BYTES = 52 << 20


def parts_of(value):
    high = value.astype(BF16)
    low = (value - high.astype(F32)).astype(BF16)
    return high, low


def stacked_state(value):
    high, low = parts_of(value)
    return jnp.concatenate([high, low, high, low], axis=0)


def stacked_table(value):
    high, low = parts_of(value)
    return jnp.concatenate([high, high, low, low], axis=1)


def kind_masks(kinds_row, rows):
    wide = jnp.broadcast_to(kinds_row, (rows, kinds_row.shape[1]))
    return [wide == t for t in range(1, KINDS)]


def select(products, masks):
    rows = products.shape[0] // KINDS
    chosen = products[:rows]
    for t in range(1, KINDS):
        chosen = jnp.where(masks[t - 1], products[t * rows : (t + 1) * rows], chosen)
    return chosen


def typed(table, state, masks):
    return select(jnp.dot(table, stacked_state(state), preferred_element_type=F32), masks)


def params(flops, moved):
    return dict(
        compiler_params=pltpu.CompilerParams(vmem_limit_bytes=VMEM_BYTES),
        cost_estimate=pl.CostEstimate(flops=flops, bytes_accessed=moved, transcendentals=0),
    )


def tables_kernel(lagged, up, down, inverse, up_out, down_out, inv_out, first_out, last_out, edges, sems):
    layers, tracers, dofs, columns = lagged.shape
    low = pltpu.make_async_copy(lagged.at[:, :, :, pl.ds(0, 128)], edges.at[0], sems.at[0])
    high = pltpu.make_async_copy(lagged.at[:, :, :, pl.ds(columns - 128, 128)], edges.at[1], sems.at[1])
    low.start()
    high.start()
    dinv = inverse[...]
    for t in range(KINDS):
        for source, target in ((up, up_out), (down, down_out)):
            folded = jnp.dot(dinv, source[t], preferred_element_type=F32, precision=lax.Precision.HIGHEST)
            target[t * dofs : (t + 1) * dofs, :] = stacked_table(folded)
    inv_out[...] = stacked_table(dinv)
    low.wait()
    high.wait()
    lane = lax.broadcasted_iota(jnp.int32, (dofs, 128), 1)
    for side, lane_at, target in ((0, 0, first_out), (1, 127, last_out)):
        packed = jnp.zeros((dofs, 128), F32)
        for layer in range(layers):
            for tracer in range(tracers):
                column = edges[side, layer, tracer][:, lane_at : lane_at + 1]
                packed = jnp.where(lane == layer * tracers + tracer, column, packed)
        target[...] = packed


def local_forward_kernel(
    place, rhs, lagged, kinds, stream, span, absorb, from_low, from_high, table, inv_table,
    g_out, f_out, m0, m1, m2, m3, state,
):
    layer = pl.program_id(0)
    layers = pl.num_programs(0)
    tracers, dofs, columns = state.shape
    row = pl.ds(layer, 1)
    scale = stream[row, :]
    span_low = span[0, row, :]
    span_high = span[1, row, :]
    inv_denom = 1.0 / (scale + span_low + span_high + absorb[row, :])
    padding = jnp.zeros((1, 128), jnp.int32)
    kinds_low = pltpu.roll(jnp.concatenate([kinds[1, row, :], padding], axis=1), columns + 127, 1)
    kinds_high = pltpu.roll(jnp.concatenate([kinds[2, row, :], padding], axis=1), 1, 1)
    masks_low = kind_masks(kinds_low, dofs)
    masks_high = kind_masks(kinds_high, dofs)
    turn = lax.rem(128 - layer * tracers, 128)
    edge_low = pltpu.roll(from_low[...], turn, 1)
    edge_high = pltpu.roll(from_high[...], turn, 1)
    lane = lax.broadcasted_iota(jnp.int32, (dofs, 128), 1)
    for tracer in range(tracers):
        beyond = jnp.where(
            lane == 127, edge_low[:, tracer : tracer + 1], edge_high[:, tracer : tracer + 1]
        )
        wide = jnp.concatenate([lagged[0, tracer], beyond], axis=1)
        products = jnp.dot(table[...], stacked_state(wide), preferred_element_type=F32)
        low_term = pltpu.roll(select(products, masks_low), 1, 1)[:, :columns]
        high_term = pltpu.roll(select(products, masks_high), columns + 127, 1)[:, :columns]
        solved = jnp.dot(inv_table[...], stacked_state(rhs[0, tracer]), preferred_element_type=F32)
        g_out[0, tracer] = inv_denom * (solved - span_low * low_term - span_high * high_term)

    @pl.when(layer == 0)
    def first():
        for tracer in range(tracers):
            state[tracer] = g_out[0, tracer]

    @pl.when(layer > 0)
    def later():
        masks = kind_masks(kinds[0, row, :], dofs)
        factor = scale * inv_denom
        for tracer in range(tracers):
            state[tracer] = g_out[0, tracer] - factor * typed(table[...], state[tracer], masks)

    f_out[0] = state[...]

    @pl.when(layer == layers - 1)
    def send():
        count = stream.shape[0]
        width = columns // MEMBERS
        for k, target in enumerate((m0, m1, m2, m3)):
            own = pl.ds(pl.multiple_of((place[0] ^ k) * width, width), width)
            for tracer in range(tracers):
                target[tracer * dofs : (tracer + 1) * dofs, :] = state[tracer, :, own]
            top = tracers * dofs
            scales = stream[:, own]
            target[top : top + count, :] = scales
            target[top + count : top + 2 * count, :] = 1.0 / (
                scales + span[0, :, own] + span[1, :, own] + absorb[:, own]
            )
            target[top + 2 * count : top + 3 * count, :] = kinds[0, :, own].astype(F32)
            if target.shape[0] > top + 3 * count:
                target[top + 3 * count :, :] = jnp.zeros((target.shape[0] - top - 3 * count, width), F32)


def local_backward_kernel(
    place, f_in, kinds, stream, span, absorb, table, m0, m1, m2, m3, carried
):
    step = pl.program_id(0)
    layers = pl.num_programs(0)
    layer = layers - 1 - step
    tracers, dofs, columns = carried.shape
    row = pl.ds(layer, 1)
    scale = stream[row, :]
    inv_denom = 1.0 / (scale + span[0, row, :] + span[1, row, :] + absorb[row, :])
    masks = kind_masks(kinds[0, row, :], dofs)

    @pl.when(step == 0)
    def first():
        for tracer in range(tracers):
            carried[tracer] = scale * typed(table[...], f_in[0, tracer], masks)

    @pl.when(step > 0)
    def later():
        for tracer in range(tracers):
            solved = f_in[0, tracer] - inv_denom * carried[tracer]
            carried[tracer] = scale * typed(table[...], solved, masks)

    @pl.when(step == layers - 1)
    def send():
        width = columns // MEMBERS
        for k, target in enumerate((m0, m1, m2, m3)):
            own = pl.ds(pl.multiple_of((place[0] ^ k) * width, width), width)
            for tracer in range(tracers):
                target[tracer * dofs : (tracer + 1) * dofs, :] = carried[tracer, :, own]


def chain_forward_kernel(
    turn, layers, tracers,
    place, inflow, table, m0, m1, m2, m3, *rest,
):
    olds, (states, out0, out1, out2, out3, outflow, blocks, entering, held, sems, out_sems) = rest[:-11], rest[-11:]
    rows = entering.shape[1]
    dofs = rows // tracers

    @pl.when(place[1] == turn)
    def active():
        arriving = [
            pltpu.make_async_copy(source, blocks.at[place[0] ^ k], sems.at[k])
            for k, source in enumerate((m0, m1, m2, m3))
        ]
        for copy in arriving:
            copy.start()
        if turn == 0:
            entering[0] = jnp.zeros(entering.shape[1:], F32)
        else:
            first = pltpu.make_async_copy(inflow, entering.at[0], sems.at[MEMBERS])
            first.start()
            first.wait()
        for copy in arriving:
            copy.wait()
        for block in range(MEMBERS):
            values = [entering[block, r * dofs : (r + 1) * dofs, :] for r in range(tracers)]
            for layer in range(layers):
                scale = blocks[block, rows + layer : rows + layer + 1, :]
                inv_denom = blocks[block, rows + layers + layer : rows + layers + layer + 1, :]
                kinds = blocks[block, rows + 2 * layers + layer : rows + 2 * layers + layer + 1, :]
                factor = -(scale * inv_denom)
                if block == 0 and turn == 0:
                    values = [jnp.zeros_like(v) for v in values]
                else:
                    masks = kind_masks(kinds, dofs)
                    values = [factor * typed(table[...], v, masks) for v in values]
                for r in range(tracers):
                    held[block, layer, r * dofs : (r + 1) * dofs, :] = values[r]
            pltpu.make_async_copy(held.at[block], states.at[block], out_sems.at[block]).start()
            for r in range(tracers):
                here = slice(r * dofs, (r + 1) * dofs)
                value = values[r] + blocks[block, here, :]
                if block < MEMBERS - 1:
                    entering[block + 1, here, :] = value
                else:
                    outflow[here, :] = value
        leaving = [
            pltpu.make_async_copy(entering.at[place[0] ^ k], target, sems.at[k])
            for k, target in enumerate((out0, out1, out2, out3))
        ]
        for copy in leaving:
            copy.start()
        for copy in leaving:
            copy.wait()
        for block in range(MEMBERS):
            pltpu.make_async_copy(held.at[block], states.at[block], out_sems.at[block]).wait()


def chain_backward_kernel(
    turn, last, layers, tracers,
    place, inflow, table, m0, m1, m2, m3, e0, e1, e2, e3, states, *rest,
):
    olds, (out0, out1, out2, out3, outflow, blocks, terms, entering, held, sems, held_sems) = rest[:-11], rest[-11:]
    rows = entering.shape[1]
    dofs = rows // tracers

    @pl.when(place[1] == turn)
    def active():
        reading = [
            pltpu.make_async_copy(states.at[block], held.at[block], held_sems.at[block])
            for block in range(MEMBERS)
        ]
        for copy in reversed(reading):
            copy.start()
        arriving = [
            pltpu.make_async_copy(source.at[pl.ds(rows, source.shape[0] - rows), :], blocks.at[place[0] ^ k], sems.at[k])
            for k, source in enumerate((m0, m1, m2, m3))
        ] + [
            pltpu.make_async_copy(source, terms.at[place[0] ^ k], sems.at[MEMBERS + k])
            for k, source in enumerate((e0, e1, e2, e3))
        ]
        for copy in arriving:
            copy.start()
        if turn == last:
            entering[MEMBERS - 1] = jnp.zeros(entering.shape[1:], F32)
        else:
            first = pltpu.make_async_copy(inflow, entering.at[MEMBERS - 1], sems.at[2 * MEMBERS])
            first.start()
            first.wait()
        for copy in arriving:
            copy.wait()
        for block in reversed(range(MEMBERS)):
            reading[block].wait()
            if block == 0 and turn == 0:
                continue
            values = [entering[block, r * dofs : (r + 1) * dofs, :] for r in range(tracers)]
            for layer in reversed(range(layers)):
                scale = blocks[block, layer : layer + 1, :]
                inv_denom = blocks[block, layers + layer : layers + layer + 1, :]
                masks = kind_masks(blocks[block, 2 * layers + layer : 2 * layers + layer + 1, :], dofs)
                values = [
                    scale * typed(
                        table[...],
                        held[block, layer, r * dofs : (r + 1) * dofs, :] - inv_denom * values[r],
                        masks,
                    )
                    for r in range(tracers)
                ]
            for r in range(tracers):
                here = slice(r * dofs, (r + 1) * dofs)
                value = values[r] + terms[block, here, :]
                if block > 0:
                    entering[block - 1, here, :] = value
                else:
                    outflow[here, :] = value
        leaving = [
            pltpu.make_async_copy(entering.at[place[0] ^ k], target, sems.at[k])
            for k, target in enumerate((out0, out1, out2, out3))
        ]
        for copy in leaving:
            copy.start()
        for copy in leaving:
            copy.wait()


def take_inflow(place, sources, state):
    tracers, dofs, columns = state.shape
    width = columns // MEMBERS
    for k, source in enumerate(sources):
        own = pl.ds(pl.multiple_of((place[0] ^ k) * width, width), width)
        for tracer in range(tracers):
            state[tracer, :, own] = source[tracer * dofs : (tracer + 1) * dofs, :]


def final_forward_kernel(place, g_in, kinds, stream, span, absorb, table, m0, m1, m2, m3, f_out, state):
    layer = pl.program_id(0)
    tracers, dofs, columns = state.shape
    row = pl.ds(layer, 1)

    @pl.when(layer == 0)
    def first():
        take_inflow(place, (m0, m1, m2, m3), state)

    scale = stream[row, :]
    factor = scale / (scale + span[0, row, :] + span[1, row, :] + absorb[row, :])
    masks = kind_masks(kinds[0, row, :], dofs)
    for tracer in range(tracers):
        value = g_in[0, tracer] - factor * typed(table[...], state[tracer], masks)
        state[tracer] = value
        f_out[0, tracer] = value


def final_backward_kernel(place, f_in, kinds, stream, span, absorb, table, m0, m1, m2, m3, out, carried):
    step = pl.program_id(0)
    layers = pl.num_programs(0)
    layer = layers - 1 - step
    tracers, dofs, columns = carried.shape
    row = pl.ds(layer, 1)

    @pl.when(step == 0)
    def first():
        take_inflow(place, (m0, m1, m2, m3), carried)

    scale = stream[row, :]
    inv_denom = 1.0 / (scale + span[0, row, :] + span[1, row, :] + absorb[row, :])
    for tracer in range(tracers):
        out[0, tracer] = f_in[0, tracer] - inv_denom * carried[tracer]

    @pl.when(step < layers - 1)
    def carry():
        masks = kind_masks(kinds[0, row, :], dofs)
        for tracer in range(tracers):
            carried[tracer] = scale * typed(table[...], out[0, tracer], masks)


def whole(shape, dims):
    return pl.BlockSpec(shape, lambda *i: (0,) * dims)


def per_device(rhs, lagged, kinds, stream, span, absorb, up, down, inverse):
    layers, tracers, dofs, columns = rhs.shape
    rows = tracers * dofs
    width = columns // MEMBERS
    count = lax.axis_size("stream")
    groups = count // MEMBERS
    position = lax.axis_index("stream")
    place = jnp.stack([position % MEMBERS, position // MEMBERS]).astype(jnp.int32)
    long_rows = rows + -(-3 * layers // 8) * 8
    vmem, anywhere, smem = (pl.BlockSpec(memory_space=s) for s in (pltpu.VMEM, pl.ANY, pltpu.SMEM))
    full = functools.partial(jax.ShapeDtypeStruct, dtype=F32)

    up_table, down_table, inv_table, first_edge, last_edge = pl.pallas_call(
        tables_kernel,
        out_shape=(
            jax.ShapeDtypeStruct((KINDS * dofs, 4 * dofs), BF16),
            jax.ShapeDtypeStruct((KINDS * dofs, 4 * dofs), BF16),
            jax.ShapeDtypeStruct((dofs, 4 * dofs), BF16),
            full((dofs, 128)),
            full((dofs, 128)),
        ),
        in_specs=[anywhere, vmem, vmem, vmem],
        out_specs=(vmem,) * 5,
        scratch_shapes=[
            pltpu.VMEM((2, layers, tracers, dofs, 128), F32),
            pltpu.SemaphoreType.DMA((2,)),
        ],
        name="tables",
        **params(1 << 24, 1 << 20),
    )(lagged, up, down, inverse)

    across = lax.axis_size("span")
    from_low = lax.ppermute(last_edge, "span", [(i, i + 1) for i in range(across - 1)])
    from_high = lax.ppermute(first_edge, "span", [(i + 1, i) for i in range(across - 1)])

    def exchanged(messages):
        return [messages[0]] + [
            lax.ppermute(messages[k], "stream", [(i, i ^ k) for i in range(count)])
            for k in range(1, MEMBERS)
        ]

    layer_block = pl.BlockSpec((1, tracers, dofs, columns), lambda i: (i, 0, 0, 0))
    layer_back = pl.BlockSpec((1, tracers, dofs, columns), lambda i: (layers - 1 - i, 0, 0, 0))
    small = [
        whole((3, layers, columns), 3),
        whole((layers, columns), 2),
        whole((2, layers, columns), 3),
        whole((layers, columns), 2),
    ]
    table_block = whole((KINDS * dofs, 4 * dofs), 2)
    message = whole((rows, width), 2)
    long_message = whole((long_rows, width), 2)
    column_state = pltpu.VMEM((tracers, dofs, columns), F32)
    product = 2 * KINDS * dofs * 4 * dofs * tracers * columns

    g, f_zero, *out_b = pl.pallas_call(
        local_forward_kernel,
        grid=(layers,),
        out_shape=(full(rhs.shape), full(rhs.shape)) + (full((long_rows, width)),) * MEMBERS,
        in_specs=[smem, layer_block, layer_block] + small
        + [whole((dofs, 128), 2)] * 2 + [table_block, whole((dofs, 4 * dofs), 2)],
        out_specs=(layer_block, layer_block) + (long_message,) * MEMBERS,
        scratch_shapes=[column_state],
        name="local_forward",
        **params(2 * layers * product, 16 * rhs.size),
    )(place, rhs, lagged, kinds, stream, span, absorb, from_low, from_high, up_table, inv_table)
    in_b = exchanged(out_b)

    out_e = pl.pallas_call(
        local_backward_kernel,
        grid=(layers,),
        out_shape=(full((rows, width)),) * MEMBERS,
        in_specs=[smem, layer_back] + small + [table_block],
        out_specs=(message,) * MEMBERS,
        scratch_shapes=[column_state],
        name="local_backward",
        **params(layers * product, 4 * rhs.size),
    )(place, f_zero, kinds, stream, span, absorb, down_table)
    in_e = exchanged(out_e)

    def between(values, step):
        pairs = [(step * MEMBERS + i, (step + 1) * MEMBERS + i) for i in range(MEMBERS)]
        return lax.ppermute(values, "stream", pairs + [(b, a) for a, b in pairs])

    state_shape = full((MEMBERS, layers, rows, width))
    block_scratch = [
        pltpu.VMEM((MEMBERS, rows, width), F32),
        pltpu.VMEM((MEMBERS, layers, rows, width), F32),
    ]
    inflow = jnp.zeros((rows, width), F32)
    kept = ()
    for turn in range(groups):
        old_count = len(kept)
        *kept, outflow = pl.pallas_call(
            functools.partial(chain_forward_kernel, turn, layers, tracers),
            out_shape=(state_shape,) + (full((rows, width)),) * (MEMBERS + 1),
            in_specs=[smem, anywhere, vmem] + [anywhere] * (MEMBERS + old_count),
            out_specs=(anywhere,) * (MEMBERS + 1) + (vmem,),
            scratch_shapes=[pltpu.VMEM((MEMBERS, long_rows, width), F32)] + block_scratch
            + [pltpu.SemaphoreType.DMA((MEMBERS + 1,)), pltpu.SemaphoreType.DMA((MEMBERS,))],
            input_output_aliases={3 + MEMBERS + i: i for i in range(old_count)},
            name=f"chain_forward_{turn}",
            **params(layers * product, 8 * rhs.size),
        )(place, inflow, up_table, *in_b, *kept)
        if turn < groups - 1:
            inflow = between(outflow, turn)
    states, *out_f = kept
    in_f = exchanged(out_f)

    kept = ()
    for turn in reversed(range(groups)):
        old_count = len(kept)
        *kept, outflow = pl.pallas_call(
            functools.partial(chain_backward_kernel, turn, groups - 1, layers, tracers),
            out_shape=(full((rows, width)),) * (MEMBERS + 1),
            in_specs=[smem, anywhere, vmem] + [anywhere] * (2 * MEMBERS + 1 + old_count),
            out_specs=(anywhere,) * MEMBERS + (vmem,),
            scratch_shapes=[
                pltpu.VMEM((MEMBERS, long_rows - rows, width), F32),
                pltpu.VMEM((MEMBERS, rows, width), F32),
            ] + block_scratch
            + [pltpu.SemaphoreType.DMA((2 * MEMBERS + 1,)), pltpu.SemaphoreType.DMA((MEMBERS,))],
            input_output_aliases={4 + 2 * MEMBERS + i: i for i in range(old_count)},
            name=f"chain_backward_{turn}",
            **params(layers * product, 8 * rhs.size),
        )(place, inflow, down_table, *in_b, *in_e, states, *kept)
        if turn > 0:
            inflow = between(outflow, turn - 1)
    in_h = exchanged(kept)

    f_part = pl.pallas_call(
        final_forward_kernel,
        grid=(layers,),
        out_shape=full(rhs.shape),
        in_specs=[smem, layer_block] + small + [table_block] + [message] * MEMBERS,
        out_specs=layer_block,
        scratch_shapes=[column_state],
        name="final_forward",
        **params(layers * product, 8 * rhs.size),
    )(place, g, kinds, stream, span, absorb, up_table, *in_f)
    return pl.pallas_call(
        final_backward_kernel,
        grid=(layers,),
        out_shape=full(rhs.shape),
        in_specs=[smem, layer_back] + small + [table_block] + [message] * MEMBERS,
        out_specs=layer_back,
        scratch_shapes=[column_state],
        name="final_backward",
        **params(layers * product, 8 * rhs.size),
    )(place, f_part, kinds, stream, span, absorb, down_table, *in_h)


def solution(mesh):
    return jax.shard_map(
        per_device,
        mesh=mesh,
        in_specs=(
            P("stream", None, None, "span"),
            P("stream", None, None, "span"),
            P(None, "stream", "span"),
            P("stream", "span"),
            P(None, "stream", "span"),
            P("stream", "span"),
            P(),
            P(),
            P(),
        ),
        out_specs=P("stream", None, None, "span"),
        check_vma=False,
    )
```

time: 567 us -> 126 us (0.22); the launches traced: 557 us -> 125 us
  waiting for transfers between devices: 257 us -> 42.9 us
  matrix products: 143 us -> 0 us
  starting transfers between devices: 117 us -> 26.1 us
  Pallas kernels: 0 us -> 51.1 us
  other arithmetic: 17.3 us -> 0.08 us
  local copies, waits for them, and re-layouts: 20.5 us -> 4.76 us
    ppermute x24 -> x16, waiting for transfers between devices: 257 us -> 42.9 us  [the longest x12 25.5 us: exchanged(): lax.ppermute(messages[k], 'stream', [(i, i ^ k) for i in range(count)])]
    dot_general x72 -> x0, matrix products: 143 us -> none  [the longest x40 96.3 us: typed_product(): jnp.einsum('tpq,rqw->trpw', blocks_table, state_in, precision=precise)]
    ppermute x24 -> x16, starting transfers between devices: 117 us -> 26.1 us  [the longest x12 15.5 us: exchanged(): lax.ppermute(messages[k], 'stream', [(i, i ^ k) for i in range(count)])]
    pallas_call x0 -> x9, Pallas kernels: none -> 51.1 us  [the longest x1 13.6 us: per_device(): pl.pallas_call(local_forward_kernel, grid=(layers,), out_shape=(full(rhs....]
    dynamic_update_slice x8 -> x0, other arithmetic: 12.6 us -> none  [the longest x4 8.33 us: forward_block(): lax.dynamic_update_slice_in_dim(forward_part, jnp.stack(results), offset, 3)]
    another operation x18 -> x0, local copies, waits for them, and re-layouts: 10.1 us -> none
  transfers between devices with their start and end apart: 24 -> 16, of which waited for: 22 -> 10; matrix products, arithmetic and copies ran while one was open for 7% -> 0% of each run, Pallas kernels for 0% -> 18%
where the time goes in v1:
time: 126 us; the launch traced here: 125 us
  Pallas kernels  51.1 us (41%)
  waiting for transfers between devices  42.9 us (34%)
  starting transfers between devices  26.1 us (21%)
  local copies, waits for them, and re-layouts  4.76 us (4%)
    ppermute x12, waiting for transfers between devices, exchanged(): lax.ppermute(messages[k], 'stream', [(i, i ^ k) for i in range(count)])  25.5 us
    ppermute x12, starting transfers between devices, exchanged(): lax.ppermute(messages[k], 'stream', [(i, i ^ k) for i in range(count)])  15.5 us
    pallas_call x1, Pallas kernels, per_device(): pl.pallas_call(local_forward_kernel, grid=(layers,), out_shape=(full(rhs....  13.6 us
    ppermute x2, waiting for transfers between devices, between(): return lax.ppermute(values, 'stream', pairs + [(b, a) for a, b in pairs])  13.5 us
    pallas_call x2, Pallas kernels, per_device(): pl.pallas_call(functools.partial(chain_backward_kernel, turn, groups - 1,...  8.47 us
    pallas_call x2, Pallas kernels, per_device(): pl.pallas_call(functools.partial(chain_forward_kernel, turn, layers, trac...  7.86 us
    pallas_call x1, Pallas kernels, per_device(): pl.pallas_call(final_forward_kernel, grid=(layers,), out_shape=full(rhs.s...  7.07 us
    ppermute x2, starting transfers between devices, between(): return lax.ppermute(values, 'stream', pairs + [(b, a) for a, b in pairs])  6.89 us
  transfers between devices with their start and end apart: 16, of which 10 were waited for; matrix products, arithmetic and copies ran while one was open for 0% of the time, Pallas kernels for 18%

profile of v1, /device:TPU:0, one launch (start us, length us, event | category | flops | bytes accessed | tf_op | source)
XLA Modules:
  0.0 125.0 jit_solution(4725150407761380691)
XLA Ops:
  0.0 0.9 copy-done
  0.9 0.9 copy-done.1
  1.9 0.8 copy-done.2
  2.6 1.8 %tables.1 = (bf16[384,256]{1,0:T(8,128)(2,1)S(1)}, bf16[384,256]{1,0:T(8,128)(2,1)S(1)}, bf16[64,256]{1,0:T(8,128)(2,1)S(1)}, f32[64,128]{1,0:T(8,128)S(1)}, f32[64,128]{1,0:T(8,128)S(1)}) custom-call(f32[4,4,64,1024]{3,2,1,0:T(8,128)} %lagged.3, f32[6,64,64]{2,1,0:T(8,128)S(1)} %copy-done, f32[6,64,64]{2,1,0:T(8,128)S(1)} %copy-done.1, f32[64,64]{1,0:T(8,128)S(1)} %copy-done.2), custom_call_target="tpu_custom_call" | custom-call | flops 16777216 | bytes 1048576 | tf_op jit(solution)/shard_map/tables/pallas_call | solution.py:369
  4.5 2.4 %collective-permute-start = (f32[64,128]{1,0:T(8,128)S(1)}, f32[64,128]{1,0:T(8,128)S(1)}, u32[]{:S(2)}, u32[]{:S(2)}) collective-permute-start(f32[64,128]{1,0:T(8,128)S(1)} %get-tuple-element.40), channel_id=1, source_target_pairs={{0,1},{1,2},{2,3},{4,5},{5,6},{6,7},{8,9},{9,10},{10,11},{12,13},{... | collective-permute-start | bytes 98312 | tf_op jit(solution)/shard_map/ppermute | solution.py:389
  6.8 1.3 %collective-permute-start.1 = (f32[64,128]{1,0:T(8,128)S(1)}, f32[64,128]{1,0:T(8,128)S(1)}, u32[]{:S(2)}, u32[]{:S(2)}) collective-permute-start(f32[64,128]{1,0:T(8,128)S(1)} %get-tuple-element.41), channel_id=1, source_target_pairs={{1,0},{2,1},{3,2},{5,4},{6,5},{7,6},{9,8},{10,9},{11,10},{13,12},{... | collective-permute-start | bytes 98312 | tf_op jit(solution)/shard_map/ppermute | solution.py:390
  8.2 3.8 %collective-permute-done.1.from_high = f32[64,128]{1,0:T(8,128)S(1)} collective-permute-done((f32[64,128]{1,0:T(8,128)S(1)}, f32[64,128]{1,0:T(8,128)S(1)}, u32[]{:S(2)}, u32[]{:S(2)}) %collective-permute-start.1) | collective-permute-done | bytes 32800 | tf_op jit(solution)/shard_map/ppermute | solution.py:390
  12.1 13.6 %local_forward.1 = (f32[4,4,64,1024]{3,2,1,0:T(8,128)}, f32[4,4,64,1024]{3,2,1,0:T(8,128)}, f32[272,256]{1,0:T(8,128)S(1)}, f32[272,256]{1,0:T(8,128)S(1)}, f32[...) custom-call(s32[2]{0:T(128)S(1)} %pad_add_fusion.place, f32[4,4,64,1024]{3,2,1,0:T(8,128)} %rhs.1, f32[4,4,64,1024]{3,2,1,0:T(8,128)} %lagged.3, ...), custom_call_target="tpu_custom_call" | custom-call | flops 6442450944 | bytes 16777216 | tf_op jit(solution)/shard_map/local_forward/pallas_call | solution.py:412
  26.5 1.5 %collective-permute-start.2 = (f32[272,256]{1,0:T(8,128)S(1)}, f32[272,256]{1,0:T(8,128)S(1)}, u32[]{:S(2)}, u32[]{:S(2)}) collective-permute-start(f32[272,256]{1,0:T(8,128)S(1)} %get-tuple-element.46), channel_id=1, source_target_pairs={{0,4},{4,0},{8,12},{12,8},{16,20},{20,16},{24,28},{28,24},{1,5},{5... | collective-permute-start | bytes 835592 | tf_op jit(solution)/shard_map/ppermute | solution.py:394
  28.0 1.6 %collective-permute-start.3 = (f32[272,256]{1,0:T(8,128)S(1)}, f32[272,256]{1,0:T(8,128)S(1)}, u32[]{:S(2)}, u32[]{:S(2)}) collective-permute-start(f32[272,256]{1,0:T(8,128)S(1)} %get-tuple-element.47), channel_id=1, source_target_pairs={{0,8},{4,12},{8,0},{12,4},{16,24},{20,28},{24,16},{28,20},{1,9},{5... | collective-permute-start | bytes 835592 | tf_op jit(solution)/shard_map/ppermute | solution.py:394
  29.9 4.3 %collective-permute-done.2.m1 = f32[272,256]{1,0:T(8,128)S(1)} collective-permute-done((f32[272,256]{1,0:T(8,128)S(1)}, f32[272,256]{1,0:T(8,128)S(1)}, u32[]{:S(2)}, u32[]{:S(2)}) %collective-permute-start.2) | collective-permute-done | bytes 278560 | tf_op jit(solution)/shard_map/ppermute | solution.py:394
  34.3 1.8 %collective-permute-done.3.m2 = f32[272,256]{1,0:T(8,128)S(1)} collective-permute-done((f32[272,256]{1,0:T(8,128)S(1)}, f32[272,256]{1,0:T(8,128)S(1)}, u32[]{:S(2)}, u32[]{:S(2)}) %collective-permute-start.3) | collective-permute-done | bytes 278560 | tf_op jit(solution)/shard_map/ppermute | solution.py:394
  36.1 5.9 %collective-permute-done.4.m3 = f32[272,256]{1,0:T(8,128)S(1)} collective-permute-done((f32[272,256]{1,0:T(8,128)S(1)}, f32[272,256]{1,0:T(8,128)S(1)}, u32[]{:S(2)}, u32[]{:S(2)}) %collective-permute-start.4) | collective-permute-done | bytes 278560 | tf_op jit(solution)/shard_map/ppermute | solution.py:394
  42.7 6.4 %chain_forward_0.1 = (f32[4,4,256,256]{3,2,1,0:T(8,128)}, f32[256,256]{1,0:T(8,128)S(1)}, f32[256,256]{1,0:T(8,128)S(1)}, f32[256,256]{1,0:T(8,128)S(1)}, f32[25...) custom-call(s32[2]{0:T(128)S(1)} %pad_add_fusion.place, f32[256,256]{1,0:T(8,128)S(1)} %broadcast_in_dim.3.inflow, ...), custom_call_target="tpu_custom_call" | custom-call | flops 3221225472 | bytes 8388608 | tf_op jit(solution)/shard_map/chain_forward_0/pallas_call | solution.py:450
  49.1 5.7 %local_backward.1 = (f32[256,256]{1,0:T(8,128)S(1)}, f32[256,256]{1,0:T(8,128)S(1)}, f32[256,256]{1,0:T(8,128)S(1)}, f32[256,256]{1,0:T(8,128)S(1)}) custom-call(s32[2]{0:T(128)S(1)} %pad_add_fusion.place, f32[4,4,64,1024]{3,2,1,0:T(8,128)} %get-tuple-element.60.f_in, s32[3,4,1024]{2,1,0:T(4,128)S(1)} %copy-done.3, f32[4,1024]{1,0:T(4,128)S(1)} %copy-done.5, ...), custom_call_target="tpu_custom_call" | custom-call | flops 3221225472 | bytes 4194304 | tf_op jit(solution)/shard_map/local_backward/pallas_call | solution.py:425
  54.9 1.6 %collective-permute-start.9 = (f32[256,256]{1,0:T(8,128)S(1)}, f32[256,256]{1,0:T(8,128)S(1)}, u32[]{:S(2)}, u32[]{:S(2)}) collective-permute-start(f32[256,256]{1,0:T(8,128)S(1)} %get-tuple-element.62), channel_id=1, source_target_pairs={{0,4},{4,0},{8,12},{12,8},{16,20},{20,16},{24,28},{28,24},{1,5},{5... | collective-permute-start | bytes 786440 | tf_op jit(solution)/shard_map/ppermute | solution.py:394
  56.5 1.6 %collective-permute-start.10 = (f32[256,256]{1,0:T(8,128)S(1)}, f32[256,256]{1,0:T(8,128)S(1)}, u32[]{:S(2)}, u32[]{:S(2)}) collective-permute-start(f32[256,256]{1,0:T(8,128)S(1)} %get-tuple-element.63), channel_id=1, source_target_pairs={{0,8},{4,12},{8,0},{12,4},{16,24},{20,28},{24,16},{28,20},{1,9},{5... | collective-permute-start | bytes 786440 | tf_op jit(solution)/shard_map/ppermute | solution.py:394
  58.4 6.2 %collective-permute-done.5.inflow = f32[256,256]{1,0:T(8,128)S(1)} collective-permute-done((f32[256,256]{1,0:T(8,128)S(1)}, f32[256,256]{1,0:T(8,128)S(1)}, u32[]{:S(2)}, u32[]{:S(2)}) %collective-permute-start.5) | collective-permute-done | bytes 262176 | tf_op jit(solution)/shard_map/ppermute | solution.py:439
  64.6 1.5 %chain_forward_1.1 = (f32[4,4,256,256]{3,2,1,0:T(8,128)}, f32[256,256]{1,0:T(8,128)S(1)}, f32[256,256]{1,0:T(8,128)S(1)}, f32[256,256]{1,0:T(8,128)S(1)}, f32[256,256]{1,0:T(8,128)S(1)}, /*index=5*/f32[256,256]{1,0:T(8,128)}) custom-call(s32[2]{0:T(128)S(1)} %pad_add_fusion.place, ...), custom_call_target="tpu_custom_call", output_to_operand_aliasing={{0}: (7, {}), {1}: (8, {}), {2}: (9, {}), {3}: (10, {}), {4... | custom-call | flops 3221225472 | bytes 8388608 | tf_op jit(solution)/shard_map/chain_forward_1/pallas_call | solution.py:450
  66.2 4.0 %collective-permute-done.10.e2 = f32[256,256]{1,0:T(8,128)S(1)} collective-permute-done((f32[256,256]{1,0:T(8,128)S(1)}, f32[256,256]{1,0:T(8,128)S(1)}, u32[]{:S(2)}, u32[]{:S(2)}) %collective-permute-start.10) | collective-permute-done | bytes 262176 | tf_op jit(solution)/shard_map/ppermute | solution.py:394
  70.2 5.5 %collective-permute-done.11.e3 = f32[256,256]{1,0:T(8,128)S(1)} collective-permute-done((f32[256,256]{1,0:T(8,128)S(1)}, f32[256,256]{1,0:T(8,128)S(1)}, u32[]{:S(2)}, u32[]{:S(2)}) %collective-permute-start.11) | collective-permute-done | bytes 262176 | tf_op jit(solution)/shard_map/ppermute | solution.py:394
  77.1 6.8 %collective-permute-start.12 = (f32[256,256]{1,0:T(8,128)S(1)}, f32[256,256]{1,0:T(8,128)S(1)}, u32[]{:S(2)}, u32[]{:S(2)}) collective-permute-start(f32[256,256]{1,0:T(8,128)S(1)} %get-tuple-element.66), channel_id=1, source_target_pairs={{0,16},{4,20},{8,24},{12,28},{16,0},{20,4},{24,8},{28,12},{1,17},{... | collective-permute-start | bytes 786440 | tf_op jit(solution)/shard_map/ppermute | solution.py:439
  83.9 1.5 %collective-permute-start.6 = (f32[256,256]{1,0:T(8,128)S(1)}, f32[256,256]{1,0:T(8,128)S(1)}, u32[]{:S(2)}, u32[]{:S(2)}) collective-permute-start(f32[256,256]{1,0:T(8,128)S(1)} %get-tuple-element.56), channel_id=1, source_target_pairs={{0,4},{4,0},{8,12},{12,8},{16,20},{20,16},{24,28},{28,24},{1,5},{5... | collective-permute-start | bytes 786440 | tf_op jit(solution)/shard_map/ppermute | solution.py:394
  85.5 2.4 %collective-permute-start.7 = (f32[256,256]{1,0:T(8,128)S(1)}, f32[256,256]{1,0:T(8,128)S(1)}, u32[]{:S(2)}, u32[]{:S(2)}) collective-permute-start(f32[256,256]{1,0:T(8,128)S(1)} %get-tuple-element.57), channel_id=1, source_target_pairs={{0,8},{4,12},{8,0},{12,4},{16,24},{20,28},{24,16},{28,20},{1,9},{5... | collective-permute-start | bytes 786440 | tf_op jit(solution)/shard_map/ppermute | solution.py:394
  87.9 1.0 collective-permute-start.8
  88.8 7.3 %collective-permute-done.12.inflow = f32[256,256]{1,0:T(8,128)S(1)} collective-permute-done((f32[256,256]{1,0:T(8,128)S(1)}, f32[256,256]{1,0:T(8,128)S(1)}, u32[]{:S(2)}, u32[]{:S(2)}) %collective-permute-start.12) | collective-permute-done | bytes 262176 | tf_op jit(solution)/shard_map/ppermute | solution.py:439
  96.2 7.8 %chain_backward_0.1 = (f32[256,256]{1,0:T(8,128)S(1)}, f32[256,256]{1,0:T(8,128)S(1)}, f32[256,256]{1,0:T(8,128)S(1)}, f32[256,256]{1,0:T(8,128)S(1)}, f32[256,256]{1,0:T(8,128)}) custom-call(s32[2]{0:T(128)S(1)} %pad_add_fusion.place, ...), custom_call_target="tpu_custom_call", output_to_operand_aliasing={{0}: (12, {}), {1}: (13, {}), {2}: (14, {}), {3}: (15, {})} | custom-call | flops 3221225472 | bytes 8388608 | tf_op jit(solution)/shard_map/chain_backward_0/pallas_call | solution.py:469
  104.0 1.6 %collective-permute-start.13 = (f32[256,256]{1,0:T(8,128)S(1)}, f32[256,256]{1,0:T(8,128)S(1)}, u32[]{:S(2)}, u32[]{:S(2)}) collective-permute-start(f32[256,256]{1,0:T(8,128)S(1)} %get-tuple-element.72), channel_id=1, source_target_pairs={{0,4},{4,0},{8,12},{12,8},{16,20},{20,16},{24,28},{28,24},{1,5},{5... | collective-permute-start | bytes 786440 | tf_op jit(solution)/shard_map/ppermute | solution.py:394
  106.3 1.3 %collective-permute-start.15 = (f32[256,256]{1,0:T(8,128)S(1)}, f32[256,256]{1,0:T(8,128)S(1)}, u32[]{:S(2)}, u32[]{:S(2)}) collective-permute-start(f32[256,256]{1,0:T(8,128)S(1)} %get-tuple-element.74), channel_id=1, source_target_pairs={{0,12},{4,8},{8,4},{12,0},{16,28},{20,24},{24,20},{28,16},{1,13},{... | collective-permute-start | bytes 786440 | tf_op jit(solution)/shard_map/ppermute | solution.py:394
  107.6 7.1 %final_forward.1.f_in = f32[4,4,64,1024]{3,2,1,0:T(8,128)} custom-call(s32[2]{0:T(128)S(1)} %pad_add_fusion.place, f32[4,4,64,1024]{3,2,1,0:T(8,128)} %get-tuple-element.44.g_in, s32[3,4,1024]{2,1,0:T(4,128)S(1)} %copy-done.3, f32[4,1024]{1,0:T(4,128)S(1)} %copy-done.5, f32[2,4,1024]{2,1,0:T(4,128)S(1)} %copy-done.4, f32[4,1024]{1,0:T(4,128)S(1)} %copy-done.6, ...), custom_call_target="tpu_custom_call" | custom-call | flops 3221225472 | bytes 8388608 | tf_op jit(solution)/shard_map/final_forward/pallas_call | solution.py:487
  114.9 3.7 %collective-permute-done.15.m3 = f32[256,256]{1,0:T(8,128)S(1)} collective-permute-done((f32[256,256]{1,0:T(8,128)S(1)}, f32[256,256]{1,0:T(8,128)S(1)}, u32[]{:S(2)}, u32[]{:S(2)}) %collective-permute-start.15) | collective-permute-done | bytes 262176 | tf_op jit(solution)/shard_map/ppermute | solution.py:394
  118.6 6.5 %final_backward.1 = f32[4,4,64,1024]{3,2,1,0:T(8,128)} custom-call(s32[2]{0:T(128)S(1)} %pad_add_fusion.place, f32[4,4,64,1024]{3,2,1,0:T(8,128)} %final_forward.1.f_in, s32[3,4,1024]{2,1,0:T(4,128)S(1)} %copy-done.3, f32[4,1024]{1,0:T(4,128)S(1)} %copy-done.5, f32[2,4,1024]{2,1,0:T(4,128)S(1)} %copy-done.4, f32[4,1024]{1,0:T(4,128)S(1)} %copy-done.6, ...), custom_call_target="tpu_custom_call" | custom-call | flops 3221225472 | bytes 8388608 | tf_op jit(solution)/shard_map/final_backward/pallas_call | solution.py:497
  (41 shorter events, 4.7 us)
Async XLA Ops:
  0.0 0.9 copy-start
  0.9 0.9 copy-start.1
  1.9 0.8 copy-start.2
  2.6 9.4 %copy-start.3 = (s32[3,4,1024]{2,1,0:T(4,128)S(1)}, s32[3,4,1024]{2,1,0:T(4,128)}, u32[]{:S(2)}) copy-start(s32[3,4,1024]{2,1,0:T(4,128)} %kinds.7) | copy-start | bytes 147460
  2.6 9.4 %copy-start.4 = (f32[2,4,1024]{2,1,0:T(4,128)S(1)}, f32[2,4,1024]{2,1,0:T(4,128)}, u32[]{:S(2)}) copy-start(f32[2,4,1024]{2,1,0:T(4,128)} %span.7) | copy-start | bytes 98308
  2.6 9.4 %copy-start.5 = (f32[4,1024]{1,0:T(4,128)S(1)}, f32[4,1024]{1,0:T(4,128)}, u32[]{:S(2)}) copy-start(f32[4,1024]{1,0:T(4,128)} %stream.7) | copy-start | bytes 49156
  2.6 9.4 %copy-start.6 = (f32[4,1024]{1,0:T(4,128)S(1)}, f32[4,1024]{1,0:T(4,128)}, u32[]{:S(2)}) copy-start(f32[4,1024]{1,0:T(4,128)} %absorb.7) | copy-start | bytes 49156
  4.5 3.8 %collective-permute-start = (f32[64,128]{1,0:T(8,128)S(1)}, f32[64,128]{1,0:T(8,128)S(1)}, u32[]{:S(2)}, u32[]{:S(2)}) collective-permute-start(f32[64,128]{1,0:T(8,128)S(1)} %get-tuple-element.40), channel_id=1, source_target_pairs={{0,1},{1,2},{2,3},{4,5},{5,6},{6,7},{8,9},{9,10},{10,11},{12,13},{... | collective-permute-start | bytes 98312 | tf_op jit(solution)/shard_map/ppermute | solution.py:389
  6.8 5.2 %collective-permute-start.1 = (f32[64,128]{1,0:T(8,128)S(1)}, f32[64,128]{1,0:T(8,128)S(1)}, u32[]{:S(2)}, u32[]{:S(2)}) collective-permute-start(f32[64,128]{1,0:T(8,128)S(1)} %get-tuple-element.41), channel_id=1, source_target_pairs={{1,0},{2,1},{3,2},{5,4},{6,5},{7,6},{9,8},{10,9},{11,10},{13,12},{... | collective-permute-start | bytes 98312 | tf_op jit(solution)/shard_map/ppermute | solution.py:390
  25.7 0.7 copy-start.7
  26.5 7.8 %collective-permute-start.2 = (f32[272,256]{1,0:T(8,128)S(1)}, f32[272,256]{1,0:T(8,128)S(1)}, u32[]{:S(2)}, u32[]{:S(2)}) collective-permute-start(f32[272,256]{1,0:T(8,128)S(1)} %get-tuple-element.46), channel_id=1, source_target_pairs={{0,4},{4,0},{8,12},{12,8},{16,20},{20,16},{24,28},{28,24},{1,5},{5... | collective-permute-start | bytes 835592 | tf_op jit(solution)/shard_map/ppermute | solution.py:394
  28.0 8.1 %collective-permute-start.3 = (f32[272,256]{1,0:T(8,128)S(1)}, f32[272,256]{1,0:T(8,128)S(1)}, u32[]{:S(2)}, u32[]{:S(2)}) collective-permute-start(f32[272,256]{1,0:T(8,128)S(1)} %get-tuple-element.47), channel_id=1, source_target_pairs={{0,8},{4,12},{8,0},{12,4},{16,24},{20,28},{24,16},{28,20},{1,9},{5... | collective-permute-start | bytes 835592 | tf_op jit(solution)/shard_map/ppermute | solution.py:394
  29.6 12.4 %collective-permute-start.4 = (f32[272,256]{1,0:T(8,128)S(1)}, f32[272,256]{1,0:T(8,128)S(1)}, u32[]{:S(2)}, u32[]{:S(2)}) collective-permute-start(f32[272,256]{1,0:T(8,128)S(1)} %get-tuple-element.48), channel_id=1, source_target_pairs={{0,12},{4,8},{8,4},{12,0},{16,28},{20,24},{24,20},{28,16},{1,13},{... | collective-permute-start | bytes 835592 | tf_op jit(solution)/shard_map/ppermute | solution.py:394
  34.3 7.8 %copy-start.9 = (f32[272,256]{1,0:T(8,128)}, f32[272,256]{1,0:T(8,128)S(1)}, u32[]{:S(2)}) copy-start(f32[272,256]{1,0:T(8,128)S(1)} %collective-permute-done.2.m1) | copy-start | bytes 835588
  36.1 5.9 %copy-start.10 = (f32[272,256]{1,0:T(8,128)}, f32[272,256]{1,0:T(8,128)S(1)}, u32[]{:S(2)}) copy-start(f32[272,256]{1,0:T(8,128)S(1)} %collective-permute-done.3.m2) | copy-start | bytes 835588
  42.0 0.7 copy-start.11
  49.1 15.6 %collective-permute-start.5 = (f32[256,256]{1,0:T(8,128)S(1)}, f32[256,256]{1,0:T(8,128)S(1)}, u32[]{:S(2)}, u32[]{:S(2)}) collective-permute-start(f32[256,256]{1,0:T(8,128)S(1)} %get-tuple-element.49), channel_id=1, source_target_pairs={{0,16},{4,20},{8,24},{12,28},{16,0},{20,4},{24,8},{28,12},{1,17},{... | collective-permute-start | bytes 786440 | tf_op jit(solution)/shard_map/ppermute | solution.py:439
  54.9 11.3 %copy-start.8 = (f32[256,256]{1,0:T(8,128)}, f32[256,256]{1,0:T(8,128)S(1)}, u32[]{:S(2)}) copy-start(f32[256,256]{1,0:T(8,128)S(1)} %get-tuple-element.61.e0) | copy-start | bytes 786436
  54.9 11.3 %collective-permute-start.9 = (f32[256,256]{1,0:T(8,128)S(1)}, f32[256,256]{1,0:T(8,128)S(1)}, u32[]{:S(2)}, u32[]{:S(2)}) collective-permute-start(f32[256,256]{1,0:T(8,128)S(1)} %get-tuple-element.62), channel_id=1, source_target_pairs={{0,4},{4,0},{8,12},{12,8},{16,20},{20,16},{24,28},{28,24},{1,5},{5... | collective-permute-start | bytes 786440 | tf_op jit(solution)/shard_map/ppermute | solution.py:394
  56.5 13.7 %collective-permute-start.10 = (f32[256,256]{1,0:T(8,128)S(1)}, f32[256,256]{1,0:T(8,128)S(1)}, u32[]{:S(2)}, u32[]{:S(2)}) collective-permute-start(f32[256,256]{1,0:T(8,128)S(1)} %get-tuple-element.63), channel_id=1, source_target_pairs={{0,8},{4,12},{8,0},{12,4},{16,24},{20,28},{24,16},{28,20},{1,9},{5... | collective-permute-start | bytes 786440 | tf_op jit(solution)/shard_map/ppermute | solution.py:394
  58.1 17.7 %collective-permute-start.11 = (f32[256,256]{1,0:T(8,128)S(1)}, f32[256,256]{1,0:T(8,128)S(1)}, u32[]{:S(2)}, u32[]{:S(2)}) collective-permute-start(f32[256,256]{1,0:T(8,128)S(1)} %get-tuple-element.64), channel_id=1, source_target_pairs={{0,12},{4,8},{8,4},{12,0},{16,28},{20,24},{24,20},{28,16},{1,13},{... | collective-permute-start | bytes 786440 | tf_op jit(solution)/shard_map/ppermute | solution.py:394
  66.2 9.6 %copy-start.12 = (f32[256,256]{1,0:T(8,128)}, f32[256,256]{1,0:T(8,128)S(1)}, u32[]{:S(2)}) copy-start(f32[256,256]{1,0:T(8,128)S(1)} %collective-permute-done.9.e1) | copy-start | bytes 786436
  70.2 5.6 %copy-start.13 = (f32[256,256]{1,0:T(8,128)}, f32[256,256]{1,0:T(8,128)S(1)}, u32[]{:S(2)}) copy-start(f32[256,256]{1,0:T(8,128)S(1)} %collective-permute-done.10.e2) | copy-start | bytes 786436
  75.7 0.7 copy-start.14
  77.1 19.1 %collective-permute-start.12 = (f32[256,256]{1,0:T(8,128)S(1)}, f32[256,256]{1,0:T(8,128)S(1)}, u32[]{:S(2)}, u32[]{:S(2)}) collective-permute-start(f32[256,256]{1,0:T(8,128)S(1)} %get-tuple-element.66), channel_id=1, source_target_pairs={{0,16},{4,20},{8,24},{12,28},{16,0},{20,4},{24,8},{28,12},{1,17},{... | collective-permute-start | bytes 786440 | tf_op jit(solution)/shard_map/ppermute | solution.py:439
  83.9 22.3 %collective-permute-start.6 = (f32[256,256]{1,0:T(8,128)S(1)}, f32[256,256]{1,0:T(8,128)S(1)}, u32[]{:S(2)}, u32[]{:S(2)}) collective-permute-start(f32[256,256]{1,0:T(8,128)S(1)} %get-tuple-element.56), channel_id=1, source_target_pairs={{0,4},{4,0},{8,12},{12,8},{16,20},{20,16},{24,28},{28,24},{1,5},{5... | collective-permute-start | bytes 786440 | tf_op jit(solution)/shard_map/ppermute | solution.py:394
  85.5 22.1 %collective-permute-start.7 = (f32[256,256]{1,0:T(8,128)S(1)}, f32[256,256]{1,0:T(8,128)S(1)}, u32[]{:S(2)}, u32[]{:S(2)}) collective-permute-start(f32[256,256]{1,0:T(8,128)S(1)} %get-tuple-element.57), channel_id=1, source_target_pairs={{0,8},{4,12},{8,0},{12,4},{16,24},{20,28},{24,16},{28,20},{1,9},{5... | collective-permute-start | bytes 786440 | tf_op jit(solution)/shard_map/ppermute | solution.py:394
  87.9 19.7 %collective-permute-start.8 = (f32[256,256]{1,0:T(8,128)S(1)}, f32[256,256]{1,0:T(8,128)S(1)}, u32[]{:S(2)}, u32[]{:S(2)}) collective-permute-start(f32[256,256]{1,0:T(8,128)S(1)} %get-tuple-element.58), channel_id=1, source_target_pairs={{0,12},{4,8},{8,4},{12,0},{16,28},{20,24},{24,20},{28,16},{1,13},{... | collective-permute-start | bytes 786440 | tf_op jit(solution)/shard_map/ppermute | solution.py:394
  104.0 10.6 %collective-permute-start.13 = (f32[256,256]{1,0:T(8,128)S(1)}, f32[256,256]{1,0:T(8,128)S(1)}, u32[]{:S(2)}, u32[]{:S(2)}) collective-permute-start(f32[256,256]{1,0:T(8,128)S(1)} %get-tuple-element.72), channel_id=1, source_target_pairs={{0,4},{4,0},{8,12},{12,8},{16,20},{20,16},{24,28},{28,24},{1,5},{5... | collective-permute-start | bytes 786440 | tf_op jit(solution)/shard_map/ppermute | solution.py:394
  105.6 9.2 %collective-permute-start.14 = (f32[256,256]{1,0:T(8,128)S(1)}, f32[256,256]{1,0:T(8,128)S(1)}, u32[]{:S(2)}, u32[]{:S(2)}) collective-permute-start(f32[256,256]{1,0:T(8,128)S(1)} %get-tuple-element.73), channel_id=1, source_target_pairs={{0,8},{4,12},{8,0},{12,4},{16,24},{20,28},{24,16},{28,20},{1,9},{5... | collective-permute-start | bytes 786440 | tf_op jit(solution)/shard_map/ppermute | solution.py:394
  106.3 12.3 %collective-permute-start.15 = (f32[256,256]{1,0:T(8,128)S(1)}, f32[256,256]{1,0:T(8,128)S(1)}, u32[]{:S(2)}, u32[]{:S(2)}) collective-permute-start(f32[256,256]{1,0:T(8,128)S(1)} %get-tuple-element.74), channel_id=1, source_target_pairs={{0,12},{4,8},{8,4},{12,0},{16,28},{20,24},{24,20},{28,16},{1,13},{... | collective-permute-start | bytes 786440 | tf_op jit(solution)/shard_map/ppermute | solution.py:394

commit v2 on v0

v2 whole, which is shorter than its diff:
```python
import functools

import jax
import jax.numpy as jnp
from jax import lax
from jax.experimental import pallas as pl
from jax.experimental.pallas import tpu as pltpu
from jax.sharding import PartitionSpec as P

KINDS = 6
MEMBERS = 4
F32 = jnp.float32
BF16 = jnp.bfloat16


def parts_of(value):
    high = value.astype(BF16)
    low = (value - high.astype(F32)).astype(BF16)
    return high, low


def stacked_state(value):
    high, low = parts_of(value)
    return jnp.concatenate([high, low, high, low], axis=0)


def stacked_table(value):
    high, low = parts_of(value)
    return jnp.concatenate([high, high, low, low], axis=1)


def kind_masks(kinds_row, rows):
    wide = jnp.broadcast_to(kinds_row, (rows, kinds_row.shape[1]))
    return [wide == t for t in range(1, KINDS)]


def select(products, masks):
    rows = products.shape[0] // KINDS
    chosen = products[:rows]
    for t in range(1, KINDS):
        chosen = jnp.where(masks[t - 1], products[t * rows : (t + 1) * rows], chosen)
    return chosen


def typed(table, state, masks):
    return select(jnp.dot(table, stacked_state(state), preferred_element_type=F32), masks)


def params(flops, moved, vmem):
    return dict(
        compiler_params=pltpu.CompilerParams(vmem_limit_bytes=vmem),
        cost_estimate=pl.CostEstimate(flops=flops, bytes_accessed=moved, transcendentals=0),
    )


def edges_kernel(place, lagged, pair_out, cross_out, edges, sems):
    layers, tracers, dofs, columns = lagged.shape
    low = pltpu.make_async_copy(lagged.at[:, :, :, pl.ds(0, 128)], edges.at[0], sems.at[0])
    high = pltpu.make_async_copy(lagged.at[:, :, :, pl.ds(columns - 128, 128)], edges.at[1], sems.at[1])
    low.start()
    high.start()
    low.wait()
    high.wait()
    lane = lax.broadcasted_iota(jnp.int32, (dofs, 128), 1)
    packed = []
    for side, lane_at in ((0, 0), (1, 127)):
        value = jnp.zeros((dofs, 128), F32)
        for layer in range(layers):
            for tracer in range(tracers):
                column = edges[side, layer, tracer][:, lane_at : lane_at + 1]
                value = jnp.where(lane == layer * 2 * tracers + tracer, column, value)
        packed.append(value)
    first, last = packed
    odd = place[2] == 1
    pair_out[...] = jnp.where(odd, first, last)
    cross_out[...] = jnp.where(odd, last, first)


def tables_kernel(up, down, inverse, up_out, down_out, inv_out, ups, downs, inv, sems):
    dofs = inv.shape[0]
    copies = [
        pltpu.make_async_copy(source, target, sems.at[i])
        for i, (source, target) in enumerate(((up, ups), (down, downs), (inverse, inv)))
    ]
    for copy in copies:
        copy.start()
    for copy in copies:
        copy.wait()
    dinv = inv[...]
    for t in range(KINDS):
        for source, target in ((ups, up_out), (downs, down_out)):
            folded = jnp.dot(dinv, source[t], preferred_element_type=F32, precision=lax.Precision.HIGHEST)
            target[t * dofs : (t + 1) * dofs, :] = stacked_table(folded)
    inv_out[...] = stacked_table(dinv)


def local_forward_kernel(
    place, rhs, lagged, kinds, stream, span, absorb, table, inv_table,
    g_out, f_out, m0, m1, m2, m3,
):
    layer = pl.program_id(0)
    layers, tracers, dofs, columns = g_out.shape
    row = pl.ds(layer, 1)
    scale = stream[row, :]
    span_low = span[0, row, :]
    span_high = span[1, row, :]
    inv_denom = 1.0 / (scale + span_low + span_high + absorb[row, :])
    lane = lax.broadcasted_iota(jnp.int32, (1, columns), 1)
    weight_low = jnp.where(lane == 0, 0.0, inv_denom * span_low)
    weight_high = jnp.where(lane == columns - 1, 0.0, inv_denom * span_high)
    masks_low = kind_masks(pltpu.roll(kinds[1, row, :], columns - 1, 1), dofs)
    masks_high = kind_masks(pltpu.roll(kinds[2, row, :], 1, 1), dofs)
    for tracer in range(tracers):
        products = jnp.dot(table[...], stacked_state(lagged[0, tracer]), preferred_element_type=F32)
        low_term = pltpu.roll(select(products, masks_low), 1, 1)
        high_term = pltpu.roll(select(products, masks_high), columns - 1, 1)
        solved = jnp.dot(inv_table[...], stacked_state(rhs[0, tracer]), preferred_element_type=F32)
        g_out[layer, tracer] = inv_denom * solved - weight_low * low_term - weight_high * high_term

    @pl.when(layer == 0)
    def first():
        for tracer in range(tracers):
            f_out[0, tracer] = g_out[0, tracer]

    @pl.when(layer > 0)
    def later():
        masks = kind_masks(kinds[0, row, :], dofs)
        factor = scale * inv_denom
        for tracer in range(tracers):
            f_out[layer, tracer] = g_out[layer, tracer] - factor * typed(
                table[...], f_out[layer - 1, tracer], masks
            )

    @pl.when(layer == layers - 1)
    def send():
        width = columns // MEMBERS
        for k, target in enumerate((m0, m1, m2, m3)):
            own = pl.ds(pl.multiple_of((place[0] ^ k) * width, width), width)
            for tracer in range(tracers):
                target[tracer * dofs : (tracer + 1) * dofs, :] = f_out[layers - 1, tracer, :, own]
            top = tracers * dofs
            scales = stream[:, own]
            target[top : top + layers, :] = scales
            target[top + layers : top + 2 * layers, :] = 1.0 / (
                scales + span[0, :, own] + span[1, :, own] + absorb[:, own]
            )
            target[top + 2 * layers : top + 3 * layers, :] = kinds[0, :, own].astype(F32)
            if target.shape[0] > top + 3 * layers:
                target[top + 3 * layers :, :] = jnp.zeros((target.shape[0] - top - 3 * layers, width), F32)


def edge_fix_kernel(
    place, pair, cross, kinds, stream, span, absorb, table, m0, m1, m2, m3,
    g_fix, f_fix, o0, o1, o2, o3,
):
    layers, columns = stream.shape
    dofs = pair.shape[0]
    width = m0.shape[1]
    tracers = m0.shape[0] // dofs
    both = 2 * tracers
    for source, target in ((m0, o0), (m1, o1), (m2, o2), (m3, o3)):
        target[...] = source[...]
    odd = place[2] == 1
    from_low = jnp.where(odd, pair[...], cross[...])
    from_high = jnp.where(odd, cross[...], pair[...])
    lane = lax.broadcasted_iota(jnp.int32, (1, 128), 1)
    halo = jnp.where(lane % both < tracers, from_low, pltpu.roll(from_high, tracers, 1))
    side_kinds = jnp.zeros((1, 128), jnp.int32)
    own_kinds = jnp.zeros((1, 128), jnp.int32)
    weight = jnp.zeros((1, 128), F32)
    factor = jnp.zeros((1, 128), F32)
    for layer in range(layers):
        row = slice(layer, layer + 1)
        for side, tile, at in ((0, 0, 0), (1, columns - 128, 127)):
            def one(value):
                return value[:, at : at + 1]

            here = lane // tracers == 2 * layer + side
            cut = slice(tile, tile + 128)
            scale = stream[row, cut]
            inv_denom = 1.0 / (scale + span[0, row, cut] + span[1, row, cut] + absorb[row, cut])
            side_kinds = jnp.where(here, one(kinds[1 + side, row, cut]), side_kinds)
            own_kinds = jnp.where(here, one(kinds[0, row, cut]), own_kinds)
            weight = jnp.where(here, one(inv_denom * span[side, row, cut]), weight)
            if layer > 0:
                factor = jnp.where(here, one(inv_denom * scale), factor)
    change = -(weight * typed(table[...], halo, kind_masks(side_kinds, dofs)))
    g_fix[...] = change
    masks = kind_masks(own_kinds, dofs)
    running = change
    for layer in range(1, layers):
        running = change - factor * typed(table[...], pltpu.roll(running, both, 1), masks)
    f_fix[...] = running
    top = (layers - 1) * both
    for k, target in enumerate((o0, o1, o2, o3)):
        @pl.when(place[0] ^ k == 0)
        def low():
            for tracer in range(tracers):
                here = slice(tracer * dofs, (tracer + 1) * dofs)
                column = running[:, top + tracer : top + tracer + 1]
                target[here, 0:128] = target[here, 0:128] + jnp.where(lane == 0, column, 0.0)

        @pl.when(place[0] ^ k == MEMBERS - 1)
        def high():
            for tracer in range(tracers):
                here = slice(tracer * dofs, (tracer + 1) * dofs)
                at = top + tracers + tracer
                column = running[:, at : at + 1]
                target[here, width - 128 : width] = target[here, width - 128 : width] + jnp.where(
                    lane == 127, column, 0.0
                )


def with_edges(value, fix, layer, tracer, tracers):
    columns = value.shape[1]
    lane = lax.broadcasted_iota(jnp.int32, (1, 128), 1)
    at = layer * 2 * tracers + tracer
    low = value[:, :128] + jnp.where(lane == 0, fix[:, at : at + 1], 0.0)
    at = at + tracers
    high = value[:, columns - 128 :] + jnp.where(lane == 127, fix[:, at : at + 1], 0.0)
    return jnp.concatenate([low, value[:, 128 : columns - 128], high], axis=1)


def local_backward_kernel(
    place, f_in, f_fix, kinds, stream, span, absorb, table, m0, m1, m2, m3, carried
):
    layers, tracers, dofs, columns = f_in.shape
    for layer in reversed(range(layers)):
        row = slice(layer, layer + 1)
        scale = stream[row, :]
        inv_denom = 1.0 / (scale + span[0, row, :] + span[1, row, :] + absorb[row, :])
        masks = kind_masks(kinds[0, row, :], dofs)
        for tracer in range(tracers):
            solved = with_edges(f_in[layer, tracer], f_fix[...], layer, tracer, tracers)
            if layer < layers - 1:
                solved = solved - inv_denom * carried[tracer]
            carried[tracer] = scale * typed(table[...], solved, masks)
    width = columns // MEMBERS
    for k, target in enumerate((m0, m1, m2, m3)):
        own = pl.ds(pl.multiple_of((place[0] ^ k) * width, width), width)
        for tracer in range(tracers):
            target[tracer * dofs : (tracer + 1) * dofs, :] = carried[tracer, :, own]


def chain_rows(block_ref, top, layers, layer):
    def row(which):
        at = top + which * layers + layer
        return block_ref[at : at + 1, :]

    return row(0), row(1), row(2)


def forward_chain(turn, layers, tracers, table, blocks, entering, held, outflow):
    rows = entering.shape[1]
    dofs = rows // tracers
    for block in range(MEMBERS):
        idle = block == 0 and turn == 0
        values = [entering[block, r * dofs : (r + 1) * dofs, :] for r in range(tracers)]
        for layer in range(layers):
            if not idle:
                scale, inv_denom, kinds = chain_rows(blocks.at[block], rows, layers, layer)
                masks = kind_masks(kinds, dofs)
                factor = -(scale * inv_denom)
                values = [factor * typed(table[...], v, masks) for v in values]
            for r in range(tracers):
                held[block, layer, r * dofs : (r + 1) * dofs, :] = values[r]
        for r in range(tracers):
            here = slice(r * dofs, (r + 1) * dofs)
            value = values[r] + blocks[block, here, :]
            if block < MEMBERS - 1:
                entering[block + 1, here, :] = value
            elif outflow is not None:
                outflow[here, :] = value


def backward_chain(turn, layers, tracers, table, blocks, terms, entering, held, outflow):
    rows = entering.shape[1]
    dofs = rows // tracers
    for block in reversed(range(MEMBERS)):
        if block == 0 and turn == 0:
            continue
        values = [entering[block, r * dofs : (r + 1) * dofs, :] for r in range(tracers)]
        for layer in reversed(range(layers)):
            scale, inv_denom, kinds = chain_rows(blocks.at[block], rows, layers, layer)
            masks = kind_masks(kinds, dofs)
            values = [
                scale * typed(
                    table[...],
                    held[block, layer, r * dofs : (r + 1) * dofs, :] - inv_denom * values[r],
                    masks,
                )
                for r in range(tracers)
            ]
        for r in range(tracers):
            here = slice(r * dofs, (r + 1) * dofs)
            value = values[r] + terms[block, here, :]
            if block > 0:
                entering[block - 1, here, :] = value
            else:
                outflow[here, :] = value


def take(place, sources, target):
    for k, source in enumerate(sources):
        target[place[0] ^ k] = source[...]


def give(place, targets, source):
    for k, target in enumerate(targets):
        target[...] = source[place[0] ^ k]


def keep(place, turn, olds, targets):
    if olds:
        @pl.when(place[1] != turn)
        def passed():
            for old, target in zip(olds, targets):
                target[...] = old[...]


def chain_forward_kernel(turn, layers, tracers, place, inflow, table, m0, m1, m2, m3, *rest):
    olds, (states, o0, o1, o2, o3, outflow, blocks, entering) = rest[:-8], rest[-8:]
    outs = (o0, o1, o2, o3)

    @pl.when(place[1] == turn)
    def active():
        take(place, (m0, m1, m2, m3), blocks)
        entering[0] = inflow[...] if turn > 0 else jnp.zeros(inflow.shape, F32)
        forward_chain(turn, layers, tracers, table, blocks, entering, states, outflow)
        give(place, outs, entering)

    keep(place, turn, olds, outs)


def chain_last_kernel(
    turn, layers, tracers, place, inflow, up_table, down_table, m0, m1, m2, m3, e0, e1, e2, e3, *rest
):
    olds, (o0, o1, o2, o3, h0, h1, h2, h3, outflow, blocks, terms, entering, returning, held) = rest[:-14], rest[-14:]
    outs = (o0, o1, o2, o3)

    @pl.when(place[1] == turn)
    def active():
        take(place, (m0, m1, m2, m3), blocks)
        take(place, (e0, e1, e2, e3), terms)
        entering[0] = inflow[...] if turn > 0 else jnp.zeros(inflow.shape, F32)
        forward_chain(turn, layers, tracers, up_table, blocks, entering, held, None)
        returning[MEMBERS - 1] = jnp.zeros(inflow.shape, F32)
        backward_chain(turn, layers, tracers, down_table, blocks, terms, returning, held, outflow)
        give(place, outs, entering)
        give(place, (h0, h1, h2, h3), returning)

    keep(place, turn, olds, outs)


def chain_backward_kernel(
    turn, layers, tracers, place, inflow, table, m0, m1, m2, m3, e0, e1, e2, e3, states, *rest
):
    olds, (o0, o1, o2, o3, outflow, blocks, terms, returning) = rest[:-8], rest[-8:]
    outs = (o0, o1, o2, o3)

    @pl.when(place[1] == turn)
    def active():
        take(place, (m0, m1, m2, m3), blocks)
        take(place, (e0, e1, e2, e3), terms)
        returning[MEMBERS - 1] = inflow[...]
        backward_chain(turn, layers, tracers, table, blocks, terms, returning, states, outflow)
        give(place, outs, returning)

    keep(place, turn, olds, outs)


def take_inflow(place, sources, state):
    tracers, dofs, columns = state.shape
    width = columns // MEMBERS
    for k, source in enumerate(sources):
        own = pl.ds(pl.multiple_of((place[0] ^ k) * width, width), width)
        for tracer in range(tracers):
            state[tracer, :, own] = source[tracer * dofs : (tracer + 1) * dofs, :]


def final_forward_kernel(
    place, g_in, g_fix, kinds, stream, span, absorb, table, m0, m1, m2, m3, f_out, state
):
    layers, tracers, dofs, columns = g_in.shape
    take_inflow(place, (m0, m1, m2, m3), state)
    for layer in range(layers):
        row = slice(layer, layer + 1)
        scale = stream[row, :]
        factor = scale / (scale + span[0, row, :] + span[1, row, :] + absorb[row, :])
        masks = kind_masks(kinds[0, row, :], dofs)
        for tracer in range(tracers):
            before = state[tracer] if layer == 0 else f_out[layer - 1, tracer]
            here = with_edges(g_in[layer, tracer], g_fix[...], layer, tracer, tracers)
            f_out[layer, tracer] = here - factor * typed(table[...], before, masks)


def final_backward_kernel(
    place, f_in, kinds, stream, span, absorb, table, m0, m1, m2, m3, out, carried, solved, sems
):
    layers, tracers, dofs, columns = f_in.shape
    take_inflow(place, (m0, m1, m2, m3), carried)
    copies = []
    for layer in reversed(range(layers)):
        row = slice(layer, layer + 1)
        scale = stream[row, :]
        inv_denom = 1.0 / (scale + span[0, row, :] + span[1, row, :] + absorb[row, :])
        for tracer in range(tracers):
            solved[layer, tracer] = f_in[layer, tracer] - inv_denom * carried[tracer]
            if layer == 0:
                copies.append(pltpu.make_async_copy(solved.at[0, tracer], out.at[0, tracer], sems.at[layers + tracer]))
                copies[-1].start()
        if layer > 0:
            copies.append(pltpu.make_async_copy(solved.at[layer], out.at[layer], sems.at[layer]))
            copies[-1].start()
            masks = kind_masks(kinds[0, row, :], dofs)
            for tracer in range(tracers):
                carried[tracer] = scale * typed(table[...], solved[layer, tracer], masks)
    for copy in copies:
        copy.wait()


def whole(shape, dims):
    return pl.BlockSpec(shape, lambda *i: (0,) * dims)


def per_device(rhs, lagged, kinds, stream, span, absorb, up, down, inverse):
    layers, tracers, dofs, columns = rhs.shape
    rows = tracers * dofs
    width = columns // MEMBERS
    count = lax.axis_size("stream")
    groups = count // MEMBERS
    position = lax.axis_index("stream")
    place = jnp.stack(
        [position % MEMBERS, position // MEMBERS, lax.axis_index("span") % 2]
    ).astype(jnp.int32)
    long_rows = rows + -(-3 * layers // 8) * 8
    vmem, anywhere, smem = (pl.BlockSpec(memory_space=s) for s in (pltpu.VMEM, pl.ANY, pltpu.SMEM))
    full = functools.partial(jax.ShapeDtypeStruct, dtype=F32)
    field = 4 * rhs.size
    product = 2 * KINDS * dofs * 4 * dofs * tracers * columns
    some = 12 << 20
    table_shape = (KINDS * dofs, 4 * dofs)

    pair_edge, cross_edge = pl.pallas_call(
        edges_kernel,
        out_shape=(full((dofs, 128)),) * 2,
        in_specs=[smem, anywhere],
        out_specs=(vmem,) * 2,
        scratch_shapes=[
            pltpu.VMEM((2, layers, tracers, dofs, 128), F32),
            pltpu.SemaphoreType.DMA((2,)),
        ],
        name="edges",
        **params(1 << 20, 1 << 20, some),
    )(place, lagged)
    across = lax.axis_size("span")
    crossing = [(i, i + 1) for i in range(1, across - 1, 2)]
    pair = lax.ppermute(pair_edge, "span", [(i, i ^ 1) for i in range(across)])
    cross = lax.ppermute(cross_edge, "span", crossing + [(b, a) for a, b in crossing])

    up_table, down_table, inv_table = pl.pallas_call(
        tables_kernel,
        out_shape=(
            jax.ShapeDtypeStruct(table_shape, BF16),
            jax.ShapeDtypeStruct(table_shape, BF16),
            jax.ShapeDtypeStruct((dofs, 4 * dofs), BF16),
        ),
        in_specs=[anywhere] * 3,
        out_specs=(vmem,) * 3,
        scratch_shapes=[
            pltpu.VMEM(up.shape, F32),
            pltpu.VMEM(down.shape, F32),
            pltpu.VMEM(inverse.shape, F32),
            pltpu.SemaphoreType.DMA((3,)),
        ],
        name="tables",
        **params(1 << 24, 1 << 20, some),
    )(up, down, inverse)

    def exchanged(messages):
        return [messages[0]] + [
            lax.ppermute(messages[k], "stream", [(i, i ^ k) for i in range(count)])
            for k in range(1, MEMBERS)
        ]

    def between(values, step):
        pairs = [(step * MEMBERS + i, (step + 1) * MEMBERS + i) for i in range(MEMBERS)]
        return lax.ppermute(values, "stream", pairs + [(b, a) for a, b in pairs])

    layer_block = pl.BlockSpec((1, tracers, dofs, columns), lambda i: (i, 0, 0, 0))
    small = (kinds, stream, span, absorb)
    small_blocks = [
        whole((3, layers, columns), 3),
        whole((layers, columns), 2),
        whole((2, layers, columns), 3),
        whole((layers, columns), 2),
    ]
    column_state = pltpu.VMEM((tracers, dofs, columns), F32)
    message = full((rows, width))
    long_message = full((long_rows, width))
    fix = full((dofs, 128))

    g, f_zero, *out_b = pl.pallas_call(
        local_forward_kernel,
        grid=(layers,),
        out_shape=(full(rhs.shape), full(rhs.shape)) + (long_message,) * MEMBERS,
        in_specs=[smem, layer_block, layer_block] + small_blocks
        + [whole(table_shape, 2), whole((dofs, 4 * dofs), 2)],
        out_specs=(whole(rhs.shape, 4),) * 2 + (whole((long_rows, width), 2),) * MEMBERS,
        name="local_forward",
        **params(3 * layers * product, 8 * rhs.size, some + 2 * field + (16 << 20)),
    )(place, rhs, lagged, *small, up_table, inv_table)

    g_fix, f_fix, *out_b = pl.pallas_call(
        edge_fix_kernel,
        out_shape=(fix, fix) + (long_message,) * MEMBERS,
        in_specs=[smem] + [vmem] * (7 + MEMBERS),
        out_specs=(vmem,) * (2 + MEMBERS),
        name="edge_fix",
        **params(1 << 24, 1 << 20, some),
    )(place, pair, cross, *small, up_table, *out_b)
    in_b = exchanged(out_b)

    out_e = pl.pallas_call(
        local_backward_kernel,
        out_shape=(message,) * MEMBERS,
        in_specs=[smem] + [vmem] * 7,
        out_specs=(vmem,) * MEMBERS,
        scratch_shapes=[column_state],
        name="local_backward",
        **params(layers * product, 4 * rhs.size, some + field),
    )(place, f_zero, f_fix, *small, down_table)
    in_e = exchanged(out_e)
    in_b, _ = lax.optimization_barrier((in_b, out_e))

    blocks = pltpu.VMEM((MEMBERS, long_rows, width), F32)
    inner = pltpu.VMEM((MEMBERS, rows, width), F32)
    held = (MEMBERS, layers, rows, width)
    inflow = jnp.zeros((rows, width), F32)
    states, out_f = [], []
    for turn in range(groups - 1):
        state, *out_f, outflow = pl.pallas_call(
            functools.partial(chain_forward_kernel, turn, layers, tracers),
            out_shape=(full(held),) + (message,) * (MEMBERS + 1),
            in_specs=[smem] + [vmem] * (2 + MEMBERS + len(out_f)),
            out_specs=(vmem,) * (MEMBERS + 2),
            scratch_shapes=[blocks, inner],
            name=f"chain_forward_{turn}",
            **params(layers * product, 8 * rhs.size, some + field),
        )(place, inflow, up_table, *in_b, *out_f)
        states.append(state)
        inflow = between(outflow, turn)

    *out_f, h0, h1, h2, h3, outflow = pl.pallas_call(
        functools.partial(chain_last_kernel, groups - 1, layers, tracers),
        out_shape=(message,) * (2 * MEMBERS + 1),
        in_specs=[smem] + [vmem] * (3 + 2 * MEMBERS + len(out_f)),
        out_specs=(vmem,) * (2 * MEMBERS + 1),
        scratch_shapes=[blocks, inner, inner, inner, pltpu.VMEM(held, F32)],
        name="chain_last",
        **params(2 * layers * product, 8 * rhs.size, some + 2 * field),
    )(place, inflow, up_table, down_table, *in_b, *in_e, *out_f)
    in_f = exchanged(out_f)

    out_h = [h0, h1, h2, h3]
    for turn in reversed(range(groups - 1)):
        inflow = between(outflow, turn)
        *out_h, outflow = pl.pallas_call(
            functools.partial(chain_backward_kernel, turn, layers, tracers),
            out_shape=(message,) * (MEMBERS + 1),
            in_specs=[smem] + [vmem] * (3 + 3 * MEMBERS),
            out_specs=(vmem,) * (MEMBERS + 1),
            scratch_shapes=[blocks, inner, inner],
            name=f"chain_backward_{turn}",
            **params(layers * product, 8 * rhs.size, some + field),
        )(place, inflow, down_table, *in_b, *in_e, states[turn], *out_h)
    in_h = exchanged(out_h)

    f_part = pl.pallas_call(
        final_forward_kernel,
        out_shape=full(rhs.shape),
        in_specs=[smem] + [vmem] * (7 + MEMBERS),
        out_specs=vmem,
        scratch_shapes=[column_state],
        name="final_forward",
        **params(layers * product, 8 * rhs.size, some + 2 * field),
    )(place, g, g_fix, *small, up_table, *in_f)
    return pl.pallas_call(
        final_backward_kernel,
        out_shape=full(rhs.shape),
        in_specs=[smem] + [vmem] * (6 + MEMBERS),
        out_specs=anywhere,
        scratch_shapes=[
            column_state,
            pltpu.VMEM(rhs.shape, F32),
            pltpu.SemaphoreType.DMA((layers + tracers,)),
        ],
        name="final_backward",
        **params(layers * product, 8 * rhs.size, some + 2 * field),
    )(place, f_part, *small, down_table, *in_h)


def solution(mesh):
    return jax.shard_map(
        per_device,
        mesh=mesh,
        in_specs=(
            P("stream", None, None, "span"),
            P("stream", None, None, "span"),
            P(None, "stream", "span"),
            P("stream", "span"),
            P(None, "stream", "span"),
            P("stream", "span"),
            P(),
            P(),
            P(),
        ),
        out_specs=P("stream", None, None, "span"),
        check_vma=False,
    )
```

time: 567 us -> 110 us (0.19); the launches traced: 557 us -> 109 us
  waiting for transfers between devices: 257 us -> 32.7 us
  matrix products: 143 us -> 0 us
  starting transfers between devices: 117 us -> 28.4 us
  Pallas kernels: 0 us -> 39.3 us
  other arithmetic: 17.3 us -> 0.08 us
  local copies, waits for them, and re-layouts: 20.5 us -> 8.48 us
    ppermute x24 -> x16, waiting for transfers between devices: 257 us -> 32.7 us  [the longest x12 22.3 us: exchanged(): lax.ppermute(messages[k], 'stream', [(i, i ^ k) for i in range(count)])]
    dot_general x72 -> x0, matrix products: 143 us -> none  [the longest x40 96.3 us: typed_product(): jnp.einsum('tpq,rqw->trpw', blocks_table, state_in, precision=precise)]
    ppermute x24 -> x16, starting transfers between devices: 117 us -> 28.4 us  [the longest x12 14.8 us: exchanged(): lax.ppermute(messages[k], 'stream', [(i, i ^ k) for i in range(count)])]
    pallas_call x0 -> x10, Pallas kernels: none -> 39.3 us  [the longest x1 12.2 us: per_device(): pl.pallas_call(local_forward_kernel, grid=(layers,), out_shape=(full(rhs....]
    dynamic_update_slice x8 -> x0, other arithmetic: 12.6 us -> none  [the longest x4 8.33 us: forward_block(): lax.dynamic_update_slice_in_dim(forward_part, jnp.stack(results), offset, 3)]
    another operation x18 -> x0, local copies, waits for them, and re-layouts: 10.1 us -> none
  transfers between devices with their start and end apart: 24 -> 16, of which waited for: 22 -> 8; matrix products, arithmetic and copies ran while one was open for 7% -> 0% of each run, Pallas kernels for 0% -> 29%
where the time goes in v2:
time: 110 us; the launch traced here: 109 us
  Pallas kernels  39.3 us (36%)
  waiting for transfers between devices  32.7 us (30%)
  starting transfers between devices  28.4 us (26%)
  local copies, waits for them, and re-layouts  8.48 us (8%)
    ppermute x12, waiting for transfers between devices, exchanged(): lax.ppermute(messages[k], 'stream', [(i, i ^ k) for i in range(count)])  22.3 us
    ppermute x12, starting transfers between devices, exchanged(): lax.ppermute(messages[k], 'stream', [(i, i ^ k) for i in range(count)])  14.8 us
    ppermute x2, starting transfers between devices, between(): return lax.ppermute(values, 'stream', pairs + [(b, a) for a, b in pairs])  12.4 us
    pallas_call x1, Pallas kernels, per_device(): pl.pallas_call(local_forward_kernel, grid=(layers,), out_shape=(full(rhs....  12.2 us
    ppermute x2, waiting for transfers between devices, between(): return lax.ppermute(values, 'stream', pairs + [(b, a) for a, b in pairs])  10.3 us
    unnamed x20, local copies, waits for them, and re-layouts  8.46 us
    pallas_call x1, Pallas kernels, per_device(): pl.pallas_call(functools.partial(chain_backward_kernel, turn, layers, tra...  5.11 us
    pallas_call x1, Pallas kernels, per_device(): pl.pallas_call(final_backward_kernel, out_shape=full(rhs.shape), in_specs...  4.31 us
  transfers between devices with their start and end apart: 16, of which 8 were waited for; matrix products, arithmetic and copies ran while one was open for 0% of the time, Pallas kernels for 29%

profile of v2, /device:TPU:0, one launch (start us, length us, event | category | flops | bytes accessed | tf_op | source)
XLA Modules:
  0.0 109.3 jit_solution(15700876130321992201)
XLA Ops:
  0.1 2.2 %copy-done = f32[4,4,64,1024]{3,2,1,0:T(8,128)S(1)} copy-done((f32[4,4,64,1024]{3,2,1,0:T(8,128)S(1)}, f32[4,4,64,1024]{3,2,1,0:T(8,128)}, u32[]{:S(2)}) %copy-start) | copy-done | bytes 4194328
  2.3 1.1 edges.1
  4.5 0.9 copy-done.2
  5.4 0.9 copy-done.3
  6.4 0.8 copy-done.6
  7.1 1.1 tables.1
  8.3 0.7 copy-done.5
  9.7 2.2 %copy-done.9 = f32[4,4,64,1024]{3,2,1,0:T(8,128)S(1)} copy-done((f32[4,4,64,1024]{3,2,1,0:T(8,128)S(1)}, f32[4,4,64,1024]{3,2,1,0:T(8,128)}, u32[]{:S(2)}) %copy-start.9) | copy-done | bytes 4194328
  11.9 12.2 %local_forward.1 = (f32[4,4,64,1024]{3,2,1,0:T(8,128)S(1)}, f32[4,4,64,1024]{3,2,1,0:T(8,128)S(1)}, f32[272,256]{1,0:T(8,128)S(1)}, f32[272,256]{1,0:T(8,128)S(1...) custom-call(s32[3]{0:T(128)S(1)} %pad_add_fusion.place, f32[4,4,64,1024]{3,2,1,0:T(8,128)S(1)} %copy-done.9, ...), custom_call_target="tpu_custom_call" | custom-call | flops 9663676416 | bytes 8388608 | tf_op jit(solution)/shard_map/local_forward/pallas_call | solution.py:503
  24.2 2.1 %edge_fix.1 = (f32[64,128]{1,0:T(8,128)S(1)}, f32[64,128]{1,0:T(8,128)S(1)}, f32[272,256]{1,0:T(8,128)S(1)}, f32[272,256]{1,0:T(8,128)S(1)}, f32[272,256]{1,0:T(8,128)S(1)}, /*index=5*/f32[272,256]{1,0:T(8,128)S(1)}) custom-call(s32[3]{0:T(128)S(1)} %pad_add_fusion.place, f32[64,128]{1,0:T(8,128)S(1)} %collective-permute-done.pair, ...), custom_call_target="tpu_custom_call" | custom-call | flops 16777216 | bytes 1048576 | tf_op jit(solution)/shard_map/edge_fix/pallas_call | solution.py:514
  26.3 2.7 %collective-permute-start.2 = (f32[272,256]{1,0:T(8,128)S(1)}, f32[272,256]{1,0:T(8,128)S(1)}, u32[]{:S(2)}, u32[]{:S(2)}) collective-permute-start(f32[272,256]{1,0:T(8,128)S(1)} %get-tuple-element.60), channel_id=1, source_target_pairs={{0,4},{4,0},{8,12},{12,8},{16,20},{20,16},{24,28},{28,24},{1,5},{5... | collective-permute-start | bytes 835592 | tf_op jit(solution)/shard_map/ppermute | solution.py:482
  29.0 1.6 %collective-permute-start.3 = (f32[272,256]{1,0:T(8,128)S(1)}, f32[272,256]{1,0:T(8,128)S(1)}, u32[]{:S(2)}, u32[]{:S(2)}) collective-permute-start(f32[272,256]{1,0:T(8,128)S(1)} %get-tuple-element.61), channel_id=1, source_target_pairs={{0,8},{4,12},{8,0},{12,4},{16,24},{20,28},{24,16},{28,20},{1,9},{5... | collective-permute-start | bytes 835592 | tf_op jit(solution)/shard_map/ppermute | solution.py:482
  30.6 4.3 %local_backward.1 = (f32[256,256]{1,0:T(8,128)S(1)}, f32[256,256]{1,0:T(8,128)S(1)}, f32[256,256]{1,0:T(8,128)S(1)}, f32[256,256]{1,0:T(8,128)S(1)}) custom-call(s32[3]{0:T(128)S(1)} %pad_add_fusion.place, f32[4,4,64,1024]{3,2,1,0:T(8,128)S(1)} %get-tuple-element.63.f_in, f32[64,128]{1,0:T(8,128)S(1)} %get-tuple-element.64.f_fix, ...), custom_call_target="tpu_custom_call" | custom-call | flops 3221225472 | bytes 4194304 | tf_op jit(solution)/shard_map/local_backward/pallas_call | solution.py:524
  34.9 2.0 %collective-permute-start.6 = (f32[256,256]{1,0:T(8,128)S(1)}, f32[256,256]{1,0:T(8,128)S(1)}, u32[]{:S(2)}, u32[]{:S(2)}) collective-permute-start(f32[256,256]{1,0:T(8,128)S(1)} %get-tuple-element.67), channel_id=1, source_target_pairs={{0,4},{4,0},{8,12},{12,8},{16,20},{20,16},{24,28},{28,24},{1,5},{5... | collective-permute-start | bytes 786440 | tf_op jit(solution)/shard_map/ppermute | solution.py:482
  36.9 1.6 %collective-permute-start.7 = (f32[256,256]{1,0:T(8,128)S(1)}, f32[256,256]{1,0:T(8,128)S(1)}, u32[]{:S(2)}, u32[]{:S(2)}) collective-permute-start(f32[256,256]{1,0:T(8,128)S(1)} %get-tuple-element.68), channel_id=1, source_target_pairs={{0,8},{4,12},{8,0},{12,4},{16,24},{20,28},{24,16},{28,20},{1,9},{5... | collective-permute-start | bytes 786440 | tf_op jit(solution)/shard_map/ppermute | solution.py:482
  38.5 3.5 %collective-permute-done.4.m3 = f32[272,256]{1,0:T(8,128)S(1)} collective-permute-done((f32[272,256]{1,0:T(8,128)S(1)}, f32[272,256]{1,0:T(8,128)S(1)}, u32[]{:S(2)}, u32[]{:S(2)}) %collective-permute-start.4) | collective-permute-done | bytes 278560 | tf_op jit(solution)/shard_map/ppermute | solution.py:482
  42.0 4.3 %chain_forward_0.1 = (f32[4,4,256,256]{3,2,1,0:T(8,128)S(1)}, f32[256,256]{1,0:T(8,128)S(1)}, f32[256,256]{1,0:T(8,128)S(1)}, f32[256,256]{1,0:T(8,128)S(1)}, f3...) custom-call(s32[3]{0:T(128)S(1)} %pad_add_fusion.place, f32[256,256]{1,0:T(8,128)S(1)} %broadcast_in_dim.3.inflow, ...), custom_call_target="tpu_custom_call" | custom-call | flops 3221225472 | bytes 8388608 | tf_op jit(solution)/shard_map/chain_forward_0/pallas_call | solution.py:542
  46.4 2.1 %collective-permute-done.6.e1 = f32[256,256]{1,0:T(8,128)S(1)} collective-permute-done((f32[256,256]{1,0:T(8,128)S(1)}, f32[256,256]{1,0:T(8,128)S(1)}, u32[]{:S(2)}, u32[]{:S(2)}) %collective-permute-start.6) | collective-permute-done | bytes 262176 | tf_op jit(solution)/shard_map/ppermute | solution.py:482
  48.5 8.6 %collective-permute-done.8.e3 = f32[256,256]{1,0:T(8,128)S(1)} collective-permute-done((f32[256,256]{1,0:T(8,128)S(1)}, f32[256,256]{1,0:T(8,128)S(1)}, u32[]{:S(2)}, u32[]{:S(2)}) %collective-permute-start.8) | collective-permute-done | bytes 262176 | tf_op jit(solution)/shard_map/ppermute | solution.py:482
  57.1 1.7 %collective-permute-done.5.inflow = f32[256,256]{1,0:T(8,128)S(1)} collective-permute-done((f32[256,256]{1,0:T(8,128)S(1)}, f32[256,256]{1,0:T(8,128)S(1)}, u32[]{:S(2)}, u32[]{:S(2)}) %collective-permute-start.5) | collective-permute-done | bytes 262176 | tf_op jit(solution)/shard_map/ppermute | solution.py:488
  59.4 12.3 %collective-permute-start.12 = (f32[256,256]{1,0:T(8,128)S(1)}, f32[256,256]{1,0:T(8,128)S(1)}, u32[]{:S(2)}, u32[]{:S(2)}) collective-permute-start(f32[256,256]{1,0:T(8,128)S(1)} %get-tuple-element.83), channel_id=1, source_target_pairs={{0,16},{4,20},{8,24},{12,28},{16,0},{20,4},{24,8},{28,12},{1,17},{... | collective-permute-start | bytes 786440 | tf_op jit(solution)/shard_map/ppermute | solution.py:488
  71.8 1.5 %collective-permute-start.10 = (f32[256,256]{1,0:T(8,128)S(1)}, f32[256,256]{1,0:T(8,128)S(1)}, u32[]{:S(2)}, u32[]{:S(2)}) collective-permute-start(f32[256,256]{1,0:T(8,128)S(1)} %get-tuple-element.81), channel_id=1, source_target_pairs={{0,8},{4,12},{8,0},{12,4},{16,24},{20,28},{24,16},{28,20},{1,9},{5... | collective-permute-start | bytes 786440 | tf_op jit(solution)/shard_map/ppermute | solution.py:482
  73.3 1.1 collective-permute-start.11
  74.4 0.9 collective-permute-start.9
  75.3 8.6 %collective-permute-done.12.inflow = f32[256,256]{1,0:T(8,128)S(1)} collective-permute-done((f32[256,256]{1,0:T(8,128)S(1)}, f32[256,256]{1,0:T(8,128)S(1)}, u32[]{:S(2)}, u32[]{:S(2)}) %collective-permute-start.12) | collective-permute-done | bytes 262176 | tf_op jit(solution)/shard_map/ppermute | solution.py:488
  83.9 5.1 %chain_backward_0.1 = (f32[256,256]{1,0:T(8,128)S(1)}, f32[256,256]{1,0:T(8,128)S(1)}, f32[256,256]{1,0:T(8,128)S(1)}, f32[256,256]{1,0:T(8,128)S(1)}, f32[256,256]{1,0:T(8,128)}) custom-call(s32[3]{0:T(128)S(1)} %pad_add_fusion.place, f32[256,256]{1,0:T(8,128)S(1)} %collective-permute-done.12.inflow, ...), custom_call_target="tpu_custom_call" | custom-call | flops 3221225472 | bytes 8388608 | tf_op jit(solution)/shard_map/chain_backward_0/pallas_call | solution.py:568
  89.6 1.7 %collective-permute-start.14 = (f32[256,256]{1,0:T(8,128)S(1)}, f32[256,256]{1,0:T(8,128)S(1)}, u32[]{:S(2)}, u32[]{:S(2)}) collective-permute-start(f32[256,256]{1,0:T(8,128)S(1)} %get-tuple-element.91), channel_id=1, source_target_pairs={{0,8},{4,12},{8,0},{12,4},{16,24},{20,28},{24,16},{28,20},{1,9},{5... | collective-permute-start | bytes 786440 | tf_op jit(solution)/shard_map/ppermute | solution.py:482
  91.3 1.2 %collective-permute-start.15 = (f32[256,256]{1,0:T(8,128)S(1)}, f32[256,256]{1,0:T(8,128)S(1)}, u32[]{:S(2)}, u32[]{:S(2)}) collective-permute-start(f32[256,256]{1,0:T(8,128)S(1)} %get-tuple-element.92), channel_id=1, source_target_pairs={{0,12},{4,8},{8,4},{12,0},{16,28},{20,24},{24,20},{28,16},{1,13},{... | collective-permute-start | bytes 786440 | tf_op jit(solution)/shard_map/ppermute | solution.py:482
  92.5 4.3 %final_forward.1.f_in = f32[4,4,64,1024]{3,2,1,0:T(8,128)S(1)} custom-call(s32[3]{0:T(128)S(1)} %pad_add_fusion.place, f32[4,4,64,1024]{3,2,1,0:T(8,128)S(1)} %get-tuple-element.51.g_in, f32[64,128]{1,0:T(8,128)S(1)} %get-tuple-element.58.g_fix, s32[3,4,1024]{2,1,0:T(4,128)S(1)} %copy-done.4, f32[4,1024]{1,0:T(4,128)S(1)} %copy-done.7, ...), custom_call_target="tpu_custom_call" | custom-call | flops 3221225472 | bytes 8388608 | tf_op jit(solution)/shard_map/final_forward/pallas_call | solution.py:579
  96.7 1.3 %collective-permute-done.13.m1 = f32[256,256]{1,0:T(8,128)S(1)} collective-permute-done((f32[256,256]{1,0:T(8,128)S(1)}, f32[256,256]{1,0:T(8,128)S(1)}, u32[]{:S(2)}, u32[]{:S(2)}) %collective-permute-start.13) | collective-permute-done | bytes 262176 | tf_op jit(solution)/shard_map/ppermute | solution.py:482
  98.7 6.1 %collective-permute-done.15.m3 = f32[256,256]{1,0:T(8,128)S(1)} collective-permute-done((f32[256,256]{1,0:T(8,128)S(1)}, f32[256,256]{1,0:T(8,128)S(1)}, u32[]{:S(2)}, u32[]{:S(2)}) %collective-permute-start.15) | collective-permute-done | bytes 262176 | tf_op jit(solution)/shard_map/ppermute | solution.py:482
  104.8 4.3 %final_backward.1 = f32[4,4,64,1024]{3,2,1,0:T(8,128)} custom-call(s32[3]{0:T(128)S(1)} %pad_add_fusion.place, f32[4,4,64,1024]{3,2,1,0:T(8,128)S(1)} %final_forward.1.f_in, s32[3,4,1024]{2,1,0:T(4,128)S(1)} %copy-done.4, f32[4,1024]{1,0:T(4,128)S(1)} %copy-done.7, f32[2,4,1024]{2,1,0:T(4,128)S(1)} %copy-done.5, f32[4,1024]{1,0:T(4,128)S(1)} %copy-done.8, ...), custom_call_target="tpu_custom_call" | custom-call | flops 3221225472 | bytes 8388608 | tf_op jit(solution)/shard_map/final_backward/pallas_call | solution.py:588
  (32 shorter events, 4.1 us)
Async XLA Ops:
  0.0 8.2 %copy-start.4 = (s32[3,4,1024]{2,1,0:T(4,128)S(1)}, s32[3,4,1024]{2,1,0:T(4,128)}, u32[]{:S(2)}) copy-start(s32[3,4,1024]{2,1,0:T(4,128)} %kinds.9) | copy-start | bytes 147460
  0.0 8.2 %copy-start.7 = (f32[4,1024]{1,0:T(4,128)S(1)}, f32[4,1024]{1,0:T(4,128)}, u32[]{:S(2)}) copy-start(f32[4,1024]{1,0:T(4,128)} %stream.9) | copy-start | bytes 49156
  0.1 2.2 %copy-start = (f32[4,4,64,1024]{3,2,1,0:T(8,128)S(1)}, f32[4,4,64,1024]{3,2,1,0:T(8,128)}, u32[]{:S(2)}) copy-start(f32[4,4,64,1024]{3,2,1,0:T(8,128)} %lagged.3) | copy-start | bytes 12582916
  2.3 6.0 %copy-start.1 = (f32[4,4,64,1024]{3,2,1,0:T(8,128)S(1)}, f32[4,4,64,1024]{3,2,1,0:T(8,128)}, u32[]{:S(2)}) copy-start(f32[4,4,64,1024]{3,2,1,0:T(8,128)} %lagged.3) | copy-start | bytes 12582916
  3.3 20.8 %collective-permute-start = (f32[64,128]{1,0:T(8,128)S(1)}, f32[64,128]{1,0:T(8,128)S(1)}, u32[]{:S(2)}, u32[]{:S(2)}) collective-permute-start(f32[64,128]{1,0:T(8,128)S(1)} %get-tuple-element.52), channel_id=1, source_target_pairs={{0,1},{1,0},{2,3},{3,2},{4,5},{5,4},{6,7},{7,6},{8,9},{9,8},{10,11... | collective-permute-start | bytes 98312 | tf_op jit(solution)/shard_map/ppermute | solution.py:458
  3.9 20.3 %collective-permute-start.1 = (f32[64,128]{1,0:T(8,128)S(1)}, f32[64,128]{1,0:T(8,128)S(1)}, u32[]{:S(2)}, u32[]{:S(2)}) collective-permute-start(f32[64,128]{1,0:T(8,128)S(1)} %get-tuple-element.53), channel_id=1, source_target_pairs={{1,2},{2,1},{5,6},{6,5},{9,10},{10,9},{13,14},{14,13},{17,18},{18,... | collective-permute-start | bytes 98312 | tf_op jit(solution)/shard_map/ppermute | solution.py:459
  4.5 0.9 copy-start.2
  5.4 0.9 copy-start.3
  6.4 0.8 copy-start.6
  8.3 0.8 copy-start.5
  9.0 0.7 copy-start.8
  9.7 2.2 %copy-start.9 = (f32[4,4,64,1024]{3,2,1,0:T(8,128)S(1)}, f32[4,4,64,1024]{3,2,1,0:T(8,128)}, u32[]{:S(2)}) copy-start(f32[4,4,64,1024]{3,2,1,0:T(8,128)} %rhs.1) | copy-start | bytes 12582916
  26.3 12.2 %collective-permute-start.2 = (f32[272,256]{1,0:T(8,128)S(1)}, f32[272,256]{1,0:T(8,128)S(1)}, u32[]{:S(2)}, u32[]{:S(2)}) collective-permute-start(f32[272,256]{1,0:T(8,128)S(1)} %get-tuple-element.60), channel_id=1, source_target_pairs={{0,4},{4,0},{8,12},{12,8},{16,20},{20,16},{24,28},{28,24},{1,5},{5... | collective-permute-start | bytes 835592 | tf_op jit(solution)/shard_map/ppermute | solution.py:482
  29.0 9.5 %collective-permute-start.3 = (f32[272,256]{1,0:T(8,128)S(1)}, f32[272,256]{1,0:T(8,128)S(1)}, u32[]{:S(2)}, u32[]{:S(2)}) collective-permute-start(f32[272,256]{1,0:T(8,128)S(1)} %get-tuple-element.61), channel_id=1, source_target_pairs={{0,8},{4,12},{8,0},{12,4},{16,24},{20,28},{24,16},{28,20},{1,9},{5... | collective-permute-start | bytes 835592 | tf_op jit(solution)/shard_map/ppermute | solution.py:482
  30.6 11.4 %collective-permute-start.4 = (f32[272,256]{1,0:T(8,128)S(1)}, f32[272,256]{1,0:T(8,128)S(1)}, u32[]{:S(2)}, u32[]{:S(2)}) collective-permute-start(f32[272,256]{1,0:T(8,128)S(1)} %get-tuple-element.62), channel_id=1, source_target_pairs={{0,12},{4,8},{8,4},{12,0},{16,28},{20,24},{24,20},{28,16},{1,13},{... | collective-permute-start | bytes 835592 | tf_op jit(solution)/shard_map/ppermute | solution.py:482
  34.9 13.6 %collective-permute-start.6 = (f32[256,256]{1,0:T(8,128)S(1)}, f32[256,256]{1,0:T(8,128)S(1)}, u32[]{:S(2)}, u32[]{:S(2)}) collective-permute-start(f32[256,256]{1,0:T(8,128)S(1)} %get-tuple-element.67), channel_id=1, source_target_pairs={{0,4},{4,0},{8,12},{12,8},{16,20},{20,16},{24,28},{28,24},{1,5},{5... | collective-permute-start | bytes 786440 | tf_op jit(solution)/shard_map/ppermute | solution.py:482
  36.9 11.6 %collective-permute-start.7 = (f32[256,256]{1,0:T(8,128)S(1)}, f32[256,256]{1,0:T(8,128)S(1)}, u32[]{:S(2)}, u32[]{:S(2)}) collective-permute-start(f32[256,256]{1,0:T(8,128)S(1)} %get-tuple-element.68), channel_id=1, source_target_pairs={{0,8},{4,12},{8,0},{12,4},{16,24},{20,28},{24,16},{28,20},{1,9},{5... | collective-permute-start | bytes 786440 | tf_op jit(solution)/shard_map/ppermute | solution.py:482
  38.4 18.6 %collective-permute-start.8 = (f32[256,256]{1,0:T(8,128)S(1)}, f32[256,256]{1,0:T(8,128)S(1)}, u32[]{:S(2)}, u32[]{:S(2)}) collective-permute-start(f32[256,256]{1,0:T(8,128)S(1)} %get-tuple-element.69), channel_id=1, source_target_pairs={{0,12},{4,8},{8,4},{12,0},{16,28},{20,24},{24,20},{28,16},{1,13},{... | collective-permute-start | bytes 786440 | tf_op jit(solution)/shard_map/ppermute | solution.py:482
  46.3 12.5 %collective-permute-start.5 = (f32[256,256]{1,0:T(8,128)S(1)}, f32[256,256]{1,0:T(8,128)S(1)}, u32[]{:S(2)}, u32[]{:S(2)}) collective-permute-start(f32[256,256]{1,0:T(8,128)S(1)} %get-tuple-element.74), channel_id=1, source_target_pairs={{0,16},{4,20},{8,24},{12,28},{16,0},{20,4},{24,8},{28,12},{1,17},{... | collective-permute-start | bytes 786440 | tf_op jit(solution)/shard_map/ppermute | solution.py:488
  59.4 24.4 %collective-permute-start.12 = (f32[256,256]{1,0:T(8,128)S(1)}, f32[256,256]{1,0:T(8,128)S(1)}, u32[]{:S(2)}, u32[]{:S(2)}) collective-permute-start(f32[256,256]{1,0:T(8,128)S(1)} %get-tuple-element.83), channel_id=1, source_target_pairs={{0,16},{4,20},{8,24},{12,28},{16,0},{20,4},{24,8},{28,12},{1,17},{... | collective-permute-start | bytes 786440 | tf_op jit(solution)/shard_map/ppermute | solution.py:488
  71.8 19.5 %collective-permute-start.10 = (f32[256,256]{1,0:T(8,128)S(1)}, f32[256,256]{1,0:T(8,128)S(1)}, u32[]{:S(2)}, u32[]{:S(2)}) collective-permute-start(f32[256,256]{1,0:T(8,128)S(1)} %get-tuple-element.81), channel_id=1, source_target_pairs={{0,8},{4,12},{8,0},{12,4},{16,24},{20,28},{24,16},{28,20},{1,9},{5... | collective-permute-start | bytes 786440 | tf_op jit(solution)/shard_map/ppermute | solution.py:482
  73.3 19.2 %collective-permute-start.11 = (f32[256,256]{1,0:T(8,128)S(1)}, f32[256,256]{1,0:T(8,128)S(1)}, u32[]{:S(2)}, u32[]{:S(2)}) collective-permute-start(f32[256,256]{1,0:T(8,128)S(1)} %get-tuple-element.82), channel_id=1, source_target_pairs={{0,12},{4,8},{8,4},{12,0},{16,28},{20,24},{24,20},{28,16},{1,13},{... | collective-permute-start | bytes 786440 | tf_op jit(solution)/shard_map/ppermute | solution.py:482
  74.4 18.1 %collective-permute-start.9 = (f32[256,256]{1,0:T(8,128)S(1)}, f32[256,256]{1,0:T(8,128)S(1)}, u32[]{:S(2)}, u32[]{:S(2)}) collective-permute-start(f32[256,256]{1,0:T(8,128)S(1)} %get-tuple-element.80), channel_id=1, source_target_pairs={{0,4},{4,0},{8,12},{12,8},{16,20},{20,16},{24,28},{28,24},{1,5},{5... | collective-permute-start | bytes 786440 | tf_op jit(solution)/shard_map/ppermute | solution.py:482
  89.0 9.1 %collective-permute-start.13 = (f32[256,256]{1,0:T(8,128)S(1)}, f32[256,256]{1,0:T(8,128)S(1)}, u32[]{:S(2)}, u32[]{:S(2)}) collective-permute-start(f32[256,256]{1,0:T(8,128)S(1)} %get-tuple-element.90), channel_id=1, source_target_pairs={{0,4},{4,0},{8,12},{12,8},{16,20},{20,16},{24,28},{28,24},{1,5},{5... | collective-permute-start | bytes 786440 | tf_op jit(solution)/shard_map/ppermute | solution.py:482
  89.6 9.1 %collective-permute-start.14 = (f32[256,256]{1,0:T(8,128)S(1)}, f32[256,256]{1,0:T(8,128)S(1)}, u32[]{:S(2)}, u32[]{:S(2)}) collective-permute-start(f32[256,256]{1,0:T(8,128)S(1)} %get-tuple-element.91), channel_id=1, source_target_pairs={{0,8},{4,12},{8,0},{12,4},{16,24},{20,28},{24,16},{28,20},{1,9},{5... | collective-permute-start | bytes 786440 | tf_op jit(solution)/shard_map/ppermute | solution.py:482
  91.3 13.6 %collective-permute-start.15 = (f32[256,256]{1,0:T(8,128)S(1)}, f32[256,256]{1,0:T(8,128)S(1)}, u32[]{:S(2)}, u32[]{:S(2)}) collective-permute-start(f32[256,256]{1,0:T(8,128)S(1)} %get-tuple-element.92), channel_id=1, source_target_pairs={{0,12},{4,8},{8,4},{12,0},{16,28},{20,24},{24,20},{28,16},{1,13},{... | collective-permute-start | bytes 786440 | tf_op jit(solution)/shard_map/ppermute | solution.py:482

commit v3 on v2

v3 whole, which is shorter than its diff:
```python
import functools

import jax
import jax.numpy as jnp
from jax import lax
from jax.experimental import pallas as pl
from jax.experimental.pallas import tpu as pltpu
from jax.sharding import PartitionSpec as P

KINDS = 6
MEMBERS = 4
PIECE = 256
F32 = jnp.float32
BF16 = jnp.bfloat16


def parts_of(value):
    high = value.astype(BF16)
    low = (value - high.astype(F32)).astype(BF16)
    return high, low


def stacked_state(value):
    high, low = parts_of(value)
    return jnp.concatenate([high, low, high, low], axis=0)


def stacked_table(value):
    high, low = parts_of(value)
    return jnp.concatenate([high, high, low, low], axis=1)


def kind_masks(kinds_row, rows):
    wide = jnp.broadcast_to(kinds_row, (rows, kinds_row.shape[1]))
    return [wide == t for t in range(1, KINDS)]


def select(products, masks):
    rows = products.shape[0] // KINDS
    chosen = products[:rows]
    for t in range(1, KINDS):
        chosen = jnp.where(masks[t - 1], products[t * rows : (t + 1) * rows], chosen)
    return chosen


def typed(table, state, masks):
    return select(jnp.dot(table, stacked_state(state), preferred_element_type=F32), masks)


def params(flops, moved, vmem):
    return dict(
        compiler_params=pltpu.CompilerParams(vmem_limit_bytes=vmem),
        cost_estimate=pl.CostEstimate(flops=flops, bytes_accessed=moved, transcendentals=0),
    )


def pieces(columns):
    return [slice(at, at + PIECE) for at in range(0, columns, PIECE)]


def span_kernel(
    rhs, lagged, kinds, stream, span, absorb, up, down, inverse,
    g_hbm, meta, sides, edges, up_table, down_table,
    inv_table, g_out, rhs_in, lagged_in, kinds_in, stream_in, span_in, absorb_in, ups, downs, inv, sems, out_sems,
):
    layers, tracers, dofs, columns = g_out.shape
    small = [
        pltpu.make_async_copy(source, target, sems.at[2 * layers + i])
        for i, (source, target) in enumerate(
            (
                (up, ups), (inverse, inv), (down, downs),
                (kinds, kinds_in), (stream, stream_in), (span, span_in), (absorb, absorb_in),
            )
        )
    ]

    def loads(layer):
        return (
            pltpu.make_async_copy(lagged.at[layer], lagged_in.at[layer], sems.at[2 * layer]),
            pltpu.make_async_copy(rhs.at[layer], rhs_in.at[layer], sems.at[2 * layer + 1]),
        )

    def store(layer):
        return pltpu.make_async_copy(g_out.at[layer], g_hbm.at[layer], out_sems.at[layer])

    for copy in small:
        copy.start()
    for layer in range(layers):
        for copy in loads(layer):
            copy.start()
    for copy in small:
        copy.wait()
    dinv = inv[...]
    for t in range(KINDS):
        for source, target in ((ups, up_table), (downs, down_table)):
            folded = jnp.dot(dinv, source[t], preferred_element_type=F32, precision=lax.Precision.HIGHEST)
            target[t * dofs : (t + 1) * dofs, :] = stacked_table(folded)
    inv_table[...] = stacked_table(dinv)
    scales = stream_in[...]
    inv_denoms = 1.0 / (scales + span_in[0] + span_in[1] + absorb_in[...])
    for i, rows in enumerate((scales, inv_denoms, scales * inv_denoms, kinds_in[0].astype(F32))):
        meta[i * layers : (i + 1) * layers, :] = rows
    lane = lax.broadcasted_iota(jnp.int32, (1, 128), 1)
    wide_lane = lax.broadcasted_iota(jnp.int32, (1, columns), 1)
    sides[...] = jnp.zeros(sides.shape, F32)
    edges[...] = jnp.zeros(edges.shape, F32)

    def step(layer, carry):
        row = pl.ds(layer, 1)
        inv_denom = meta[pl.ds(layers + layer, 1), :]
        weight_low = inv_denom * span_in[0, row, :]
        weight_high = inv_denom * span_in[1, row, :]
        kinds_low = kinds_in[1, row, :]
        kinds_high = kinds_in[2, row, :]
        for side, weight, kind, at in (
            (0, weight_low, kinds_low, 0),
            (1, weight_high, kinds_high, columns - 1),
        ):
            here = lane // tracers == 2 * layer + side
            sides[0:1, :] = jnp.where(here, kind[:, at : at + 1].astype(F32), sides[0:1, :])
            sides[1:2, :] = jnp.where(here, weight[:, at : at + 1], sides[1:2, :])
        weight_low = jnp.where(wide_lane == 0, 0.0, weight_low)
        weight_high = jnp.where(wide_lane == columns - 1, 0.0, weight_high)
        kinds_low = pltpu.roll(kinds_low, columns - 1, 1)
        kinds_high = pltpu.roll(kinds_high, 1, 1)
        for copy in loads(layer):
            copy.wait()
        edge_values = edges[...]
        for tracer in range(tracers):
            for side, at in ((0, 0), (1, columns - 1)):
                here = lane == side * 64 + layer * 2 * tracers + tracer
                edge_values = jnp.where(here, lagged_in[layer, tracer, :, at : at + 1], edge_values)
        edges[...] = edge_values
        for tracer in range(tracers):
            lows, highs, solved = [], [], []
            for piece in pieces(columns):
                products = jnp.dot(
                    up_table[...], stacked_state(lagged_in[layer, tracer, :, piece]), preferred_element_type=F32
                )
                lows.append(select(products, kind_masks(kinds_low[:, piece], dofs)))
                highs.append(select(products, kind_masks(kinds_high[:, piece], dofs)))
                solved.append(
                    jnp.dot(
                        inv_table[...], stacked_state(rhs_in[layer, tracer, :, piece]), preferred_element_type=F32
                    )
                )
            low_term = pltpu.roll(jnp.concatenate(lows, axis=1), 1, 1)
            high_term = pltpu.roll(jnp.concatenate(highs, axis=1), columns - 1, 1)
            g_out[layer, tracer] = (
                inv_denom * jnp.concatenate(solved, axis=1) - weight_low * low_term - weight_high * high_term
            )
        store(layer).start()
        return carry

    lax.fori_loop(0, layers, step, 0)
    for layer in range(layers):
        store(layer).wait()


def edge_value(fix, layer, tracer, tracers, side):
    lane = lax.broadcasted_iota(jnp.int32, (1, 128), 1)
    at = (2 * layer + side) * tracers + tracer
    return jnp.where(lane == (127 if side else 0), fix[:, at : at + 1], 0.0)


def with_edges(value, fix, layer, tracer, tracers, piece, columns):
    if piece.start == 0:
        low = value[:, :128] + edge_value(fix, layer, tracer, tracers, 0)
        value = jnp.concatenate([low, value[:, 128:]], axis=1)
    if piece.stop == columns:
        end = value.shape[1] - 128
        high = value[:, end:] + edge_value(fix, layer, tracer, tracers, 1)
        value = jnp.concatenate([value[:, :end], high], axis=1)
    return value


def local_forward_kernel(
    place, pair, cross, g_hbm, meta, sides, table, f_out, m0, m1, m2, m3, g_in, sems
):
    layers, tracers, dofs, columns = g_in.shape
    copies = [pltpu.make_async_copy(g_hbm.at[layer], g_in.at[layer], sems.at[layer]) for layer in range(layers)]
    for copy in copies:
        copy.start()
    odd = place[2] == 1
    from_low = pltpu.roll(jnp.where(odd, pair[...], cross[...]), 64, 1)
    from_high = pltpu.roll(jnp.where(odd, cross[...], pair[...]), tracers, 1)
    lane = lax.broadcasted_iota(jnp.int32, (1, 128), 1)
    halo = jnp.where(lane % (2 * tracers) < tracers, from_low, from_high)
    fix = -(sides[1:2, :] * typed(table[...], halo, kind_masks(sides[0:1, :], dofs)))
    for layer in range(layers):
        copies[layer].wait()
        factor = meta[2 * layers + layer : 2 * layers + layer + 1, :]
        kinds = meta[3 * layers + layer : 3 * layers + layer + 1, :]
        for piece in pieces(columns):
            masks = kind_masks(kinds[:, piece], dofs)
            for tracer in range(tracers):
                value = with_edges(g_in[layer, tracer, :, piece], fix, layer, tracer, tracers, piece, columns)
                if layer > 0:
                    value = value - factor[:, piece] * typed(
                        table[...], f_out[layer - 1, tracer, :, piece], masks
                    )
                f_out[layer, tracer, :, piece] = value
    width = columns // MEMBERS
    top = tracers * dofs
    for k, target in enumerate((m0, m1, m2, m3)):
        own = pl.ds(pl.multiple_of((place[0] ^ k) * width, width), width)
        for tracer in range(tracers):
            target[tracer * dofs : (tracer + 1) * dofs, :] = f_out[layers - 1, tracer, :, own]
        target[top : top + 2 * layers, :] = meta[0 : 2 * layers, own]
        target[top + 2 * layers : top + 3 * layers, :] = meta[3 * layers : 4 * layers, own]
        if target.shape[0] > top + 3 * layers:
            target[top + 3 * layers :, :] = jnp.zeros((target.shape[0] - top - 3 * layers, width), F32)


def local_backward_kernel(place, f_in, meta, table, m0, m1, m2, m3, carried):
    layers, tracers, dofs, columns = f_in.shape
    for layer in reversed(range(layers)):
        scale, inv_denom, kinds = (meta[i * layers + layer : i * layers + layer + 1, :] for i in (0, 1, 3))
        for piece in pieces(columns):
            masks = kind_masks(kinds[:, piece], dofs)
            for tracer in range(tracers):
                solved = f_in[layer, tracer, :, piece]
                if layer < layers - 1:
                    solved = solved - inv_denom[:, piece] * carried[tracer, :, piece]
                carried[tracer, :, piece] = scale[:, piece] * typed(table[...], solved, masks)
    width = columns // MEMBERS
    for k, target in enumerate((m0, m1, m2, m3)):
        own = pl.ds(pl.multiple_of((place[0] ^ k) * width, width), width)
        for tracer in range(tracers):
            target[tracer * dofs : (tracer + 1) * dofs, :] = carried[tracer, :, own]


def chain_rows(block_ref, top, layers, layer):
    def row(which):
        at = top + which * layers + layer
        return block_ref[at : at + 1, :]

    return row(0), row(1), row(2)


def forward_chain(turn, layers, tracers, table, blocks, entering, held):
    rows = entering.shape[1]
    dofs = rows // tracers
    parts = [slice(r * dofs, (r + 1) * dofs) for r in range(tracers)]
    if turn == 0:
        held[0] = jnp.zeros(held.shape[1:], F32)
        entering[1] = blocks[0, 0:rows, :]

    def step(block, carry):
        values = [entering[block, here, :] for here in parts]
        for layer in range(layers):
            scale, inv_denom, kinds = chain_rows(blocks.at[block], rows, layers, layer)
            masks = kind_masks(kinds, dofs)
            factor = -(scale * inv_denom)
            values = [factor * typed(table[...], v, masks) for v in values]
            for value, here in zip(values, parts):
                held[block, layer, here, :] = value
        for value, here in zip(values, parts):
            entering[block + 1, here, :] = value + blocks[block, here, :]
        return carry

    lax.fori_loop(1 if turn == 0 else 0, MEMBERS, step, 0)


def backward_chain(turn, layers, tracers, table, blocks, terms, returning, held):
    rows = returning.shape[1]
    dofs = rows // tracers
    parts = [slice(r * dofs, (r + 1) * dofs) for r in range(tracers)]

    def step(index, carry):
        block = MEMBERS - 1 - index
        values = [returning[block + 1, here, :] for here in parts]
        for layer in reversed(range(layers)):
            scale, inv_denom, kinds = chain_rows(blocks.at[block], rows, layers, layer)
            masks = kind_masks(kinds, dofs)
            values = [
                scale * typed(table[...], held[block, layer, here, :] - inv_denom * value, masks)
                for value, here in zip(values, parts)
            ]
        for value, here in zip(values, parts):
            returning[block, here, :] = value + terms[block, here, :]
        return carry

    lax.fori_loop(0, MEMBERS - 1 if turn == 0 else MEMBERS, step, 0)


def take(place, sources, target):
    for k, source in enumerate(sources):
        target[place[0] ^ k] = source[...]


def give(place, targets, source, first):
    for k, target in enumerate(targets):
        target[...] = source[first + (place[0] ^ k)]


def keep(place, turn, olds, targets):
    if olds:
        @pl.when(place[1] != turn)
        def passed():
            for old, target in zip(olds, targets):
                target[...] = old[...]


def chain_forward_kernel(turn, layers, tracers, place, inflow, table, m0, m1, m2, m3, *rest):
    olds, (states, o0, o1, o2, o3, outflow, blocks, entering) = rest[:-8], rest[-8:]
    outs = (o0, o1, o2, o3)

    @pl.when(place[1] == turn)
    def active():
        take(place, (m0, m1, m2, m3), blocks)
        entering[0] = inflow[...] if turn > 0 else jnp.zeros(inflow.shape, F32)
        forward_chain(turn, layers, tracers, table, blocks, entering, states)
        outflow[...] = entering[MEMBERS]
        give(place, outs, entering, 0)

    keep(place, turn, olds, outs)


def chain_last_kernel(
    turn, layers, tracers, place, inflow, up_table, down_table, m0, m1, m2, m3, e0, e1, e2, e3, *rest
):
    olds, (o0, o1, o2, o3, h0, h1, h2, h3, outflow, blocks, terms, entering, returning, held) = rest[:-14], rest[-14:]
    outs = (o0, o1, o2, o3)

    @pl.when(place[1] == turn)
    def active():
        take(place, (m0, m1, m2, m3), blocks)
        take(place, (e0, e1, e2, e3), terms)
        entering[0] = inflow[...] if turn > 0 else jnp.zeros(inflow.shape, F32)
        forward_chain(turn, layers, tracers, up_table, blocks, entering, held)
        returning[MEMBERS] = jnp.zeros(inflow.shape, F32)
        backward_chain(turn, layers, tracers, down_table, blocks, terms, returning, held)
        outflow[...] = returning[0]
        give(place, outs, entering, 0)
        give(place, (h0, h1, h2, h3), returning, 1)

    keep(place, turn, olds, outs)


def chain_backward_kernel(
    turn, layers, tracers, place, inflow, table, m0, m1, m2, m3, e0, e1, e2, e3, states, *rest
):
    olds, (o0, o1, o2, o3, outflow, blocks, terms, returning) = rest[:-8], rest[-8:]
    outs = (o0, o1, o2, o3)

    @pl.when(place[1] == turn)
    def active():
        take(place, (m0, m1, m2, m3), blocks)
        take(place, (e0, e1, e2, e3), terms)
        returning[MEMBERS] = inflow[...]
        backward_chain(turn, layers, tracers, table, blocks, terms, returning, states)
        outflow[...] = returning[0]
        give(place, outs, returning, 1)

    keep(place, turn, olds, outs)


def take_inflow(place, sources, state):
    tracers, dofs, columns = state.shape
    width = columns // MEMBERS
    for k, source in enumerate(sources):
        own = pl.ds(pl.multiple_of((place[0] ^ k) * width, width), width)
        for tracer in range(tracers):
            state[tracer, :, own] = source[tracer * dofs : (tracer + 1) * dofs, :]


def final_forward_kernel(place, f_in, meta, table, *rest):
    sources, (f_out, state) = rest[:-2], rest[-2:]
    layers, tracers, dofs, columns = f_in.shape
    take_inflow(place, sources, state)
    for layer in range(layers):
        factor, kinds = (meta[i * layers + layer : i * layers + layer + 1, :] for i in (2, 3))
        for piece in pieces(columns):
            masks = kind_masks(kinds[:, piece], dofs)
            for tracer in range(tracers):
                value = -(factor[:, piece] * typed(table[...], state[tracer, :, piece], masks))
                f_out[layer, tracer, :, piece] = f_in[layer, tracer, :, piece] + value
                if layer < layers - 1:
                    state[tracer, :, piece] = value


def final_backward_kernel(place, f_in, meta, table, *rest):
    sources, (out, carried, solved, sems) = rest[:-4], rest[-4:]
    layers, tracers, dofs, columns = f_in.shape
    take_inflow(place, sources, carried)
    copies = []
    for layer in reversed(range(layers)):
        scale, inv_denom, kinds = (meta[i * layers + layer : i * layers + layer + 1, :] for i in (0, 1, 3))
        for tracer in range(tracers):
            solved[layer, tracer] = f_in[layer, tracer] - inv_denom * carried[tracer]
            copies.append(
                pltpu.make_async_copy(
                    solved.at[layer, tracer], out.at[layer, tracer], sems.at[layer * tracers + tracer]
                )
            )
            copies[-1].start()
        if layer > 0:
            for piece in pieces(columns):
                masks = kind_masks(kinds[:, piece], dofs)
                for tracer in range(tracers):
                    carried[tracer, :, piece] = scale[:, piece] * typed(
                        table[...], solved[layer, tracer, :, piece], masks
                    )
    for copy in copies:
        copy.wait()


def per_device(rhs, lagged, kinds, stream, span, absorb, up, down, inverse):
    layers, tracers, dofs, columns = rhs.shape
    rows = tracers * dofs
    width = columns // MEMBERS
    count = lax.axis_size("stream")
    groups = count // MEMBERS
    position = lax.axis_index("stream")
    place = jnp.stack(
        [position % MEMBERS, position // MEMBERS, lax.axis_index("span") % 2]
    ).astype(jnp.int32)
    long_rows = rows + -(-3 * layers // 8) * 8
    vmem, anywhere, smem = (pl.BlockSpec(memory_space=s) for s in (pltpu.VMEM, pl.ANY, pltpu.SMEM))
    full = functools.partial(jax.ShapeDtypeStruct, dtype=F32)
    field = 4 * rhs.size
    product = 2 * KINDS * dofs * 4 * dofs * tracers * columns
    some = 12 << 20
    table_shape = (KINDS * dofs, 4 * dofs)
    fix = full((dofs, 128))

    def exchanged(messages):
        return [messages[0]] + [
            lax.ppermute(messages[k], "stream", [(i, i ^ k) for i in range(count)])
            for k in range(1, MEMBERS)
        ]

    def between(values, step):
        pairs = [(step * MEMBERS + i, (step + 1) * MEMBERS + i) for i in range(MEMBERS)]
        return lax.ppermute(values, "stream", pairs + [(b, a) for a, b in pairs])

    column_state = pltpu.VMEM((tracers, dofs, columns), F32)
    message = full((rows, width))
    long_message = full((long_rows, width))
    table = jax.ShapeDtypeStruct(table_shape, BF16)
    inputs = (rhs, lagged, kinds, stream, span, absorb, up, down, inverse)

    g, meta, sides, edges, up_table, down_table = pl.pallas_call(
        span_kernel,
        out_shape=(
            pltpu.HBM(rhs.shape, F32), full((4 * layers, columns)), full((8, 128)), fix, table, table,
        ),
        in_specs=[anywhere] * len(inputs),
        out_specs=(anywhere,) + (vmem,) * 5,
        scratch_shapes=[pltpu.VMEM((dofs, 4 * dofs), BF16), pltpu.VMEM(rhs.shape, F32)]
        + [pltpu.VMEM(value.shape, value.dtype) for value in inputs]
        + [pltpu.SemaphoreType.DMA((2 * layers + 7,)), pltpu.SemaphoreType.DMA((layers,))],
        name="span_terms",
        **params(2 * layers * product, 3 * field, some + 4 * field),
    )(*(pltpu.with_memory_space_constraint(value, pltpu.HBM) for value in inputs))

    across = lax.axis_size("span")
    crossing = [(i, i + 1) for i in range(1, across - 1, 2)]
    pair = lax.ppermute(edges, "span", [(i, i ^ 1) for i in range(across)])
    cross = lax.ppermute(edges, "span", crossing + [(b, a) for a, b in crossing])

    f_zero, *out_b = pl.pallas_call(
        local_forward_kernel,
        out_shape=(full(rhs.shape),) + (long_message,) * MEMBERS,
        in_specs=[smem, vmem, vmem, anywhere] + [vmem] * 3,
        out_specs=(vmem,) * (1 + MEMBERS),
        scratch_shapes=[pltpu.VMEM(rhs.shape, F32), pltpu.SemaphoreType.DMA((layers,))],
        name="local_forward",
        **params(layers * product, field, some + 2 * field),
    )(place, pair, cross, pltpu.with_memory_space_constraint(g, pltpu.HBM), meta, sides, up_table)
    in_b = exchanged(out_b)

    out_e = pl.pallas_call(
        local_backward_kernel,
        out_shape=(message,) * MEMBERS,
        in_specs=[smem] + [vmem] * 3,
        out_specs=(vmem,) * MEMBERS,
        scratch_shapes=[column_state],
        name="local_backward",
        **params(layers * product, field, some + field),
    )(place, f_zero, meta, down_table)
    in_e = exchanged(out_e)
    in_b, _ = lax.optimization_barrier((in_b, out_e))

    blocks = pltpu.VMEM((MEMBERS, long_rows, width), F32)
    inner = pltpu.VMEM((MEMBERS + 1, rows, width), F32)
    held = (MEMBERS, layers, rows, width)
    inflow = jnp.zeros((rows, width), F32)
    states, out_f = [], []
    for turn in range(groups - 1):
        state, *out_f, outflow = pl.pallas_call(
            functools.partial(chain_forward_kernel, turn, layers, tracers),
            out_shape=(full(held),) + (message,) * (MEMBERS + 1),
            in_specs=[smem] + [vmem] * (2 + MEMBERS + len(out_f)),
            out_specs=(vmem,) * (MEMBERS + 2),
            scratch_shapes=[blocks, inner],
            name=f"chain_forward_{turn}",
            **params(layers * product, 2 * field, some + field),
        )(place, inflow, up_table, *in_b, *out_f)
        states.append(state)
        inflow = between(outflow, turn)

    *out_f, h0, h1, h2, h3, outflow = pl.pallas_call(
        functools.partial(chain_last_kernel, groups - 1, layers, tracers),
        out_shape=(message,) * (2 * MEMBERS + 1),
        in_specs=[smem] + [vmem] * (3 + 2 * MEMBERS + len(out_f)),
        out_specs=(vmem,) * (2 * MEMBERS + 1),
        scratch_shapes=[blocks, inner, inner, inner, pltpu.VMEM(held, F32)],
        name="chain_last",
        **params(2 * layers * product, 2 * field, some + 2 * field),
    )(place, inflow, up_table, down_table, *in_b, *in_e, *out_f)
    in_f = exchanged(out_f)
    out_h = [h0, h1, h2, h3]

    for turn in reversed(range(groups - 1)):
        inflow = between(outflow, turn)
        *out_h, outflow = pl.pallas_call(
            functools.partial(chain_backward_kernel, turn, layers, tracers),
            out_shape=(message,) * (MEMBERS + 1),
            in_specs=[smem] + [vmem] * (3 + 3 * MEMBERS),
            out_specs=(vmem,) * (MEMBERS + 1),
            scratch_shapes=[blocks, inner, inner],
            name=f"chain_backward_{turn}",
            **params(layers * product, 2 * field, some + field),
        )(place, inflow, down_table, *in_b, *in_e, states[turn], *out_h)
    in_h = exchanged(out_h)

    f_part = pl.pallas_call(
        final_forward_kernel,
        out_shape=full(rhs.shape),
        in_specs=[smem] + [vmem] * (3 + len(in_f)),
        out_specs=vmem,
        scratch_shapes=[column_state],
        name="final_forward",
        **params(layers * product, 2 * field, some + 2 * field),
    )(place, f_zero, meta, up_table, *in_f)
    return pl.pallas_call(
        final_backward_kernel,
        out_shape=full(rhs.shape),
        in_specs=[smem] + [vmem] * (3 + len(in_h)),
        out_specs=anywhere,
        scratch_shapes=[
            column_state,
            pltpu.VMEM(rhs.shape, F32),
            pltpu.SemaphoreType.DMA((layers * tracers,)),
        ],
        name="final_backward",
        **params(layers * product, 2 * field, some + 2 * field),
    )(place, f_part, meta, down_table, *in_h)


def solution(mesh):
    return jax.shard_map(
        per_device,
        mesh=mesh,
        in_specs=(
            P("stream", None, None, "span"),
            P("stream", None, None, "span"),
            P(None, "stream", "span"),
            P("stream", "span"),
            P(None, "stream", "span"),
            P("stream", "span"),
            P(),
            P(),
            P(),
        ),
        out_specs=P("stream", None, None, "span"),
        check_vma=False,
    )
```

time: 110 us -> 98.7 us (0.90)
  local copies, waits for them, and re-layouts: 8.48 us -> 0.02 us
  waiting for transfers between devices: 32.7 us -> 30.3 us
  starting transfers between devices: 28.4 us -> 29.5 us
    unnamed x20 -> x0, local copies, waits for them, and re-layouts: 8.46 us -> none
    ppermute x12, waiting for transfers between devices: 22.3 us -> 19.8 us  [exchanged(): lax.ppermute(messages[k], 'stream', [(i, i ^ k) for i in range(count)])]
    pallas_call x4 -> x2, Pallas kernels: 16.4 us -> 15.2 us  [the longest x1 10 us: per_device(): pl.pallas_call(span_kernel, out_shape=(pltpu.HBM(rhs.shape, F32), full((4...]
  transfers between devices with their start and end apart: 16 -> 16, of which waited for: 8 -> 9; matrix products, arithmetic and copies ran while one was open for 0% -> 0% of each run, Pallas kernels for 29% -> 18%
where the time goes in v3:
time: 98.7 us; the launch traced here: 98.6 us
  Pallas kernels  38.4 us (39%)
  waiting for transfers between devices  30.3 us (31%)
  starting transfers between devices  29.5 us (30%)
    ppermute x12, waiting for transfers between devices, exchanged(): lax.ppermute(messages[k], 'stream', [(i, i ^ k) for i in range(count)])  19.8 us
    ppermute x12, starting transfers between devices, exchanged(): lax.ppermute(messages[k], 'stream', [(i, i ^ k) for i in range(count)])  15 us
    ppermute x2, starting transfers between devices, between(): return lax.ppermute(values, 'stream', pairs + [(b, a) for a, b in pairs])  13.3 us
    ppermute x2, waiting for transfers between devices, between(): return lax.ppermute(values, 'stream', pairs + [(b, a) for a, b in pairs])  10.4 us
    pallas_call x1, Pallas kernels, per_device(): pl.pallas_call(span_kernel, out_shape=(pltpu.HBM(rhs.shape, F32), full((4...  10 us
    pallas_call x1, Pallas kernels, per_device(): pl.pallas_call(local_forward_kernel, out_shape=(full(rhs.shape),) + (long...  5.21 us
    pallas_call x1, Pallas kernels, per_device(): pl.pallas_call(functools.partial(chain_backward_kernel, turn, layers, tra...  5.09 us
    pallas_call x1, Pallas kernels, per_device(): pl.pallas_call(final_backward_kernel, out_shape=full(rhs.shape), in_specs...  4.6 us
  transfers between devices with their start and end apart: 16, of which 9 were waited for; matrix products, arithmetic and copies ran while one was open for 0% of the time, Pallas kernels for 18%

profile of v3, /device:TPU:0, one launch (start us, length us, event | category | flops | bytes accessed | tf_op | source)
XLA Modules:
  0.0 98.6 jit_solution(18034904465911460161)
XLA Ops:
  0.0 10.0 %span_terms.1 = (f32[4,4,64,1024]{3,2,1,0:T(8,128)}, f32[16,1024]{1,0:T(8,128)S(1)}, f32[8,128]{1,0:T(8,128)S(1)}, f32[64,128]{1,0:T(8,128)S(1)}, bf16[384,256]{...) custom-call(f32[4,4,64,1024]{3,2,1,0:T(8,128)} %rhs.1, f32[4,4,64,1024]{3,2,1,0:T(8,128)} %lagged.1, s32[3,4,1024]{2,1,0:T(4,128)} %kinds.1, ...), custom_call_target="tpu_custom_call" | custom-call | flops 6442450944 | bytes 12582912 | tf_op jit(solution)/shard_map/span_terms/pallas_call | solution.py:444
  10.0 0.5 collective-permute-start
  10.5 0.7 collective-permute-start.1
  11.2 0.1 pad_add_fusion.place
  11.3 0.1 collective-permute-done.pair
  11.4 0.0 collective-permute-done.1.cross
  11.4 5.2 %local_forward.1 = (f32[4,4,64,1024]{3,2,1,0:T(8,128)S(1)}, f32[272,256]{1,0:T(8,128)S(1)}, f32[272,256]{1,0:T(8,128)S(1)}, f32[272,256]{1,0:T(8,128)S(1)}, f32[272,256]{1,0:T(8,128)S(1)}) custom-call(s32[3]{0:T(128)S(1)} %pad_add_fusion.place, f32[64,128]{1,0:T(8,128)S(1)} %collective-permute-done.pair, f32[64,128]{1,0:T(8,128)S(1)} %collective-permute-done.1.cross, ...), custom_call_target="tpu_custom_call" | custom-call | flops 3221225472 | bytes 4194304 | tf_op jit(solution)/shard_map/local_forward/pallas_call | solution.py:463
  16.6 2.9 %collective-permute-start.2 = (f32[272,256]{1,0:T(8,128)S(1)}, f32[272,256]{1,0:T(8,128)S(1)}, u32[]{:S(2)}, u32[]{:S(2)}) collective-permute-start(f32[272,256]{1,0:T(8,128)S(1)} %get-tuple-element.50), channel_id=1, source_target_pairs={{0,4},{4,0},{8,12},{12,8},{16,20},{20,16},{24,28},{28,24},{1,5},{5... | collective-permute-start | bytes 835592 | tf_op jit(solution)/shard_map/ppermute | solution.py:430
  19.5 1.6 %collective-permute-start.3 = (f32[272,256]{1,0:T(8,128)S(1)}, f32[272,256]{1,0:T(8,128)S(1)}, u32[]{:S(2)}, u32[]{:S(2)}) collective-permute-start(f32[272,256]{1,0:T(8,128)S(1)} %get-tuple-element.51), channel_id=1, source_target_pairs={{0,8},{4,12},{8,0},{12,4},{16,24},{20,28},{24,16},{28,20},{1,9},{5... | collective-permute-start | bytes 835592 | tf_op jit(solution)/shard_map/ppermute | solution.py:430
  21.1 4.1 %local_backward.1 = (f32[256,256]{1,0:T(8,128)S(1)}, f32[256,256]{1,0:T(8,128)S(1)}, f32[256,256]{1,0:T(8,128)S(1)}, f32[256,256]{1,0:T(8,128)S(1)}) custom-call(s32[3]{0:T(128)S(1)} %pad_add_fusion.place, f32[4,4,64,1024]{3,2,1,0:T(8,128)S(1)} %get-tuple-element.48.f_in, f32[16,1024]{1,0:T(8,128)S(1)} %get-tuple-element.45.meta, ...), custom_call_target="tpu_custom_call" | custom-call | flops 3221225472 | bytes 4194304 | tf_op jit(solution)/shard_map/local_backward/pallas_call | solution.py:474
  25.2 2.0 %collective-permute-start.6 = (f32[256,256]{1,0:T(8,128)S(1)}, f32[256,256]{1,0:T(8,128)S(1)}, u32[]{:S(2)}, u32[]{:S(2)}) collective-permute-start(f32[256,256]{1,0:T(8,128)S(1)} %get-tuple-element.55), channel_id=1, source_target_pairs={{0,4},{4,0},{8,12},{12,8},{16,20},{20,16},{24,28},{28,24},{1,5},{5... | collective-permute-start | bytes 786440 | tf_op jit(solution)/shard_map/ppermute | solution.py:430
  27.2 1.6 %collective-permute-start.7 = (f32[256,256]{1,0:T(8,128)S(1)}, f32[256,256]{1,0:T(8,128)S(1)}, u32[]{:S(2)}, u32[]{:S(2)}) collective-permute-start(f32[256,256]{1,0:T(8,128)S(1)} %get-tuple-element.56), channel_id=1, source_target_pairs={{0,8},{4,12},{8,0},{12,4},{16,24},{20,28},{24,16},{28,20},{1,9},{5... | collective-permute-start | bytes 786440 | tf_op jit(solution)/shard_map/ppermute | solution.py:430
  28.8 2.1 %collective-permute-done.4.m3 = f32[272,256]{1,0:T(8,128)S(1)} collective-permute-done((f32[272,256]{1,0:T(8,128)S(1)}, f32[272,256]{1,0:T(8,128)S(1)}, u32[]{:S(2)}, u32[]{:S(2)}) %collective-permute-start.4) | collective-permute-done | bytes 278560 | tf_op jit(solution)/shard_map/ppermute | solution.py:430
  31.0 4.4 %chain_forward_0.1 = (f32[4,4,256,256]{3,2,1,0:T(8,128)S(1)}, f32[256,256]{1,0:T(8,128)S(1)}, f32[256,256]{1,0:T(8,128)S(1)}, f32[256,256]{1,0:T(8,128)S(1)}, f3...) custom-call(s32[3]{0:T(128)S(1)} %pad_add_fusion.place, f32[256,256]{1,0:T(8,128)S(1)} %broadcast_in_dim.3.inflow, ...), custom_call_target="tpu_custom_call" | custom-call | flops 3221225472 | bytes 8388608 | tf_op jit(solution)/shard_map/chain_forward_0/pallas_call | solution.py:492
  35.4 0.1 collective-permute-start.5
  35.4 4.8 %collective-permute-done.6.e1 = f32[256,256]{1,0:T(8,128)S(1)} collective-permute-done((f32[256,256]{1,0:T(8,128)S(1)}, f32[256,256]{1,0:T(8,128)S(1)}, u32[]{:S(2)}, u32[]{:S(2)}) %collective-permute-start.6) | collective-permute-done | bytes 262176 | tf_op jit(solution)/shard_map/ppermute | solution.py:430
  40.3 4.8 %collective-permute-done.8.e3 = f32[256,256]{1,0:T(8,128)S(1)} collective-permute-done((f32[256,256]{1,0:T(8,128)S(1)}, f32[256,256]{1,0:T(8,128)S(1)}, u32[]{:S(2)}, u32[]{:S(2)}) %collective-permute-start.8) | collective-permute-done | bytes 262176 | tf_op jit(solution)/shard_map/ppermute | solution.py:430
  45.0 2.7 %collective-permute-done.5.inflow = f32[256,256]{1,0:T(8,128)S(1)} collective-permute-done((f32[256,256]{1,0:T(8,128)S(1)}, f32[256,256]{1,0:T(8,128)S(1)}, u32[]{:S(2)}, u32[]{:S(2)}) %collective-permute-start.5) | collective-permute-done | bytes 262176 | tf_op jit(solution)/shard_map/ppermute | solution.py:436
  47.7 0.8 chain_last.1
  48.5 13.2 %collective-permute-start.12 = (f32[256,256]{1,0:T(8,128)S(1)}, f32[256,256]{1,0:T(8,128)S(1)}, u32[]{:S(2)}, u32[]{:S(2)}) collective-permute-start(f32[256,256]{1,0:T(8,128)S(1)} %get-tuple-element.71), channel_id=1, source_target_pairs={{0,16},{4,20},{8,24},{12,28},{16,0},{20,4},{24,8},{28,12},{1,17},{... | collective-permute-start | bytes 786440 | tf_op jit(solution)/shard_map/ppermute | solution.py:436
  61.7 2.0 %collective-permute-start.11 = (f32[256,256]{1,0:T(8,128)S(1)}, f32[256,256]{1,0:T(8,128)S(1)}, u32[]{:S(2)}, u32[]{:S(2)}) collective-permute-start(f32[256,256]{1,0:T(8,128)S(1)} %get-tuple-element.70), channel_id=1, source_target_pairs={{0,12},{4,8},{8,4},{12,0},{16,28},{20,24},{24,20},{28,16},{1,13},{... | collective-permute-start | bytes 786440 | tf_op jit(solution)/shard_map/ppermute | solution.py:430
  63.7 1.5 %collective-permute-start.9 = (f32[256,256]{1,0:T(8,128)S(1)}, f32[256,256]{1,0:T(8,128)S(1)}, u32[]{:S(2)}, u32[]{:S(2)}) collective-permute-start(f32[256,256]{1,0:T(8,128)S(1)} %get-tuple-element.68), channel_id=1, source_target_pairs={{0,4},{4,0},{8,12},{12,8},{16,20},{20,16},{24,28},{28,24},{1,5},{5... | collective-permute-start | bytes 786440 | tf_op jit(solution)/shard_map/ppermute | solution.py:430
  65.2 7.7 %collective-permute-done.12.inflow = f32[256,256]{1,0:T(8,128)S(1)} collective-permute-done((f32[256,256]{1,0:T(8,128)S(1)}, f32[256,256]{1,0:T(8,128)S(1)}, u32[]{:S(2)}, u32[]{:S(2)}) %collective-permute-start.12) | collective-permute-done | bytes 262176 | tf_op jit(solution)/shard_map/ppermute | solution.py:436
  72.9 5.1 %chain_backward_0.1 = (f32[256,256]{1,0:T(8,128)S(1)}, f32[256,256]{1,0:T(8,128)S(1)}, f32[256,256]{1,0:T(8,128)S(1)}, f32[256,256]{1,0:T(8,128)S(1)}, f32[256,256]{1,0:T(8,128)}) custom-call(s32[3]{0:T(128)S(1)} %pad_add_fusion.place, f32[256,256]{1,0:T(8,128)S(1)} %collective-permute-done.12.inflow, ...), custom_call_target="tpu_custom_call" | custom-call | flops 3221225472 | bytes 8388608 | tf_op jit(solution)/shard_map/chain_backward_0/pallas_call | solution.py:518
  78.0 1.1 %collective-permute-start.13 = (f32[256,256]{1,0:T(8,128)S(1)}, f32[256,256]{1,0:T(8,128)S(1)}, u32[]{:S(2)}, u32[]{:S(2)}) collective-permute-start(f32[256,256]{1,0:T(8,128)S(1)} %get-tuple-element.78), channel_id=1, source_target_pairs={{0,4},{4,0},{8,12},{12,8},{16,20},{20,16},{24,28},{28,24},{1,5},{5... | collective-permute-start | bytes 786440 | tf_op jit(solution)/shard_map/ppermute | solution.py:430
  79.1 1.9 %collective-permute-start.14 = (f32[256,256]{1,0:T(8,128)S(1)}, f32[256,256]{1,0:T(8,128)S(1)}, u32[]{:S(2)}, u32[]{:S(2)}) collective-permute-start(f32[256,256]{1,0:T(8,128)S(1)} %get-tuple-element.79), channel_id=1, source_target_pairs={{0,8},{4,12},{8,0},{12,4},{16,24},{20,28},{24,16},{28,20},{1,9},{5... | collective-permute-start | bytes 786440 | tf_op jit(solution)/shard_map/ppermute | solution.py:430
  80.9 0.6 collective-permute-start.15
  81.5 4.2 %final_forward.1.f_in = f32[4,4,64,1024]{3,2,1,0:T(8,128)S(1)} custom-call(s32[3]{0:T(128)S(1)} %pad_add_fusion.place, f32[4,4,64,1024]{3,2,1,0:T(8,128)S(1)} %get-tuple-element.48.f_in, f32[16,1024]{1,0:T(8,128)S(1)} %get-tuple-element.45.meta, bf16[384,256]{1,0:T(8,128)(2,1)S(1)} %get-tuple-element.47.table.up_table, ...), custom_call_target="tpu_custom_call" | custom-call | flops 3221225472 | bytes 8388608 | tf_op jit(solution)/shard_map/final_forward/pallas_call | solution.py:529
  85.7 1.3 %collective-permute-done.13.rest_1_ = f32[256,256]{1,0:T(8,128)S(1)} collective-permute-done((f32[256,256]{1,0:T(8,128)S(1)}, f32[256,256]{1,0:T(8,128)S(1)}, u32[]{:S(2)}, u32[]{:S(2)}) %collective-permute-start.13) | collective-permute-done | bytes 262176 | tf_op jit(solution)/shard_map/ppermute | solution.py:430
  87.0 1.1 %collective-permute-done.14.rest_2_ = f32[256,256]{1,0:T(8,128)S(1)} collective-permute-done((f32[256,256]{1,0:T(8,128)S(1)}, f32[256,256]{1,0:T(8,128)S(1)}, u32[]{:S(2)}, u32[]{:S(2)}) %collective-permute-start.14) | collective-permute-done | bytes 262176 | tf_op jit(solution)/shard_map/ppermute | solution.py:430
  88.1 5.7 %collective-permute-done.15.rest_3_ = f32[256,256]{1,0:T(8,128)S(1)} collective-permute-done((f32[256,256]{1,0:T(8,128)S(1)}, f32[256,256]{1,0:T(8,128)S(1)}, u32[]{:S(2)}, u32[]{:S(2)}) %collective-permute-start.15) | collective-permute-done | bytes 262176 | tf_op jit(solution)/shard_map/ppermute | solution.py:430
  93.8 4.6 %final_backward.1 = f32[4,4,64,1024]{3,2,1,0:T(8,128)} custom-call(s32[3]{0:T(128)S(1)} %pad_add_fusion.place, f32[4,4,64,1024]{3,2,1,0:T(8,128)S(1)} %final_forward.1.f_in, f32[16,1024]{1,0:T(8,128)S(1)} %get-tuple-element.45.meta, bf16[384,256]{1,0:T(8,128)(2,1)S(1)} %get-tuple-element.53.table.down_table, f32[256,256]{1,0:T(8,128)S(1)} %get-tuple-element.77.rest_0_, ...), custom_call_target="tpu_custom_call" | custom-call | flops 3221225472 | bytes 8388608 | tf_op jit(solution)/shard_map/final_backward/pallas_call | solution.py:538
  (10 shorter events, 0.0 us)
Async XLA Ops:
  10.0 1.4 %collective-permute-start = (f32[64,128]{1,0:T(8,128)S(1)}, f32[64,128]{1,0:T(8,128)S(1)}, u32[]{:S(2)}, u32[]{:S(2)}) collective-permute-start(f32[64,128]{1,0:T(8,128)S(1)} %get-tuple-element.43), channel_id=1, source_target_pairs={{0,1},{1,0},{2,3},{3,2},{4,5},{5,4},{6,7},{7,6},{8,9},{9,8},{10,11... | collective-permute-start | bytes 98312 | tf_op jit(solution)/shard_map/ppermute | solution.py:460
  10.5 0.9 collective-permute-start.1
  16.6 12.2 %collective-permute-start.2 = (f32[272,256]{1,0:T(8,128)S(1)}, f32[272,256]{1,0:T(8,128)S(1)}, u32[]{:S(2)}, u32[]{:S(2)}) collective-permute-start(f32[272,256]{1,0:T(8,128)S(1)} %get-tuple-element.50), channel_id=1, source_target_pairs={{0,4},{4,0},{8,12},{12,8},{16,20},{20,16},{24,28},{28,24},{1,5},{5... | collective-permute-start | bytes 835592 | tf_op jit(solution)/shard_map/ppermute | solution.py:430
  19.5 9.3 %collective-permute-start.3 = (f32[272,256]{1,0:T(8,128)S(1)}, f32[272,256]{1,0:T(8,128)S(1)}, u32[]{:S(2)}, u32[]{:S(2)}) collective-permute-start(f32[272,256]{1,0:T(8,128)S(1)} %get-tuple-element.51), channel_id=1, source_target_pairs={{0,8},{4,12},{8,0},{12,4},{16,24},{20,28},{24,16},{28,20},{1,9},{5... | collective-permute-start | bytes 835592 | tf_op jit(solution)/shard_map/ppermute | solution.py:430
  21.1 9.8 %collective-permute-start.4 = (f32[272,256]{1,0:T(8,128)S(1)}, f32[272,256]{1,0:T(8,128)S(1)}, u32[]{:S(2)}, u32[]{:S(2)}) collective-permute-start(f32[272,256]{1,0:T(8,128)S(1)} %get-tuple-element.52), channel_id=1, source_target_pairs={{0,12},{4,8},{8,4},{12,0},{16,28},{20,24},{24,20},{28,16},{1,13},{... | collective-permute-start | bytes 835592 | tf_op jit(solution)/shard_map/ppermute | solution.py:430
  25.2 15.0 %collective-permute-start.6 = (f32[256,256]{1,0:T(8,128)S(1)}, f32[256,256]{1,0:T(8,128)S(1)}, u32[]{:S(2)}, u32[]{:S(2)}) collective-permute-start(f32[256,256]{1,0:T(8,128)S(1)} %get-tuple-element.55), channel_id=1, source_target_pairs={{0,4},{4,0},{8,12},{12,8},{16,20},{20,16},{24,28},{28,24},{1,5},{5... | collective-permute-start | bytes 786440 | tf_op jit(solution)/shard_map/ppermute | solution.py:430
  27.2 13.1 %collective-permute-start.7 = (f32[256,256]{1,0:T(8,128)S(1)}, f32[256,256]{1,0:T(8,128)S(1)}, u32[]{:S(2)}, u32[]{:S(2)}) collective-permute-start(f32[256,256]{1,0:T(8,128)S(1)} %get-tuple-element.56), channel_id=1, source_target_pairs={{0,8},{4,12},{8,0},{12,4},{16,24},{20,28},{24,16},{28,20},{1,9},{5... | collective-permute-start | bytes 786440 | tf_op jit(solution)/shard_map/ppermute | solution.py:430
  28.8 16.2 %collective-permute-start.8 = (f32[256,256]{1,0:T(8,128)S(1)}, f32[256,256]{1,0:T(8,128)S(1)}, u32[]{:S(2)}, u32[]{:S(2)}) collective-permute-start(f32[256,256]{1,0:T(8,128)S(1)} %get-tuple-element.57), channel_id=1, source_target_pairs={{0,12},{4,8},{8,4},{12,0},{16,28},{20,24},{24,20},{28,16},{1,13},{... | collective-permute-start | bytes 786440 | tf_op jit(solution)/shard_map/ppermute | solution.py:430
  35.4 12.3 %collective-permute-start.5 = (f32[256,256]{1,0:T(8,128)S(1)}, f32[256,256]{1,0:T(8,128)S(1)}, u32[]{:S(2)}, u32[]{:S(2)}) collective-permute-start(f32[256,256]{1,0:T(8,128)S(1)} %get-tuple-element.62), channel_id=1, source_target_pairs={{0,16},{4,20},{8,24},{12,28},{16,0},{20,4},{24,8},{28,12},{1,17},{... | collective-permute-start | bytes 786440 | tf_op jit(solution)/shard_map/ppermute | solution.py:436
  48.5 24.4 %collective-permute-start.12 = (f32[256,256]{1,0:T(8,128)S(1)}, f32[256,256]{1,0:T(8,128)S(1)}, u32[]{:S(2)}, u32[]{:S(2)}) collective-permute-start(f32[256,256]{1,0:T(8,128)S(1)} %get-tuple-element.71), channel_id=1, source_target_pairs={{0,16},{4,20},{8,24},{12,28},{16,0},{20,4},{24,8},{28,12},{1,17},{... | collective-permute-start | bytes 786440 | tf_op jit(solution)/shard_map/ppermute | solution.py:436
  61.7 19.2 %collective-permute-start.10 = (f32[256,256]{1,0:T(8,128)S(1)}, f32[256,256]{1,0:T(8,128)S(1)}, u32[]{:S(2)}, u32[]{:S(2)}) collective-permute-start(f32[256,256]{1,0:T(8,128)S(1)} %get-tuple-element.69), channel_id=1, source_target_pairs={{0,8},{4,12},{8,0},{12,4},{16,24},{20,28},{24,16},{28,20},{1,9},{5... | collective-permute-start | bytes 786440 | tf_op jit(solution)/shard_map/ppermute | solution.py:430
  61.7 19.8 %collective-permute-start.11 = (f32[256,256]{1,0:T(8,128)S(1)}, f32[256,256]{1,0:T(8,128)S(1)}, u32[]{:S(2)}, u32[]{:S(2)}) collective-permute-start(f32[256,256]{1,0:T(8,128)S(1)} %get-tuple-element.70), channel_id=1, source_target_pairs={{0,12},{4,8},{8,4},{12,0},{16,28},{20,24},{24,20},{28,16},{1,13},{... | collective-permute-start | bytes 786440 | tf_op jit(solution)/shard_map/ppermute | solution.py:430
  63.7 17.8 %collective-permute-start.9 = (f32[256,256]{1,0:T(8,128)S(1)}, f32[256,256]{1,0:T(8,128)S(1)}, u32[]{:S(2)}, u32[]{:S(2)}) collective-permute-start(f32[256,256]{1,0:T(8,128)S(1)} %get-tuple-element.68), channel_id=1, source_target_pairs={{0,4},{4,0},{8,12},{12,8},{16,20},{20,16},{24,28},{28,24},{1,5},{5... | collective-permute-start | bytes 786440 | tf_op jit(solution)/shard_map/ppermute | solution.py:430
  78.0 9.0 %collective-permute-start.13 = (f32[256,256]{1,0:T(8,128)S(1)}, f32[256,256]{1,0:T(8,128)S(1)}, u32[]{:S(2)}, u32[]{:S(2)}) collective-permute-start(f32[256,256]{1,0:T(8,128)S(1)} %get-tuple-element.78), channel_id=1, source_target_pairs={{0,4},{4,0},{8,12},{12,8},{16,20},{20,16},{24,28},{28,24},{1,5},{5... | collective-permute-start | bytes 786440 | tf_op jit(solution)/shard_map/ppermute | solution.py:430
  79.1 9.1 %collective-permute-start.14 = (f32[256,256]{1,0:T(8,128)S(1)}, f32[256,256]{1,0:T(8,128)S(1)}, u32[]{:S(2)}, u32[]{:S(2)}) collective-permute-start(f32[256,256]{1,0:T(8,128)S(1)} %get-tuple-element.79), channel_id=1, source_target_pairs={{0,8},{4,12},{8,0},{12,4},{16,24},{20,28},{24,16},{28,20},{1,9},{5... | collective-permute-start | bytes 786440 | tf_op jit(solution)/shard_map/ppermute | solution.py:430
  80.9 12.9 %collective-permute-start.15 = (f32[256,256]{1,0:T(8,128)S(1)}, f32[256,256]{1,0:T(8,128)S(1)}, u32[]{:S(2)}, u32[]{:S(2)}) collective-permute-start(f32[256,256]{1,0:T(8,128)S(1)} %get-tuple-element.80), channel_id=1, source_target_pairs={{0,12},{4,8},{8,4},{12,0},{16,28},{20,24},{24,20},{28,16},{1,13},{... | collective-permute-start | bytes 786440 | tf_op jit(solution)/shard_map/ppermute | solution.py:430

commit v4 on v3

--- a/solution.py
+++ b/solution.py
@@ -58,17 +58,25 @@
     return [slice(at, at + PIECE) for at in range(0, columns, PIECE)]
 
 
+def fold_table(inverse, source, target):
+    dofs = inverse.shape[0]
+    dinv = inverse[...]
+    for t in range(KINDS):
+        folded = jnp.dot(dinv, source[t], preferred_element_type=F32, precision=lax.Precision.HIGHEST)
+        target[t * dofs : (t + 1) * dofs, :] = stacked_table(folded)
+
+
 def span_kernel(
-    rhs, lagged, kinds, stream, span, absorb, up, down, inverse,
-    g_hbm, meta, sides, edges, up_table, down_table,
-    inv_table, g_out, rhs_in, lagged_in, kinds_in, stream_in, span_in, absorb_in, ups, downs, inv, sems, out_sems,
+    place, rhs, lagged, kinds, stream, span, absorb, up, inverse,
+    g_out, meta, sides, edges, up_table,
+    inv_table, rhs_in, lagged_in, kinds_in, stream_in, span_in, absorb_in, ups, inv, sems,
 ):
     layers, tracers, dofs, columns = g_out.shape
     small = [
         pltpu.make_async_copy(source, target, sems.at[2 * layers + i])
         for i, (source, target) in enumerate(
             (
-                (up, ups), (inverse, inv), (down, downs),
+                (up, ups), (inverse, inv),
                 (kinds, kinds_in), (stream, stream_in), (span, span_in), (absorb, absorb_in),
             )
         )
@@ -79,9 +87,6 @@
             pltpu.make_async_copy(lagged.at[layer], lagged_in.at[layer], sems.at[2 * layer]),
             pltpu.make_async_copy(rhs.at[layer], rhs_in.at[layer], sems.at[2 * layer + 1]),
         )
-
-    def store(layer):
-        return pltpu.make_async_copy(g_out.at[layer], g_hbm.at[layer], out_sems.at[layer])
 
     for copy in small:
         copy.start()
@@ -90,12 +95,8 @@
             copy.start()
     for copy in small:
         copy.wait()
-    dinv = inv[...]
-    for t in range(KINDS):
-        for source, target in ((ups, up_table), (downs, down_table)):
-            folded = jnp.dot(dinv, source[t], preferred_element_type=F32, precision=lax.Precision.HIGHEST)
-            target[t * dofs : (t + 1) * dofs, :] = stacked_table(folded)
-    inv_table[...] = stacked_table(dinv)
+    fold_table(inv, ups, up_table)
+    inv_table[...] = stacked_table(inv[...])
     scales = stream_in[...]
     inv_denoms = 1.0 / (scales + span_in[0] + span_in[1] + absorb_in[...])
     for i, rows in enumerate((scales, inv_denoms, scales * inv_denoms, kinds_in[0].astype(F32))):
@@ -105,9 +106,9 @@
     sides[...] = jnp.zeros(sides.shape, F32)
     edges[...] = jnp.zeros(edges.shape, F32)
 
-    def step(layer, carry):
-        row = pl.ds(layer, 1)
-        inv_denom = meta[pl.ds(layers + layer, 1), :]
+    def step(layer):
+        row = slice(layer, layer + 1)
+        inv_denom = inv_denoms[row]
         weight_low = inv_denom * span_in[0, row, :]
         weight_high = inv_denom * span_in[1, row, :]
         kinds_low = kinds_in[1, row, :]
@@ -149,12 +150,17 @@
             g_out[layer, tracer] = (
                 inv_denom * jnp.concatenate(solved, axis=1) - weight_low * low_term - weight_high * high_term
             )
-        store(layer).start()
-        return carry
-
-    lax.fori_loop(0, layers, step, 0)
+
     for layer in range(layers):
-        store(layer).wait()
+        step(layer)
+
+
+def own_columns(place, k, width):
+    return pl.ds(pl.multiple_of((place[0] ^ k) * width, width), width)
+
+
+def meta_rows(meta, own, layers, layer):
+    return [meta[i * layers + layer : i * layers + layer + 1, own] for i in range(4)]
 
 
 def edge_value(fix, layer, tracer, tracers, side):
@@ -175,12 +181,9 @@
 
 
 def local_forward_kernel(
-    place, pair, cross, g_hbm, meta, sides, table, f_out, m0, m1, m2, m3, g_in, sems
+    place, pair, cross, g_in, meta, sides, table, f_out, m0, m1, m2, m3
 ):
     layers, tracers, dofs, columns = g_in.shape
-    copies = [pltpu.make_async_copy(g_hbm.at[layer], g_in.at[layer], sems.at[layer]) for layer in range(layers)]
-    for copy in copies:
-        copy.start()
     odd = place[2] == 1
     from_low = pltpu.roll(jnp.where(odd, pair[...], cross[...]), 64, 1)
     from_high = pltpu.roll(jnp.where(odd, cross[...], pair[...]), tracers, 1)
@@ -188,7 +191,6 @@
     halo = jnp.where(lane % (2 * tracers) < tracers, from_low, from_high)
     fix = -(sides[1:2, :] * typed(table[...], halo, kind_masks(sides[0:1, :], dofs)))
     for layer in range(layers):
-        copies[layer].wait()
         factor = meta[2 * layers + layer : 2 * layers + layer + 1, :]
         kinds = meta[3 * layers + layer : 3 * layers + layer + 1, :]
         for piece in pieces(columns):
@@ -212,7 +214,18 @@
             target[top + 3 * layers :, :] = jnp.zeros((target.shape[0] - top - 3 * layers, width), F32)
 
 
-def local_backward_kernel(place, f_in, meta, table, m0, m1, m2, m3, carried):
+def local_backward_kernel(
+    place, f_in, meta, down, inverse, table, m0, m1, m2, m3, carried, downs, inv, sems
+):
+    copies = [
+        pltpu.make_async_copy(source, target, sems.at[i])
+        for i, (source, target) in enumerate(((down, downs), (inverse, inv)))
+    ]
+    for copy in copies:
+        copy.start()
+    for copy in copies:
+        copy.wait()
+    fold_table(inv, downs, table)
     layers, tracers, dofs, columns = f_in.shape
     for layer in reversed(range(layers)):
         scale, inv_denom, kinds = (meta[i * layers + layer : i * layers + layer + 1, :] for i in (0, 1, 3))
@@ -284,9 +297,9 @@
     lax.fori_loop(0, MEMBERS - 1 if turn == 0 else MEMBERS, step, 0)
 
 
-def take(place, sources, target):
+def take(place, sources, target, top=0):
     for k, source in enumerate(sources):
-        target[place[0] ^ k] = source[...]
+        target[place[0] ^ k, top:, :] = source[top:, :]
 
 
 def give(place, targets, source, first):
@@ -346,7 +359,7 @@
 
     @pl.when(place[1] == turn)
     def active():
-        take(place, (m0, m1, m2, m3), blocks)
+        take(place, (m0, m1, m2, m3), blocks, returning.shape[1])
         take(place, (e0, e1, e2, e3), terms)
         returning[MEMBERS] = inflow[...]
         backward_chain(turn, layers, tracers, table, blocks, terms, returning, states)
@@ -356,52 +369,43 @@
     keep(place, turn, olds, outs)
 
 
-def take_inflow(place, sources, state):
-    tracers, dofs, columns = state.shape
-    width = columns // MEMBERS
-    for k, source in enumerate(sources):
-        own = pl.ds(pl.multiple_of((place[0] ^ k) * width, width), width)
-        for tracer in range(tracers):
-            state[tracer, :, own] = source[tracer * dofs : (tracer + 1) * dofs, :]
-
-
-def final_forward_kernel(place, f_in, meta, table, *rest):
-    sources, (f_out, state) = rest[:-2], rest[-2:]
-    layers, tracers, dofs, columns = f_in.shape
-    take_inflow(place, sources, state)
+def final_forward_kernel(place, f_in, meta, table, m0, m1, m2, m3, f_out, state):
+    _, layers, tracers, dofs, width = f_out.shape
     for layer in range(layers):
-        factor, kinds = (meta[i * layers + layer : i * layers + layer + 1, :] for i in (2, 3))
-        for piece in pieces(columns):
-            masks = kind_masks(kinds[:, piece], dofs)
+        for k, message in enumerate((m0, m1, m2, m3)):
+            own = own_columns(place, k, width)
+            factor, kinds = meta_rows(meta, own, layers, layer)[2:]
+            masks = kind_masks(kinds, dofs)
             for tracer in range(tracers):
-                value = -(factor[:, piece] * typed(table[...], state[tracer, :, piece], masks))
-                f_out[layer, tracer, :, piece] = f_in[layer, tracer, :, piece] + value
+                here = slice(tracer * dofs, (tracer + 1) * dofs)
+                before = message[here, :] if layer == 0 else state[k, tracer]
+                value = -(factor * typed(table[...], before, masks))
+                f_out[k, layer, tracer] = f_in[layer, tracer, :, own] + value
                 if layer < layers - 1:
-                    state[tracer, :, piece] = value
-
-
-def final_backward_kernel(place, f_in, meta, table, *rest):
-    sources, (out, carried, solved, sems) = rest[:-4], rest[-4:]
-    layers, tracers, dofs, columns = f_in.shape
-    take_inflow(place, sources, carried)
+                    state[k, tracer] = value
+
+
+def final_backward_kernel(ks, place, f_in, meta, table, *rest):
+    messages = rest[: len(ks)]
+    out, carried, solved, sems = rest[-4:]
+    _, layers, tracers, dofs, width = f_in.shape
     copies = []
     for layer in reversed(range(layers)):
-        scale, inv_denom, kinds = (meta[i * layers + layer : i * layers + layer + 1, :] for i in (0, 1, 3))
-        for tracer in range(tracers):
-            solved[layer, tracer] = f_in[layer, tracer] - inv_denom * carried[tracer]
+        for i, (k, message) in enumerate(zip(ks, messages)):
+            own = own_columns(place, k, width)
+            scale, inv_denom, _, kinds = meta_rows(meta, own, layers, layer)
+            masks = kind_masks(kinds, dofs)
+            for tracer in range(tracers):
+                here = slice(tracer * dofs, (tracer + 1) * dofs)
+                before = message[here, :] if layer == layers - 1 else carried[i, tracer]
+                solved[i, layer, tracer] = f_in[k, layer, tracer] - inv_denom * before
             copies.append(
-                pltpu.make_async_copy(
-                    solved.at[layer, tracer], out.at[layer, tracer], sems.at[layer * tracers + tracer]
-                )
+                pltpu.make_async_copy(solved.at[i, layer], out.at[layer, :, :, own], sems.at[i, layer])
             )
             copies[-1].start()
-        if layer > 0:
-            for piece in pieces(columns):
-                masks = kind_masks(kinds[:, piece], dofs)
+            if layer > 0:
                 for tracer in range(tracers):
-                    carried[tracer, :, piece] = scale[:, piece] * typed(
-                        table[...], solved[layer, tracer, :, piece], masks
-                    )
+                    carried[i, tracer] = scale * typed(table[...], solved[i, layer, tracer], masks)
     for copy in copies:
         copy.wait()
 
@@ -425,68 +429,74 @@
     table_shape = (KINDS * dofs, 4 * dofs)
     fix = full((dofs, 128))
 
+    def sent(value, k):
+        return lax.ppermute(value, "stream", [(i, i ^ k) for i in range(count)]) if k else value
+
     def exchanged(messages):
-        return [messages[0]] + [
-            lax.ppermute(messages[k], "stream", [(i, i ^ k) for i in range(count)])
-            for k in range(1, MEMBERS)
-        ]
+        return [sent(value, k) for k, value in enumerate(messages)]
 
     def between(values, step):
         pairs = [(step * MEMBERS + i, (step + 1) * MEMBERS + i) for i in range(MEMBERS)]
         return lax.ppermute(values, "stream", pairs + [(b, a) for a, b in pairs])
 
-    column_state = pltpu.VMEM((tracers, dofs, columns), F32)
+    piece = (layers, tracers, dofs, width)
+    early, late = tuple(range(MEMBERS - 1)), (MEMBERS - 1,)
     message = full((rows, width))
     long_message = full((long_rows, width))
     table = jax.ShapeDtypeStruct(table_shape, BF16)
-    inputs = (rhs, lagged, kinds, stream, span, absorb, up, down, inverse)
-
-    g, meta, sides, edges, up_table, down_table = pl.pallas_call(
+    inputs = (rhs, lagged, kinds, stream, span, absorb, up, inverse)
+
+    g, meta, sides, edges, up_table = pl.pallas_call(
         span_kernel,
         out_shape=(
-            pltpu.HBM(rhs.shape, F32), full((4 * layers, columns)), full((8, 128)), fix, table, table,
+            full(rhs.shape), full((4 * layers, columns)), full((8, 128)), fix, table,
         ),
-        in_specs=[anywhere] * len(inputs),
-        out_specs=(anywhere,) + (vmem,) * 5,
-        scratch_shapes=[pltpu.VMEM((dofs, 4 * dofs), BF16), pltpu.VMEM(rhs.shape, F32)]
+        in_specs=[smem] + [anywhere] * len(inputs),
+        out_specs=(vmem,) * 5,
+        scratch_shapes=[pltpu.VMEM((dofs, 4 * dofs), BF16)]
         + [pltpu.VMEM(value.shape, value.dtype) for value in inputs]
-        + [pltpu.SemaphoreType.DMA((2 * layers + 7,)), pltpu.SemaphoreType.DMA((layers,))],
+        + [pltpu.SemaphoreType.DMA((2 * layers + 6,))],
         name="span_terms",
-        **params(2 * layers * product, 3 * field, some + 4 * field),
-    )(*(pltpu.with_memory_space_constraint(value, pltpu.HBM) for value in inputs))
+        **params(1 << 10, 1 << 10, some + 3 * field),
+    )(place, *(pltpu.with_memory_space_constraint(value, pltpu.HBM) for value in inputs))
 
     across = lax.axis_size("span")
     crossing = [(i, i + 1) for i in range(1, across - 1, 2)]
     pair = lax.ppermute(edges, "span", [(i, i ^ 1) for i in range(across)])
     cross = lax.ppermute(edges, "span", crossing + [(b, a) for a, b in crossing])
 
+    def piece_scratch(ks):
+        return [pltpu.VMEM((len(ks), *piece), F32), pltpu.SemaphoreType.DMA((len(ks), layers))]
+
     f_zero, *out_b = pl.pallas_call(
         local_forward_kernel,
         out_shape=(full(rhs.shape),) + (long_message,) * MEMBERS,
-        in_specs=[smem, vmem, vmem, anywhere] + [vmem] * 3,
+        in_specs=[smem] + [vmem] * 6,
         out_specs=(vmem,) * (1 + MEMBERS),
-        scratch_shapes=[pltpu.VMEM(rhs.shape, F32), pltpu.SemaphoreType.DMA((layers,))],
         name="local_forward",
-        **params(layers * product, field, some + 2 * field),
-    )(place, pair, cross, pltpu.with_memory_space_constraint(g, pltpu.HBM), meta, sides, up_table)
+        **params(1 << 10, 1 << 10, some + field),
+    )(place, pair, cross, g, meta, sides, up_table)
     in_b = exchanged(out_b)
 
-    out_e = pl.pallas_call(
+    down_table, *out_e = pl.pallas_call(
         local_backward_kernel,
-        out_shape=(message,) * MEMBERS,
-        in_specs=[smem] + [vmem] * 3,
-        out_specs=(vmem,) * MEMBERS,
-        scratch_shapes=[column_state],
+        out_shape=(table,) + (message,) * MEMBERS,
+        in_specs=[smem] + [vmem] * 2 + [anywhere] * 2,
+        out_specs=(vmem,) * (1 + MEMBERS),
+        scratch_shapes=[
+            pltpu.VMEM((tracers, dofs, columns), F32), pltpu.VMEM(down.shape, F32),
+            pltpu.VMEM(inverse.shape, F32), pltpu.SemaphoreType.DMA((2,)),
+        ],
         name="local_backward",
-        **params(layers * product, field, some + field),
-    )(place, f_zero, meta, down_table)
+        **params(1 << 10, 1 << 10, some + field),
+    )(place, f_zero, meta, *(pltpu.with_memory_space_constraint(value, pltpu.HBM) for value in (down, inverse)))
     in_e = exchanged(out_e)
     in_b, _ = lax.optimization_barrier((in_b, out_e))
 
     blocks = pltpu.VMEM((MEMBERS, long_rows, width), F32)
     inner = pltpu.VMEM((MEMBERS + 1, rows, width), F32)
     held = (MEMBERS, layers, rows, width)
-    inflow = jnp.zeros((rows, width), F32)
+    inflow = out_e[0]
     states, out_f = [], []
     for turn in range(groups - 1):
         state, *out_f, outflow = pl.pallas_call(
@@ -496,7 +506,7 @@
             out_specs=(vmem,) * (MEMBERS + 2),
             scratch_shapes=[blocks, inner],
             name=f"chain_forward_{turn}",
-            **params(layers * product, 2 * field, some + field),
+            **params(1 << 10, 1 << 10, some + field),
         )(place, inflow, up_table, *in_b, *out_f)
         states.append(state)
         inflow = between(outflow, turn)
@@ -508,7 +518,7 @@
         out_specs=(vmem,) * (2 * MEMBERS + 1),
         scratch_shapes=[blocks, inner, inner, inner, pltpu.VMEM(held, F32)],
         name="chain_last",
-        **params(2 * layers * product, 2 * field, some + 2 * field),
+        **params(1 << 10, 1 << 10, some + 2 * field),
     )(place, inflow, up_table, down_table, *in_b, *in_e, *out_f)
     in_f = exchanged(out_f)
     out_h = [h0, h1, h2, h3]
@@ -522,32 +532,34 @@
             out_specs=(vmem,) * (MEMBERS + 1),
             scratch_shapes=[blocks, inner, inner],
             name=f"chain_backward_{turn}",
-            **params(layers * product, 2 * field, some + field),
+            **params(1 << 10, 1 << 10, some + field),
         )(place, inflow, down_table, *in_b, *in_e, states[turn], *out_h)
     in_h = exchanged(out_h)
 
     f_part = pl.pallas_call(
         final_forward_kernel,
-        out_shape=full(rhs.shape),
-        in_specs=[smem] + [vmem] * (3 + len(in_f)),
+        out_shape=full((MEMBERS, *piece)),
+        in_specs=[smem] + [vmem] * (3 + MEMBERS),
         out_specs=vmem,
-        scratch_shapes=[column_state],
+        scratch_shapes=[pltpu.VMEM((MEMBERS, tracers, dofs, width), F32)],
         name="final_forward",
-        **params(layers * product, 2 * field, some + 2 * field),
+        **params(1 << 10, 1 << 10, some + 2 * field),
     )(place, f_zero, meta, up_table, *in_f)
-    return pl.pallas_call(
-        final_backward_kernel,
-        out_shape=full(rhs.shape),
-        in_specs=[smem] + [vmem] * (3 + len(in_h)),
-        out_specs=anywhere,
-        scratch_shapes=[
-            column_state,
-            pltpu.VMEM(rhs.shape, F32),
-            pltpu.SemaphoreType.DMA((layers * tracers,)),
-        ],
-        name="final_backward",
-        **params(layers * product, 2 * field, some + 2 * field),
-    )(place, f_part, meta, down_table, *in_h)
+    out = ()
+    for ks in (early, late):
+        out = (
+            pl.pallas_call(
+                functools.partial(final_backward_kernel, ks),
+                out_shape=full(rhs.shape),
+                in_specs=[smem] + [vmem] * (3 + len(ks)) + [anywhere] * len(out),
+                out_specs=anywhere,
+                scratch_shapes=[pltpu.VMEM((len(ks), tracers, dofs, width), F32)] + piece_scratch(ks),
+                input_output_aliases={4 + len(ks): 0} if out else {},
+                name=f"final_backward_{ks[0]}",
+                **params(1 << 10, 1 << 10, some + field),
+            )(place, f_part, meta, down_table, *(in_h[k] for k in ks), *out),
+        )
+    return out[0]
 
 
 def solution(mesh):

time: 98.7 us -> 95.4 us (0.967)
  waiting for transfers between devices: 30.3 us -> 26.6 us
    ppermute x12, waiting for transfers between devices: 19.8 us -> 15.2 us  [sent(): lax.ppermute(value, 'stream', [(i, i ^ k) for i in range(count)])]
    pallas_call x4 -> x5, Pallas kernels: 22.9 us -> 24.6 us  [the longest x1 9.25 us: per_device(): pl.pallas_call(span_kernel, out_shape=(full(rhs.shape), full((4 * layers,...]
    pallas_call x1, Pallas kernels: 5.21 us -> 3.75 us  [per_device(): pl.pallas_call(local_forward_kernel, out_shape=(full(rhs.shape),) + (long...]
    ppermute x2, waiting for transfers between devices: 10.4 us -> 11.4 us  [between(): return lax.ppermute(values, 'stream', pairs + [(b, a) for a, b in pairs])]
  transfers between devices with their start and end apart: 16 -> 16, of which waited for: 9 -> 8; matrix products, arithmetic and copies ran while one was open for 0% -> 0% of each run, Pallas kernels for 18% -> 24%
where the time goes in v4:
time: 95.4 us; the launch traced here: 95.2 us
  Pallas kernels  38.6 us (40%)
  starting transfers between devices  29.7 us (31%)
  waiting for transfers between devices  26.6 us (28%)
    ppermute x12, waiting for transfers between devices, sent(): lax.ppermute(value, 'stream', [(i, i ^ k) for i in range(count)])  15.2 us
    ppermute x12, starting transfers between devices, sent(): lax.ppermute(value, 'stream', [(i, i ^ k) for i in range(count)])  15 us
    ppermute x2, starting transfers between devices, between(): return lax.ppermute(values, 'stream', pairs + [(b, a) for a, b in pairs])  13.3 us
    ppermute x2, waiting for transfers between devices, between(): return lax.ppermute(values, 'stream', pairs + [(b, a) for a, b in pairs])  11.4 us
    pallas_call x1, Pallas kernels, per_device(): pl.pallas_call(span_kernel, out_shape=(full(rhs.shape), full((4 * layers,...  9.25 us
    pallas_call x2, Pallas kernels, per_device(): pl.pallas_call(functools.partial(final_backward_kernel, ks), out_shape=fu...  5.7 us
    pallas_call x1, Pallas kernels, per_device(): pl.pallas_call(local_backward_kernel, out_shape=(table,) + (message,) * M...  5.44 us
    pallas_call x1, Pallas kernels, per_device(): pl.pallas_call(functools.partial(chain_backward_kernel, turn, layers, tra...  5.24 us
  transfers between devices with their start and end apart: 16, of which 8 were waited for; matrix products, arithmetic and copies ran while one was open for 0% of the time, Pallas kernels for 24%

profile of v4, /device:TPU:0, one launch (start us, length us, event | category | flops | bytes accessed | tf_op | source)
XLA Modules:
  0.0 95.2 jit_solution(17320529734980637015)
XLA Ops:
  0.0 0.1 pad_add_fusion.place
  0.1 9.3 %span_terms.1 = (f32[4,4,64,1024]{3,2,1,0:T(8,128)S(1)}, f32[16,1024]{1,0:T(8,128)S(1)}, f32[8,128]{1,0:T(8,128)S(1)}, f32[64,128]{1,0:T(8,128)S(1)}, bf16[384,256]{1,0:T(8,128)(2,1)S(1)}) custom-call(s32[3]{0:T(128)S(1)} %pad_add_fusion.place, f32[4,4,64,1024]{3,2,1,0:T(8,128)} %rhs.1, f32[4,4,64,1024]{3,2,1,0:T(8,128)} %lagged.1, s32[3,4,1024]{2,1,0:T(4,128)} %kinds.1, ...), custom_call_target="tpu_custom_call" | custom-call | flops 1024 | bytes 1024 | tf_op jit(solution)/shard_map/span_terms/pallas_call | solution.py:449
  9.3 0.5 collective-permute-start
  9.9 0.8 collective-permute-start.1
  10.7 3.7 %local_forward.1 = (f32[4,4,64,1024]{3,2,1,0:T(8,128)S(1)}, f32[272,256]{1,0:T(8,128)S(1)}, f32[272,256]{1,0:T(8,128)S(1)}, f32[272,256]{1,0:T(8,128)S(1)}, f32[272,256]{1,0:T(8,128)S(1)}) custom-call(s32[3]{0:T(128)S(1)} %pad_add_fusion.place, f32[64,128]{1,0:T(8,128)S(1)} %collective-permute-done.pair, f32[64,128]{1,0:T(8,128)S(1)} %collective-permute-done.1.cross, ...), custom_call_target="tpu_custom_call" | custom-call | flops 1024 | bytes 1024 | tf_op jit(solution)/shard_map/local_forward/pallas_call | solution.py:471
  14.5 2.9 %collective-permute-start.2 = (f32[272,256]{1,0:T(8,128)S(1)}, f32[272,256]{1,0:T(8,128)S(1)}, u32[]{:S(2)}, u32[]{:S(2)}) collective-permute-start(f32[272,256]{1,0:T(8,128)S(1)} %get-tuple-element.51), channel_id=1, source_target_pairs={{0,4},{4,0},{8,12},{12,8},{16,20},{20,16},{24,28},{28,24},{1,5},{5... | collective-permute-start | bytes 835592 | tf_op jit(solution)/shard_map/ppermute | solution.py:433
  17.4 1.6 %collective-permute-start.3 = (f32[272,256]{1,0:T(8,128)S(1)}, f32[272,256]{1,0:T(8,128)S(1)}, u32[]{:S(2)}, u32[]{:S(2)}) collective-permute-start(f32[272,256]{1,0:T(8,128)S(1)} %get-tuple-element.52), channel_id=1, source_target_pairs={{0,8},{4,12},{8,0},{12,4},{16,24},{20,28},{24,16},{28,20},{1,9},{5... | collective-permute-start | bytes 835592 | tf_op jit(solution)/shard_map/ppermute | solution.py:433
  19.0 5.4 %local_backward.1 = (bf16[384,256]{1,0:T(8,128)(2,1)S(1)}, f32[256,256]{1,0:T(8,128)S(1)}, f32[256,256]{1,0:T(8,128)S(1)}, f32[256,256]{1,0:T(8,128)S(1)}, f32[256,256]{1,0:T(8,128)S(1)}) custom-call(s32[3]{0:T(128)S(1)} %pad_add_fusion.place, f32[4,4,64,1024]{3,2,1,0:T(8,128)S(1)} %get-tuple-element.48.f_in, f32[16,1024]{1,0:T(8,128)S(1)} %get-tuple-element.45.meta, ...), custom_call_target="tpu_custom_call" | custom-call | flops 1024 | bytes 1024 | tf_op jit(solution)/shard_map/local_backward/pallas_call | solution.py:481
  24.4 2.0 %collective-permute-start.6 = (f32[256,256]{1,0:T(8,128)S(1)}, f32[256,256]{1,0:T(8,128)S(1)}, u32[]{:S(2)}, u32[]{:S(2)}) collective-permute-start(f32[256,256]{1,0:T(8,128)S(1)} %get-tuple-element.54), channel_id=1, source_target_pairs={{0,4},{4,0},{8,12},{12,8},{16,20},{20,16},{24,28},{28,24},{1,5},{5... | collective-permute-start | bytes 786440 | tf_op jit(solution)/shard_map/ppermute | solution.py:433
  26.4 1.6 %collective-permute-start.7 = (f32[256,256]{1,0:T(8,128)S(1)}, f32[256,256]{1,0:T(8,128)S(1)}, u32[]{:S(2)}, u32[]{:S(2)}) collective-permute-start(f32[256,256]{1,0:T(8,128)S(1)} %get-tuple-element.55), channel_id=1, source_target_pairs={{0,8},{4,12},{8,0},{12,4},{16,24},{20,28},{24,16},{28,20},{1,9},{5... | collective-permute-start | bytes 786440 | tf_op jit(solution)/shard_map/ppermute | solution.py:433
  28.0 0.0 collective-permute-start.8
  28.0 0.8 collective-permute-done.4.m3
  28.8 4.4 %chain_forward_0.1 = (f32[4,4,256,256]{3,2,1,0:T(8,128)S(1)}, f32[256,256]{1,0:T(8,128)S(1)}, f32[256,256]{1,0:T(8,128)S(1)}, f32[256,256]{1,0:T(8,128)S(1)}, f3...) custom-call(s32[3]{0:T(128)S(1)} %pad_add_fusion.place, f32[256,256]{1,0:T(8,128)S(1)} %get-tuple-element.49.inflow.e0, ...), custom_call_target="tpu_custom_call" | custom-call | flops 1024 | bytes 1024 | tf_op jit(solution)/shard_map/chain_forward_0/pallas_call | solution.py:502
  33.2 0.1 collective-permute-start.5
  33.3 3.2 %collective-permute-done.6.e1 = f32[256,256]{1,0:T(8,128)S(1)} collective-permute-done((f32[256,256]{1,0:T(8,128)S(1)}, f32[256,256]{1,0:T(8,128)S(1)}, u32[]{:S(2)}, u32[]{:S(2)}) %collective-permute-start.6) | collective-permute-done | bytes 262176 | tf_op jit(solution)/shard_map/ppermute | solution.py:433
  36.5 7.1 %collective-permute-done.8.e3 = f32[256,256]{1,0:T(8,128)S(1)} collective-permute-done((f32[256,256]{1,0:T(8,128)S(1)}, f32[256,256]{1,0:T(8,128)S(1)}, u32[]{:S(2)}, u32[]{:S(2)}) %collective-permute-start.8) | collective-permute-done | bytes 262176 | tf_op jit(solution)/shard_map/ppermute | solution.py:433
  43.6 2.3 %collective-permute-done.5.inflow = f32[256,256]{1,0:T(8,128)S(1)} collective-permute-done((f32[256,256]{1,0:T(8,128)S(1)}, f32[256,256]{1,0:T(8,128)S(1)}, u32[]{:S(2)}, u32[]{:S(2)}) %collective-permute-start.5) | collective-permute-done | bytes 262176 | tf_op jit(solution)/shard_map/ppermute | solution.py:440
  46.0 0.6 chain_last.1
  46.6 13.3 %collective-permute-start.12 = (f32[256,256]{1,0:T(8,128)S(1)}, f32[256,256]{1,0:T(8,128)S(1)}, u32[]{:S(2)}, u32[]{:S(2)}) collective-permute-start(f32[256,256]{1,0:T(8,128)S(1)} %get-tuple-element.71), channel_id=1, source_target_pairs={{0,16},{4,20},{8,24},{12,28},{16,0},{20,4},{24,8},{28,12},{1,17},{... | collective-permute-start | bytes 786440 | tf_op jit(solution)/shard_map/ppermute | solution.py:440
  59.9 0.4 collective-permute-start.10
  60.2 2.0 %collective-permute-start.11 = (f32[256,256]{1,0:T(8,128)S(1)}, f32[256,256]{1,0:T(8,128)S(1)}, u32[]{:S(2)}, u32[]{:S(2)}) collective-permute-start(f32[256,256]{1,0:T(8,128)S(1)} %get-tuple-element.70), channel_id=1, source_target_pairs={{0,12},{4,8},{8,4},{12,0},{16,28},{20,24},{24,20},{28,16},{1,13},{... | collective-permute-start | bytes 786440 | tf_op jit(solution)/shard_map/ppermute | solution.py:433
  62.2 1.1 %collective-permute-start.9 = (f32[256,256]{1,0:T(8,128)S(1)}, f32[256,256]{1,0:T(8,128)S(1)}, u32[]{:S(2)}, u32[]{:S(2)}) collective-permute-start(f32[256,256]{1,0:T(8,128)S(1)} %get-tuple-element.68), channel_id=1, source_target_pairs={{0,4},{4,0},{8,12},{12,8},{16,20},{20,16},{24,28},{28,24},{1,5},{5... | collective-permute-start | bytes 786440 | tf_op jit(solution)/shard_map/ppermute | solution.py:433
  63.3 9.1 %collective-permute-done.12.inflow = f32[256,256]{1,0:T(8,128)S(1)} collective-permute-done((f32[256,256]{1,0:T(8,128)S(1)}, f32[256,256]{1,0:T(8,128)S(1)}, u32[]{:S(2)}, u32[]{:S(2)}) %collective-permute-start.12) | collective-permute-done | bytes 262176 | tf_op jit(solution)/shard_map/ppermute | solution.py:440
  72.4 5.2 %chain_backward_0.1 = (f32[256,256]{1,0:T(8,128)S(1)}, f32[256,256]{1,0:T(8,128)S(1)}, f32[256,256]{1,0:T(8,128)S(1)}, f32[256,256]{1,0:T(8,128)S(1)}, f32[256,256]{1,0:T(8,128)}) custom-call(s32[3]{0:T(128)S(1)} %pad_add_fusion.place, f32[256,256]{1,0:T(8,128)S(1)} %collective-permute-done.12.inflow, ...), custom_call_target="tpu_custom_call" | custom-call | flops 1024 | bytes 1024 | tf_op jit(solution)/shard_map/chain_backward_0/pallas_call | solution.py:528
  77.7 1.7 %collective-permute-start.15 = (f32[256,256]{1,0:T(8,128)S(1)}, f32[256,256]{1,0:T(8,128)S(1)}, u32[]{:S(2)}, u32[]{:S(2)}) collective-permute-start(f32[256,256]{1,0:T(8,128)S(1)} %get-tuple-element.80), channel_id=1, source_target_pairs={{0,8},{4,12},{8,0},{12,4},{16,24},{20,28},{24,16},{28,20},{1,9},{5... | collective-permute-start | bytes 786440 | tf_op jit(solution)/shard_map/ppermute | solution.py:433
  79.3 1.8 %collective-permute-start.13 = (f32[256,256]{1,0:T(8,128)S(1)}, f32[256,256]{1,0:T(8,128)S(1)}, u32[]{:S(2)}, u32[]{:S(2)}) collective-permute-start(f32[256,256]{1,0:T(8,128)S(1)} %get-tuple-element.77), channel_id=1, source_target_pairs={{0,12},{4,8},{8,4},{12,0},{16,28},{20,24},{24,20},{28,16},{1,13},{... | collective-permute-start | bytes 786440 | tf_op jit(solution)/shard_map/ppermute | solution.py:433
  81.1 4.2 %final_forward.1.f_in = f32[4,4,4,64,256]{4,3,2,1,0:T(8,128)S(1)} custom-call(s32[3]{0:T(128)S(1)} %pad_add_fusion.place, f32[4,4,64,1024]{3,2,1,0:T(8,128)S(1)} %get-tuple-element.48.f_in, f32[16,1024]{1,0:T(8,128)S(1)} %get-tuple-element.45.meta, bf16[384,256]{1,0:T(8,128)(2,1)S(1)} %get-tuple-element.47.table.up_table, ...), custom_call_target="tpu_custom_call" | custom-call | flops 1024 | bytes 1024 | tf_op jit(solution)/shard_map/final_forward/pallas_call | solution.py:539
  85.3 0.7 collective-permute-done.14.rest_1_
  86.0 0.8 collective-permute-done.15.rest_2_
  86.8 3.5 %final_backward_0.1.rest_1_ = f32[4,4,64,1024]{3,2,1,0:T(8,128)} custom-call(s32[3]{0:T(128)S(1)} %pad_add_fusion.place, f32[4,4,4,64,256]{4,3,2,1,0:T(8,128)S(1)} %final_forward.1.f_in, f32[16,1024]{1,0:T(8,128)S(1)} %get-tuple-element.45.meta, bf16[384,256]{1,0:T(8,128)(2,1)S(1)} %get-tuple-element.62.down_table.table, ...), custom_call_target="tpu_custom_call" | custom-call | flops 1024 | bytes 1024 | tf_op jit(solution)/shard_map/final_backward_0/pallas_call | solution.py:551
  90.3 2.5 %collective-permute-done.13.rest_0_ = f32[256,256]{1,0:T(8,128)S(1)} collective-permute-done((f32[256,256]{1,0:T(8,128)S(1)}, f32[256,256]{1,0:T(8,128)S(1)}, u32[]{:S(2)}, u32[]{:S(2)}) %collective-permute-start.13) | collective-permute-done | bytes 262176 | tf_op jit(solution)/shard_map/ppermute | solution.py:433
  92.8 2.2 %final_backward_3.1 = f32[4,4,64,1024]{3,2,1,0:T(8,128)} custom-call(s32[3]{0:T(128)S(1)} %pad_add_fusion.place, f32[4,4,4,64,256]{4,3,2,1,0:T(8,128)S(1)} %final_forward.1.f_in, f32[16,1024]{1,0:T(8,128)S(1)} %get-tuple-element.45.meta, bf16[384,256]{1,0:T(8,128)(2,1)S(1)} %get-tuple-element.62.down_table.table, ...), custom_call_target="tpu_custom_call", output_to_operand_aliasing={{}: (5, {})} | custom-call | flops 1024 | bytes 1024 | tf_op jit(solution)/shard_map/final_backward_3/pallas_call | solution.py:551
  (10 shorter events, 0.0 us)
Async XLA Ops:
  9.3 1.4 %collective-permute-start = (f32[64,128]{1,0:T(8,128)S(1)}, f32[64,128]{1,0:T(8,128)S(1)}, u32[]{:S(2)}, u32[]{:S(2)}) collective-permute-start(f32[64,128]{1,0:T(8,128)S(1)} %get-tuple-element.43), channel_id=1, source_target_pairs={{0,1},{1,0},{2,3},{3,2},{4,5},{5,4},{6,7},{7,6},{8,9},{9,8},{10,11... | collective-permute-start | bytes 98312 | tf_op jit(solution)/shard_map/ppermute | solution.py:465
  9.9 0.9 collective-permute-start.1
  14.5 13.5 %collective-permute-start.2 = (f32[272,256]{1,0:T(8,128)S(1)}, f32[272,256]{1,0:T(8,128)S(1)}, u32[]{:S(2)}, u32[]{:S(2)}) collective-permute-start(f32[272,256]{1,0:T(8,128)S(1)} %get-tuple-element.51), channel_id=1, source_target_pairs={{0,4},{4,0},{8,12},{12,8},{16,20},{20,16},{24,28},{28,24},{1,5},{5... | collective-permute-start | bytes 835592 | tf_op jit(solution)/shard_map/ppermute | solution.py:433
  17.4 10.6 %collective-permute-start.3 = (f32[272,256]{1,0:T(8,128)S(1)}, f32[272,256]{1,0:T(8,128)S(1)}, u32[]{:S(2)}, u32[]{:S(2)}) collective-permute-start(f32[272,256]{1,0:T(8,128)S(1)} %get-tuple-element.52), channel_id=1, source_target_pairs={{0,8},{4,12},{8,0},{12,4},{16,24},{20,28},{24,16},{28,20},{1,9},{5... | collective-permute-start | bytes 835592 | tf_op jit(solution)/shard_map/ppermute | solution.py:433
  19.0 9.8 %collective-permute-start.4 = (f32[272,256]{1,0:T(8,128)S(1)}, f32[272,256]{1,0:T(8,128)S(1)}, u32[]{:S(2)}, u32[]{:S(2)}) collective-permute-start(f32[272,256]{1,0:T(8,128)S(1)} %get-tuple-element.53), channel_id=1, source_target_pairs={{0,12},{4,8},{8,4},{12,0},{16,28},{20,24},{24,20},{28,16},{1,13},{... | collective-permute-start | bytes 835592 | tf_op jit(solution)/shard_map/ppermute | solution.py:433
  24.4 12.1 %collective-permute-start.6 = (f32[256,256]{1,0:T(8,128)S(1)}, f32[256,256]{1,0:T(8,128)S(1)}, u32[]{:S(2)}, u32[]{:S(2)}) collective-permute-start(f32[256,256]{1,0:T(8,128)S(1)} %get-tuple-element.54), channel_id=1, source_target_pairs={{0,4},{4,0},{8,12},{12,8},{16,20},{20,16},{24,28},{28,24},{1,5},{5... | collective-permute-start | bytes 786440 | tf_op jit(solution)/shard_map/ppermute | solution.py:433
  26.4 10.1 %collective-permute-start.7 = (f32[256,256]{1,0:T(8,128)S(1)}, f32[256,256]{1,0:T(8,128)S(1)}, u32[]{:S(2)}, u32[]{:S(2)}) collective-permute-start(f32[256,256]{1,0:T(8,128)S(1)} %get-tuple-element.55), channel_id=1, source_target_pairs={{0,8},{4,12},{8,0},{12,4},{16,24},{20,28},{24,16},{28,20},{1,9},{5... | collective-permute-start | bytes 786440 | tf_op jit(solution)/shard_map/ppermute | solution.py:433
  28.0 15.7 %collective-permute-start.8 = (f32[256,256]{1,0:T(8,128)S(1)}, f32[256,256]{1,0:T(8,128)S(1)}, u32[]{:S(2)}, u32[]{:S(2)}) collective-permute-start(f32[256,256]{1,0:T(8,128)S(1)} %get-tuple-element.56), channel_id=1, source_target_pairs={{0,12},{4,8},{8,4},{12,0},{16,28},{20,24},{24,20},{28,16},{1,13},{... | collective-permute-start | bytes 786440 | tf_op jit(solution)/shard_map/ppermute | solution.py:433
  33.2 12.8 %collective-permute-start.5 = (f32[256,256]{1,0:T(8,128)S(1)}, f32[256,256]{1,0:T(8,128)S(1)}, u32[]{:S(2)}, u32[]{:S(2)}) collective-permute-start(f32[256,256]{1,0:T(8,128)S(1)} %get-tuple-element.61), channel_id=1, source_target_pairs={{0,16},{4,20},{8,24},{12,28},{16,0},{20,4},{24,8},{28,12},{1,17},{... | collective-permute-start | bytes 786440 | tf_op jit(solution)/shard_map/ppermute | solution.py:440
  46.6 25.8 %collective-permute-start.12 = (f32[256,256]{1,0:T(8,128)S(1)}, f32[256,256]{1,0:T(8,128)S(1)}, u32[]{:S(2)}, u32[]{:S(2)}) collective-permute-start(f32[256,256]{1,0:T(8,128)S(1)} %get-tuple-element.71), channel_id=1, source_target_pairs={{0,16},{4,20},{8,24},{12,28},{16,0},{20,4},{24,8},{28,12},{1,17},{... | collective-permute-start | bytes 786440 | tf_op jit(solution)/shard_map/ppermute | solution.py:440
  59.9 19.5 %collective-permute-start.10 = (f32[256,256]{1,0:T(8,128)S(1)}, f32[256,256]{1,0:T(8,128)S(1)}, u32[]{:S(2)}, u32[]{:S(2)}) collective-permute-start(f32[256,256]{1,0:T(8,128)S(1)} %get-tuple-element.69), channel_id=1, source_target_pairs={{0,8},{4,12},{8,0},{12,4},{16,24},{20,28},{24,16},{28,20},{1,9},{5... | collective-permute-start | bytes 786440 | tf_op jit(solution)/shard_map/ppermute | solution.py:433
  60.2 20.9 %collective-permute-start.11 = (f32[256,256]{1,0:T(8,128)S(1)}, f32[256,256]{1,0:T(8,128)S(1)}, u32[]{:S(2)}, u32[]{:S(2)}) collective-permute-start(f32[256,256]{1,0:T(8,128)S(1)} %get-tuple-element.70), channel_id=1, source_target_pairs={{0,12},{4,8},{8,4},{12,0},{16,28},{20,24},{24,20},{28,16},{1,13},{... | collective-permute-start | bytes 786440 | tf_op jit(solution)/shard_map/ppermute | solution.py:433
  62.2 19.0 %collective-permute-start.9 = (f32[256,256]{1,0:T(8,128)S(1)}, f32[256,256]{1,0:T(8,128)S(1)}, u32[]{:S(2)}, u32[]{:S(2)}) collective-permute-start(f32[256,256]{1,0:T(8,128)S(1)} %get-tuple-element.68), channel_id=1, source_target_pairs={{0,4},{4,0},{8,12},{12,8},{16,20},{20,16},{24,28},{28,24},{1,5},{5... | collective-permute-start | bytes 786440 | tf_op jit(solution)/shard_map/ppermute | solution.py:433
  77.6 8.4 %collective-permute-start.14 = (f32[256,256]{1,0:T(8,128)S(1)}, f32[256,256]{1,0:T(8,128)S(1)}, u32[]{:S(2)}, u32[]{:S(2)}) collective-permute-start(f32[256,256]{1,0:T(8,128)S(1)} %get-tuple-element.79), channel_id=1, source_target_pairs={{0,4},{4,0},{8,12},{12,8},{16,20},{20,16},{24,28},{28,24},{1,5},{5... | collective-permute-start | bytes 786440 | tf_op jit(solution)/shard_map/ppermute | solution.py:433
  77.7 9.1 %collective-permute-start.15 = (f32[256,256]{1,0:T(8,128)S(1)}, f32[256,256]{1,0:T(8,128)S(1)}, u32[]{:S(2)}, u32[]{:S(2)}) collective-permute-start(f32[256,256]{1,0:T(8,128)S(1)} %get-tuple-element.80), channel_id=1, source_target_pairs={{0,8},{4,12},{8,0},{12,4},{16,24},{20,28},{24,16},{28,20},{1,9},{5... | collective-permute-start | bytes 786440 | tf_op jit(solution)/shard_map/ppermute | solution.py:433
  79.3 13.5 %collective-permute-start.13 = (f32[256,256]{1,0:T(8,128)S(1)}, f32[256,256]{1,0:T(8,128)S(1)}, u32[]{:S(2)}, u32[]{:S(2)}) collective-permute-start(f32[256,256]{1,0:T(8,128)S(1)} %get-tuple-element.77), channel_id=1, source_target_pairs={{0,12},{4,8},{8,4},{12,0},{16,28},{20,24},{24,20},{28,16},{1,13},{... | collective-permute-start | bytes 786440 | tf_op jit(solution)/shard_map/ppermute | solution.py:433

commit v5 on v4

--- a/solution.py
+++ b/solution.py
@@ -22,12 +22,12 @@
 
 def stacked_state(value):
     high, low = parts_of(value)
-    return jnp.concatenate([high, low, high, low], axis=0)
+    return jnp.concatenate([high, low, high], axis=0)
 
 
 def stacked_table(value):
     high, low = parts_of(value)
-    return jnp.concatenate([high, high, low, low], axis=1)
+    return jnp.concatenate([high, high, low], axis=1)
 
 
 def kind_masks(kinds_row, rows):
@@ -307,66 +307,61 @@
         target[...] = source[first + (place[0] ^ k)]
 
 
-def keep(place, turn, olds, targets):
-    if olds:
-        @pl.when(place[1] != turn)
-        def passed():
-            for old, target in zip(olds, targets):
-                target[...] = old[...]
-
-
-def chain_forward_kernel(turn, layers, tracers, place, inflow, table, m0, m1, m2, m3, *rest):
-    olds, (states, o0, o1, o2, o3, outflow, blocks, entering) = rest[:-8], rest[-8:]
-    outs = (o0, o1, o2, o3)
+def chain_forward_kernel(turn, layers, tracers, place, inflow, table, *rest):
+    if turn == 0:
+        *messages, states, entering, outflow, blocks = rest
+        take(place, messages, blocks)
+    else:
+        blocks, states, entering, outflow = rest
 
     @pl.when(place[1] == turn)
     def active():
-        take(place, (m0, m1, m2, m3), blocks)
         entering[0] = inflow[...] if turn > 0 else jnp.zeros(inflow.shape, F32)
         forward_chain(turn, layers, tracers, table, blocks, entering, states)
         outflow[...] = entering[MEMBERS]
-        give(place, outs, entering, 0)
-
-    keep(place, turn, olds, outs)
 
 
 def chain_last_kernel(
-    turn, layers, tracers, place, inflow, up_table, down_table, m0, m1, m2, m3, e0, e1, e2, e3, *rest
+    turn, layers, tracers, place, inflow, up_table, down_table, blocks, e0, e1, e2, e3,
+    entering, returning, outflow, terms, held,
 ):
-    olds, (o0, o1, o2, o3, h0, h1, h2, h3, outflow, blocks, terms, entering, returning, held) = rest[:-14], rest[-14:]
-    outs = (o0, o1, o2, o3)
+    take(place, (e0, e1, e2, e3), terms)
 
     @pl.when(place[1] == turn)
     def active():
-        take(place, (m0, m1, m2, m3), blocks)
-        take(place, (e0, e1, e2, e3), terms)
         entering[0] = inflow[...] if turn > 0 else jnp.zeros(inflow.shape, F32)
         forward_chain(turn, layers, tracers, up_table, blocks, entering, held)
         returning[MEMBERS] = jnp.zeros(inflow.shape, F32)
         backward_chain(turn, layers, tracers, down_table, blocks, terms, returning, held)
         outflow[...] = returning[0]
-        give(place, outs, entering, 0)
-        give(place, (h0, h1, h2, h3), returning, 1)
-
-    keep(place, turn, olds, outs)
-
-
-def chain_backward_kernel(
-    turn, layers, tracers, place, inflow, table, m0, m1, m2, m3, e0, e1, e2, e3, states, *rest
-):
-    olds, (o0, o1, o2, o3, outflow, blocks, terms, returning) = rest[:-8], rest[-8:]
-    outs = (o0, o1, o2, o3)
-
+
+
+def chain_backward_kernel(turn, layers, tracers, place, inflow, table, blocks, terms, states, returning, outflow):
     @pl.when(place[1] == turn)
     def active():
-        take(place, (m0, m1, m2, m3), blocks, returning.shape[1])
-        take(place, (e0, e1, e2, e3), terms)
         returning[MEMBERS] = inflow[...]
         backward_chain(turn, layers, tracers, table, blocks, terms, returning, states)
         outflow[...] = returning[0]
+
+
+def chain_first_kernel(layers, tracers, place, inflow, table, blocks, terms, states, *rest):
+    others, outs, returning = rest[: -MEMBERS - 1], rest[-MEMBERS - 1 : -1], rest[-1]
+
+    @pl.when(place[1] == 0)
+    def active():
+        returning[MEMBERS] = inflow[...]
+        backward_chain(0, layers, tracers, table, blocks, terms, returning, states)
         give(place, outs, returning, 1)
 
-    keep(place, turn, olds, outs)
+    give_kernel(1, 1, place, *others, *outs)
+
+
+def give_kernel(first, turn, place, *rest):
+    sources, outs = rest[:-MEMBERS], rest[-MEMBERS:]
+    for at, source in enumerate(sources):
+        @pl.when(place[1] == turn + at)
+        def mine():
+            give(place, outs, source, first)
 
 
 def final_forward_kernel(place, f_in, meta, table, m0, m1, m2, m3, f_out, state):
@@ -424,9 +419,9 @@
     vmem, anywhere, smem = (pl.BlockSpec(memory_space=s) for s in (pltpu.VMEM, pl.ANY, pltpu.SMEM))
     full = functools.partial(jax.ShapeDtypeStruct, dtype=F32)
     field = 4 * rhs.size
-    product = 2 * KINDS * dofs * 4 * dofs * tracers * columns
+    product = 2 * KINDS * dofs * 3 * dofs * tracers * columns
     some = 12 << 20
-    table_shape = (KINDS * dofs, 4 * dofs)
+    table_shape = (KINDS * dofs, 3 * dofs)
     fix = full((dofs, 128))
 
     def sent(value, k):
@@ -435,9 +430,9 @@
     def exchanged(messages):
         return [sent(value, k) for k, value in enumerate(messages)]
 
-    def between(values, step):
-        pairs = [(step * MEMBERS + i, (step + 1) * MEMBERS + i) for i in range(MEMBERS)]
-        return lax.ppermute(values, "stream", pairs + [(b, a) for a, b in pairs])
+    def between(values, source, target):
+        pairs = [(source * MEMBERS + i, target * MEMBERS + i) for i in range(MEMBERS)]
+        return lax.ppermute(values, "stream", pairs)
 
     piece = (layers, tracers, dofs, width)
     early, late = tuple(range(MEMBERS - 1)), (MEMBERS - 1,)
@@ -453,7 +448,7 @@
         ),
         in_specs=[smem] + [anywhere] * len(inputs),
         out_specs=(vmem,) * 5,
-        scratch_shapes=[pltpu.VMEM((dofs, 4 * dofs), BF16)]
+        scratch_shapes=[pltpu.VMEM((dofs, 3 * dofs), BF16)]
         + [pltpu.VMEM(value.shape, value.dtype) for value in inputs]
         + [pltpu.SemaphoreType.DMA((2 * layers + 6,))],
         name="span_terms",
@@ -493,47 +488,70 @@
     in_e = exchanged(out_e)
     in_b, _ = lax.optimization_barrier((in_b, out_e))
 
-    blocks = pltpu.VMEM((MEMBERS, long_rows, width), F32)
-    inner = pltpu.VMEM((MEMBERS + 1, rows, width), F32)
+    blocks = full((MEMBERS, long_rows, width))
+    terms = full((MEMBERS, rows, width))
+    flows = full((MEMBERS + 1, rows, width))
     held = (MEMBERS, layers, rows, width)
     inflow = out_e[0]
-    states, out_f = [], []
+    states, entering, returning = [], [], []
+    gathered = in_b
     for turn in range(groups - 1):
-        state, *out_f, outflow = pl.pallas_call(
+        state, entered, outflow, *block_values = pl.pallas_call(
             functools.partial(chain_forward_kernel, turn, layers, tracers),
-            out_shape=(full(held),) + (message,) * (MEMBERS + 1),
-            in_specs=[smem] + [vmem] * (2 + MEMBERS + len(out_f)),
-            out_specs=(vmem,) * (MEMBERS + 2),
-            scratch_shapes=[blocks, inner],
+            out_shape=(full(held), flows, message) + (blocks,) * (turn == 0),
+            in_specs=[smem] + [vmem] * (2 + len(gathered)),
+            out_specs=(vmem,) * (4 if turn == 0 else 3),
             name=f"chain_forward_{turn}",
-            **params(1 << 10, 1 << 10, some + field),
-        )(place, inflow, up_table, *in_b, *out_f)
+            **params(layers * product, 2 * field, some + 2 * field),
+        )(place, inflow, up_table, *gathered)
+        if turn == 0:
+            gathered = block_values
         states.append(state)
-        inflow = between(outflow, turn)
-
-    *out_f, h0, h1, h2, h3, outflow = pl.pallas_call(
+        entering.append(entered)
+        inflow = between(outflow, turn, turn + 1)
+
+    entered, returned, outflow, terms = pl.pallas_call(
         functools.partial(chain_last_kernel, groups - 1, layers, tracers),
-        out_shape=(message,) * (2 * MEMBERS + 1),
-        in_specs=[smem] + [vmem] * (3 + 2 * MEMBERS + len(out_f)),
-        out_specs=(vmem,) * (2 * MEMBERS + 1),
-        scratch_shapes=[blocks, inner, inner, inner, pltpu.VMEM(held, F32)],
+        out_shape=(flows, flows, message, terms),
+        in_specs=[smem] + [vmem] * (4 + MEMBERS),
+        out_specs=(vmem,) * 4,
+        scratch_shapes=[pltpu.VMEM(held, F32)],
         name="chain_last",
-        **params(1 << 10, 1 << 10, some + 2 * field),
-    )(place, inflow, up_table, down_table, *in_b, *in_e, *out_f)
+        **params(2 * layers * product, 2 * field, some + 2 * field),
+    )(place, inflow, up_table, down_table, *gathered, *in_e)
+    entering.append(entered)
+    returning.insert(0, returned)
+    out_f = pl.pallas_call(
+        functools.partial(give_kernel, 0, 0),
+        out_shape=(message,) * MEMBERS,
+        in_specs=[smem] + [vmem] * groups,
+        out_specs=(vmem,) * MEMBERS,
+        name="give_forward",
+        **params(1 << 10, 1 << 10, some),
+    )(place, *entering)
     in_f = exchanged(out_f)
-    out_h = [h0, h1, h2, h3]
-
-    for turn in reversed(range(groups - 1)):
-        inflow = between(outflow, turn)
-        *out_h, outflow = pl.pallas_call(
+
+    for turn in reversed(range(1, groups - 1)):
+        inflow = between(outflow, turn + 1, turn)
+        returned, outflow = pl.pallas_call(
             functools.partial(chain_backward_kernel, turn, layers, tracers),
-            out_shape=(message,) * (MEMBERS + 1),
-            in_specs=[smem] + [vmem] * (3 + 3 * MEMBERS),
-            out_specs=(vmem,) * (MEMBERS + 1),
-            scratch_shapes=[blocks, inner, inner],
+            out_shape=(flows, message),
+            in_specs=[smem] + [vmem] * 5,
+            out_specs=(vmem,) * 2,
             name=f"chain_backward_{turn}",
-            **params(1 << 10, 1 << 10, some + field),
-        )(place, inflow, down_table, *in_b, *in_e, states[turn], *out_h)
+            **params(layers * product, 2 * field, some + field),
+        )(place, inflow, down_table, *gathered, terms, states[turn])
+        returning.insert(0, returned)
+    inflow = between(outflow, 1, 0)
+    out_h = pl.pallas_call(
+        functools.partial(chain_first_kernel, layers, tracers),
+        out_shape=(message,) * MEMBERS,
+        in_specs=[smem] + [vmem] * (5 + len(returning)),
+        out_specs=(vmem,) * MEMBERS,
+        scratch_shapes=[pltpu.VMEM(flows.shape, F32)],
+        name="chain_backward_0",
+        **params(layers * product, 2 * field, some + field),
+    )(place, inflow, down_table, *gathered, terms, states[0], *returning)
     in_h = exchanged(out_h)
 
     f_part = pl.pallas_call(

time: 95.4 us -> 93.7 us (0.982)
  starting transfers between devices: 29.7 us -> 19.4 us
  waiting for transfers between devices: 26.6 us -> 35.8 us
    ppermute x2, waiting for transfers between devices: 11.4 us -> 24.6 us  [between(): return lax.ppermute(values, 'stream', pairs)]
    ppermute x2, starting transfers between devices: 13.3 us -> 2.9 us  [between(): return lax.ppermute(values, 'stream', pairs)]
    ppermute x12, waiting for transfers between devices: 15.2 us -> 11.2 us  [sent(): lax.ppermute(value, 'stream', [(i, i ^ k) for i in range(count)])]
    pallas_call x1 -> x2, Pallas kernels: 5.24 us -> 4.98 us  [the longest x1 4.36 us: per_device(): pl.pallas_call(functools.partial(chain_first_kernel, layers, tracers), ou...]
where the time goes in v5:
time: 93.7 us; the launch traced here: 93.5 us
  Pallas kernels  37.9 us (40%)
  waiting for transfers between devices  35.8 us (38%)
  starting transfers between devices  19.4 us (21%)
    ppermute x2, waiting for transfers between devices, between(): return lax.ppermute(values, 'stream', pairs)  24.6 us
    ppermute x12, starting transfers between devices, sent(): lax.ppermute(value, 'stream', [(i, i ^ k) for i in range(count)])  15.2 us
    ppermute x12, waiting for transfers between devices, sent(): lax.ppermute(value, 'stream', [(i, i ^ k) for i in range(count)])  11.2 us
    pallas_call x1, Pallas kernels, per_device(): pl.pallas_call(span_kernel, out_shape=(full(rhs.shape), full((4 * layers,...  8.91 us
    pallas_call x2, Pallas kernels, per_device(): pl.pallas_call(functools.partial(final_backward_kernel, ks), out_shape=fu...  5.7 us
    pallas_call x1, Pallas kernels, per_device(): pl.pallas_call(local_backward_kernel, out_shape=(table,) + (message,) * M...  5.42 us
    pallas_call x1, Pallas kernels, per_device(): pl.pallas_call(functools.partial(chain_first_kernel, layers, tracers), ou...  4.36 us
    pallas_call x1, Pallas kernels, per_device(): pl.pallas_call(final_forward_kernel, out_shape=full((MEMBERS, *piece)), i...  4.27 us
  transfers between devices with their start and end apart: 16, of which 8 were waited for; matrix products, arithmetic and copies ran while one was open for 0% of the time, Pallas kernels for 24%

profile of v5, /device:TPU:0, one launch (start us, length us, event | category | flops | bytes accessed | tf_op | source)
XLA Modules:
  0.0 93.5 jit_solution(6618048029310024779)
XLA Ops:
  0.0 0.1 pad_add_fusion.place
  0.1 8.9 %span_terms.1 = (f32[4,4,64,1024]{3,2,1,0:T(8,128)S(1)}, f32[16,1024]{1,0:T(8,128)S(1)}, f32[8,128]{1,0:T(8,128)S(1)}, f32[64,128]{1,0:T(8,128)S(1)}, bf16[384,192]{1,0:T(8,128)(2,1)S(1)}) custom-call(s32[3]{0:T(128)S(1)} %pad_add_fusion.place, f32[4,4,64,1024]{3,2,1,0:T(8,128)} %rhs.1, f32[4,4,64,1024]{3,2,1,0:T(8,128)} %lagged.1, s32[3,4,1024]{2,1,0:T(4,128)} %kinds.1, ...), custom_call_target="tpu_custom_call" | custom-call | flops 1024 | bytes 1024 | tf_op jit(solution)/shard_map/span_terms/pallas_call | solution.py:444
  9.0 0.5 collective-permute-start
  9.5 0.8 collective-permute-start.1
  10.4 3.8 %local_forward.1 = (f32[4,4,64,1024]{3,2,1,0:T(8,128)S(1)}, f32[272,256]{1,0:T(8,128)S(1)}, f32[272,256]{1,0:T(8,128)S(1)}, f32[272,256]{1,0:T(8,128)S(1)}, f32[272,256]{1,0:T(8,128)S(1)}) custom-call(s32[3]{0:T(128)S(1)} %pad_add_fusion.place, f32[64,128]{1,0:T(8,128)S(1)} %collective-permute-done.pair, f32[64,128]{1,0:T(8,128)S(1)} %collective-permute-done.1.cross, ...), custom_call_target="tpu_custom_call" | custom-call | flops 1024 | bytes 1024 | tf_op jit(solution)/shard_map/local_forward/pallas_call | solution.py:466
  14.1 2.9 %collective-permute-start.2 = (f32[272,256]{1,0:T(8,128)S(1)}, f32[272,256]{1,0:T(8,128)S(1)}, u32[]{:S(2)}, u32[]{:S(2)}) collective-permute-start(f32[272,256]{1,0:T(8,128)S(1)} %get-tuple-element.48), channel_id=1, source_target_pairs={{0,4},{4,0},{8,12},{12,8},{16,20},{20,16},{24,28},{28,24},{1,5},{5... | collective-permute-start | bytes 835592 | tf_op jit(solution)/shard_map/ppermute | solution.py:428
  17.1 1.6 %collective-permute-start.3 = (f32[272,256]{1,0:T(8,128)S(1)}, f32[272,256]{1,0:T(8,128)S(1)}, u32[]{:S(2)}, u32[]{:S(2)}) collective-permute-start(f32[272,256]{1,0:T(8,128)S(1)} %get-tuple-element.49), channel_id=1, source_target_pairs={{0,8},{4,12},{8,0},{12,4},{16,24},{20,28},{24,16},{28,20},{1,9},{5... | collective-permute-start | bytes 835592 | tf_op jit(solution)/shard_map/ppermute | solution.py:428
  18.7 5.4 %local_backward.1 = (bf16[384,192]{1,0:T(8,128)(2,1)S(1)}, f32[256,256]{1,0:T(8,128)S(1)}, f32[256,256]{1,0:T(8,128)S(1)}, f32[256,256]{1,0:T(8,128)S(1)}, f32[256,256]{1,0:T(8,128)S(1)}) custom-call(s32[3]{0:T(128)S(1)} %pad_add_fusion.place, f32[4,4,64,1024]{3,2,1,0:T(8,128)S(1)} %get-tuple-element.45.f_in, f32[16,1024]{1,0:T(8,128)S(1)} %get-tuple-element.42.meta, ...), custom_call_target="tpu_custom_call" | custom-call | flops 1024 | bytes 1024 | tf_op jit(solution)/shard_map/local_backward/pallas_call | solution.py:476
  24.1 2.0 %collective-permute-start.6 = (f32[256,256]{1,0:T(8,128)S(1)}, f32[256,256]{1,0:T(8,128)S(1)}, u32[]{:S(2)}, u32[]{:S(2)}) collective-permute-start(f32[256,256]{1,0:T(8,128)S(1)} %get-tuple-element.51), channel_id=1, source_target_pairs={{0,4},{4,0},{8,12},{12,8},{16,20},{20,16},{24,28},{28,24},{1,5},{5... | collective-permute-start | bytes 786440 | tf_op jit(solution)/shard_map/ppermute | solution.py:428
  26.1 1.6 %collective-permute-start.7 = (f32[256,256]{1,0:T(8,128)S(1)}, f32[256,256]{1,0:T(8,128)S(1)}, u32[]{:S(2)}, u32[]{:S(2)}) collective-permute-start(f32[256,256]{1,0:T(8,128)S(1)} %get-tuple-element.52), channel_id=1, source_target_pairs={{0,8},{4,12},{8,0},{12,4},{16,24},{20,28},{24,16},{28,20},{1,9},{5... | collective-permute-start | bytes 786440 | tf_op jit(solution)/shard_map/ppermute | solution.py:428
  27.7 0.8 collective-permute-done.4.rest_3_
  28.5 4.2 %chain_forward_0.1 = (f32[4,4,256,256]{3,2,1,0:T(8,128)S(1)}, f32[5,256,256]{2,1,0:T(8,128)S(1)}, f32[256,256]{1,0:T(8,128)S(1)}, f32[4,272,256]{2,1,0:T(8,128)S(1)}) custom-call(s32[3]{0:T(128)S(1)} %pad_add_fusion.place, f32[256,256]{1,0:T(8,128)S(1)} %get-tuple-element.46.inflow.e0, bf16[384,192]{1,0:T(8,128)(2,1)S(1)} %get-tuple-element.44.table.up_table, ...), custom_call_target="tpu_custom_call" | custom-call | flops 2415919104 | bytes 8388608 | tf_op jit(solution)/shard_map/chain_forward_0/pallas_call | solution.py:499
  32.7 1.6 %collective-permute-start.5 = (f32[256,256]{1,0:T(8,128)S(1)}, f32[256,256]{1,0:T(8,128)S(1)}, u32[]{:S(2)}, u32[]{:S(2)}) collective-permute-start(f32[256,256]{1,0:T(8,128)S(1)} %get-tuple-element.59), channel_id=1, source_target_pairs={{0,16},{4,20},{8,24},{12,28},{1,17},{5,21},{9,25},{13,29},{2,18},{... | collective-permute-start | bytes 786440 | tf_op jit(solution)/shard_map/ppermute | solution.py:435
  34.3 1.9 %collective-permute-done.6.e1 = f32[256,256]{1,0:T(8,128)S(1)} collective-permute-done((f32[256,256]{1,0:T(8,128)S(1)}, f32[256,256]{1,0:T(8,128)S(1)}, u32[]{:S(2)}, u32[]{:S(2)}) %collective-permute-start.6) | collective-permute-done | bytes 262176 | tf_op jit(solution)/shard_map/ppermute | solution.py:428
  36.2 4.3 %collective-permute-done.8.e3 = f32[256,256]{1,0:T(8,128)S(1)} collective-permute-done((f32[256,256]{1,0:T(8,128)S(1)}, f32[256,256]{1,0:T(8,128)S(1)}, u32[]{:S(2)}, u32[]{:S(2)}) %collective-permute-start.8) | collective-permute-done | bytes 262176 | tf_op jit(solution)/shard_map/ppermute | solution.py:428
  40.5 5.2 %collective-permute-done.5.inflow = f32[256,256]{1,0:T(8,128)S(1)} collective-permute-done((f32[256,256]{1,0:T(8,128)S(1)}, f32[256,256]{1,0:T(8,128)S(1)}, u32[]{:S(2)}, u32[]{:S(2)}) %collective-permute-start.5) | collective-permute-done | bytes 262176 | tf_op jit(solution)/shard_map/ppermute | solution.py:435
  45.7 0.6 chain_last.1
  46.3 1.3 %collective-permute-start.12 = (f32[256,256]{1,0:T(8,128)S(1)}, f32[256,256]{1,0:T(8,128)S(1)}, u32[]{:S(2)}, u32[]{:S(2)}) collective-permute-start(f32[256,256]{1,0:T(8,128)S(1)} %get-tuple-element.67), channel_id=1, source_target_pairs={{16,0},{20,4},{24,8},{28,12},{17,1},{21,5},{25,9},{29,13},{18,2},{... | collective-permute-start | bytes 786440 | tf_op jit(solution)/shard_map/ppermute | solution.py:435
  47.6 0.6 give_forward.1
  48.2 0.1 collective-permute-start.10
  48.3 1.9 %collective-permute-start.11 = (f32[256,256]{1,0:T(8,128)S(1)}, f32[256,256]{1,0:T(8,128)S(1)}, u32[]{:S(2)}, u32[]{:S(2)}) collective-permute-start(f32[256,256]{1,0:T(8,128)S(1)} %get-tuple-element.66), channel_id=1, source_target_pairs={{0,12},{4,8},{8,4},{12,0},{16,28},{20,24},{24,20},{28,16},{1,13},{... | collective-permute-start | bytes 786440 | tf_op jit(solution)/shard_map/ppermute | solution.py:428
  50.2 1.5 %collective-permute-start.9 = (f32[256,256]{1,0:T(8,128)S(1)}, f32[256,256]{1,0:T(8,128)S(1)}, u32[]{:S(2)}, u32[]{:S(2)}) collective-permute-start(f32[256,256]{1,0:T(8,128)S(1)} %get-tuple-element.64), channel_id=1, source_target_pairs={{0,4},{4,0},{8,12},{12,8},{16,20},{20,16},{24,28},{28,24},{1,5},{5... | collective-permute-start | bytes 786440 | tf_op jit(solution)/shard_map/ppermute | solution.py:428
  51.8 19.4 %collective-permute-done.12.inflow = f32[256,256]{1,0:T(8,128)S(1)} collective-permute-done((f32[256,256]{1,0:T(8,128)S(1)}, f32[256,256]{1,0:T(8,128)S(1)}, u32[]{:S(2)}, u32[]{:S(2)}) %collective-permute-start.12) | collective-permute-done | bytes 262176 | tf_op jit(solution)/shard_map/ppermute | solution.py:435
  71.2 4.4 %chain_backward_0.1 = (f32[256,256]{1,0:T(8,128)S(1)}, f32[256,256]{1,0:T(8,128)S(1)}, f32[256,256]{1,0:T(8,128)S(1)}, f32[256,256]{1,0:T(8,128)S(1)}) custom-call(s32[3]{0:T(128)S(1)} %pad_add_fusion.place, f32[256,256]{1,0:T(8,128)S(1)} %collective-permute-done.12.inflow, bf16[384,192]{1,0:T(8,128)(2,1)S(1)} %get-tuple-element.60.down_table.table, ...), custom_call_target="tpu_custom_call" | custom-call | flops 2415919104 | bytes 8388608 | tf_op jit(solution)/shard_map/chain_backward_0/pallas_call | solution.py:546
  75.5 1.5 %collective-permute-start.14 = (f32[256,256]{1,0:T(8,128)S(1)}, f32[256,256]{1,0:T(8,128)S(1)}, u32[]{:S(2)}, u32[]{:S(2)}) collective-permute-start(f32[256,256]{1,0:T(8,128)S(1)} %get-tuple-element.73), channel_id=1, source_target_pairs={{0,4},{4,0},{8,12},{12,8},{16,20},{20,16},{24,28},{28,24},{1,5},{5... | collective-permute-start | bytes 786440 | tf_op jit(solution)/shard_map/ppermute | solution.py:428
  77.0 2.1 %collective-permute-start.13 = (f32[256,256]{1,0:T(8,128)S(1)}, f32[256,256]{1,0:T(8,128)S(1)}, u32[]{:S(2)}, u32[]{:S(2)}) collective-permute-start(f32[256,256]{1,0:T(8,128)S(1)} %get-tuple-element.71), channel_id=1, source_target_pairs={{0,12},{4,8},{8,4},{12,0},{16,28},{20,24},{24,20},{28,16},{1,13},{... | collective-permute-start | bytes 786440 | tf_op jit(solution)/shard_map/ppermute | solution.py:428
  79.1 4.3 %final_forward.1.f_in = f32[4,4,4,64,256]{4,3,2,1,0:T(8,128)S(1)} custom-call(s32[3]{0:T(128)S(1)} %pad_add_fusion.place, f32[4,4,64,1024]{3,2,1,0:T(8,128)S(1)} %get-tuple-element.45.f_in, f32[16,1024]{1,0:T(8,128)S(1)} %get-tuple-element.42.meta, bf16[384,192]{1,0:T(8,128)(2,1)S(1)} %get-tuple-element.44.table.up_table, ...), custom_call_target="tpu_custom_call" | custom-call | flops 1024 | bytes 1024 | tf_op jit(solution)/shard_map/final_forward/pallas_call | solution.py:557
  83.4 0.9 collective-permute-done.14.rest_1_
  84.3 1.9 %collective-permute-done.15.rest_2_ = f32[256,256]{1,0:T(8,128)S(1)} collective-permute-done((f32[256,256]{1,0:T(8,128)S(1)}, f32[256,256]{1,0:T(8,128)S(1)}, u32[]{:S(2)}, u32[]{:S(2)}) %collective-permute-start.15) | collective-permute-done | bytes 262176 | tf_op jit(solution)/shard_map/ppermute | solution.py:428
  86.2 3.5 %final_backward_0.1.rest_1_ = f32[4,4,64,1024]{3,2,1,0:T(8,128)} custom-call(s32[3]{0:T(128)S(1)} %pad_add_fusion.place, f32[4,4,4,64,256]{4,3,2,1,0:T(8,128)S(1)} %final_forward.1.f_in, f32[16,1024]{1,0:T(8,128)S(1)} %get-tuple-element.42.meta, bf16[384,192]{1,0:T(8,128)(2,1)S(1)} %get-tuple-element.60.down_table.table, ...), custom_call_target="tpu_custom_call" | custom-call | flops 1024 | bytes 1024 | tf_op jit(solution)/shard_map/final_backward_0/pallas_call | solution.py:569
  89.7 1.5 %collective-permute-done.13.rest_0_ = f32[256,256]{1,0:T(8,128)S(1)} collective-permute-done((f32[256,256]{1,0:T(8,128)S(1)}, f32[256,256]{1,0:T(8,128)S(1)}, u32[]{:S(2)}, u32[]{:S(2)}) %collective-permute-start.13) | collective-permute-done | bytes 262176 | tf_op jit(solution)/shard_map/ppermute | solution.py:428
  91.1 2.2 %final_backward_3.1 = f32[4,4,64,1024]{3,2,1,0:T(8,128)} custom-call(s32[3]{0:T(128)S(1)} %pad_add_fusion.place, f32[4,4,4,64,256]{4,3,2,1,0:T(8,128)S(1)} %final_forward.1.f_in, f32[16,1024]{1,0:T(8,128)S(1)} %get-tuple-element.42.meta, bf16[384,192]{1,0:T(8,128)(2,1)S(1)} %get-tuple-element.60.down_table.table, ...), custom_call_target="tpu_custom_call", output_to_operand_aliasing={{}: (5, {})} | custom-call | flops 1024 | bytes 1024 | tf_op jit(solution)/shard_map/final_backward_3/pallas_call | solution.py:569
  (11 shorter events, 0.0 us)
Async XLA Ops:
  9.0 1.4 %collective-permute-start = (f32[64,128]{1,0:T(8,128)S(1)}, f32[64,128]{1,0:T(8,128)S(1)}, u32[]{:S(2)}, u32[]{:S(2)}) collective-permute-start(f32[64,128]{1,0:T(8,128)S(1)} %get-tuple-element.40), channel_id=1, source_target_pairs={{0,1},{1,0},{2,3},{3,2},{4,5},{5,4},{6,7},{7,6},{8,9},{9,8},{10,11... | collective-permute-start | bytes 98312 | tf_op jit(solution)/shard_map/ppermute | solution.py:460
  9.5 0.9 collective-permute-start.1
  14.1 13.5 %collective-permute-start.2 = (f32[272,256]{1,0:T(8,128)S(1)}, f32[272,256]{1,0:T(8,128)S(1)}, u32[]{:S(2)}, u32[]{:S(2)}) collective-permute-start(f32[272,256]{1,0:T(8,128)S(1)} %get-tuple-element.48), channel_id=1, source_target_pairs={{0,4},{4,0},{8,12},{12,8},{16,20},{20,16},{24,28},{28,24},{1,5},{5... | collective-permute-start | bytes 835592 | tf_op jit(solution)/shard_map/ppermute | solution.py:428
  17.1 10.6 %collective-permute-start.3 = (f32[272,256]{1,0:T(8,128)S(1)}, f32[272,256]{1,0:T(8,128)S(1)}, u32[]{:S(2)}, u32[]{:S(2)}) collective-permute-start(f32[272,256]{1,0:T(8,128)S(1)} %get-tuple-element.49), channel_id=1, source_target_pairs={{0,8},{4,12},{8,0},{12,4},{16,24},{20,28},{24,16},{28,20},{1,9},{5... | collective-permute-start | bytes 835592 | tf_op jit(solution)/shard_map/ppermute | solution.py:428
  18.7 9.8 %collective-permute-start.4 = (f32[272,256]{1,0:T(8,128)S(1)}, f32[272,256]{1,0:T(8,128)S(1)}, u32[]{:S(2)}, u32[]{:S(2)}) collective-permute-start(f32[272,256]{1,0:T(8,128)S(1)} %get-tuple-element.50), channel_id=1, source_target_pairs={{0,12},{4,8},{8,4},{12,0},{16,28},{20,24},{24,20},{28,16},{1,13},{... | collective-permute-start | bytes 835592 | tf_op jit(solution)/shard_map/ppermute | solution.py:428
  24.1 12.1 %collective-permute-start.6 = (f32[256,256]{1,0:T(8,128)S(1)}, f32[256,256]{1,0:T(8,128)S(1)}, u32[]{:S(2)}, u32[]{:S(2)}) collective-permute-start(f32[256,256]{1,0:T(8,128)S(1)} %get-tuple-element.51), channel_id=1, source_target_pairs={{0,4},{4,0},{8,12},{12,8},{16,20},{20,16},{24,28},{28,24},{1,5},{5... | collective-permute-start | bytes 786440 | tf_op jit(solution)/shard_map/ppermute | solution.py:428
  26.1 10.1 %collective-permute-start.7 = (f32[256,256]{1,0:T(8,128)S(1)}, f32[256,256]{1,0:T(8,128)S(1)}, u32[]{:S(2)}, u32[]{:S(2)}) collective-permute-start(f32[256,256]{1,0:T(8,128)S(1)} %get-tuple-element.52), channel_id=1, source_target_pairs={{0,8},{4,12},{8,0},{12,4},{16,24},{20,28},{24,16},{28,20},{1,9},{5... | collective-permute-start | bytes 786440 | tf_op jit(solution)/shard_map/ppermute | solution.py:428
  27.7 12.8 %collective-permute-start.8 = (f32[256,256]{1,0:T(8,128)S(1)}, f32[256,256]{1,0:T(8,128)S(1)}, u32[]{:S(2)}, u32[]{:S(2)}) collective-permute-start(f32[256,256]{1,0:T(8,128)S(1)} %get-tuple-element.53), channel_id=1, source_target_pairs={{0,12},{4,8},{8,4},{12,0},{16,28},{20,24},{24,20},{28,16},{1,13},{... | collective-permute-start | bytes 786440 | tf_op jit(solution)/shard_map/ppermute | solution.py:428
  32.7 13.0 %collective-permute-start.5 = (f32[256,256]{1,0:T(8,128)S(1)}, f32[256,256]{1,0:T(8,128)S(1)}, u32[]{:S(2)}, u32[]{:S(2)}) collective-permute-start(f32[256,256]{1,0:T(8,128)S(1)} %get-tuple-element.59), channel_id=1, source_target_pairs={{0,16},{4,20},{8,24},{12,28},{1,17},{5,21},{9,25},{13,29},{2,18},{... | collective-permute-start | bytes 786440 | tf_op jit(solution)/shard_map/ppermute | solution.py:435
  46.3 24.9 %collective-permute-start.12 = (f32[256,256]{1,0:T(8,128)S(1)}, f32[256,256]{1,0:T(8,128)S(1)}, u32[]{:S(2)}, u32[]{:S(2)}) collective-permute-start(f32[256,256]{1,0:T(8,128)S(1)} %get-tuple-element.67), channel_id=1, source_target_pairs={{16,0},{20,4},{24,8},{28,12},{17,1},{21,5},{25,9},{29,13},{18,2},{... | collective-permute-start | bytes 786440 | tf_op jit(solution)/shard_map/ppermute | solution.py:435
  48.2 28.8 %collective-permute-start.10 = (f32[256,256]{1,0:T(8,128)S(1)}, f32[256,256]{1,0:T(8,128)S(1)}, u32[]{:S(2)}, u32[]{:S(2)}) collective-permute-start(f32[256,256]{1,0:T(8,128)S(1)} %get-tuple-element.65), channel_id=1, source_target_pairs={{0,8},{4,12},{8,0},{12,4},{16,24},{20,28},{24,16},{28,20},{1,9},{5... | collective-permute-start | bytes 786440 | tf_op jit(solution)/shard_map/ppermute | solution.py:428
  48.3 30.8 %collective-permute-start.11 = (f32[256,256]{1,0:T(8,128)S(1)}, f32[256,256]{1,0:T(8,128)S(1)}, u32[]{:S(2)}, u32[]{:S(2)}) collective-permute-start(f32[256,256]{1,0:T(8,128)S(1)} %get-tuple-element.66), channel_id=1, source_target_pairs={{0,12},{4,8},{8,4},{12,0},{16,28},{20,24},{24,20},{28,16},{1,13},{... | collective-permute-start | bytes 786440 | tf_op jit(solution)/shard_map/ppermute | solution.py:428
  50.2 28.9 %collective-permute-start.9 = (f32[256,256]{1,0:T(8,128)S(1)}, f32[256,256]{1,0:T(8,128)S(1)}, u32[]{:S(2)}, u32[]{:S(2)}) collective-permute-start(f32[256,256]{1,0:T(8,128)S(1)} %get-tuple-element.64), channel_id=1, source_target_pairs={{0,4},{4,0},{8,12},{12,8},{16,20},{20,16},{24,28},{28,24},{1,5},{5... | collective-permute-start | bytes 786440 | tf_op jit(solution)/shard_map/ppermute | solution.py:428
  75.5 8.7 %collective-permute-start.14 = (f32[256,256]{1,0:T(8,128)S(1)}, f32[256,256]{1,0:T(8,128)S(1)}, u32[]{:S(2)}, u32[]{:S(2)}) collective-permute-start(f32[256,256]{1,0:T(8,128)S(1)} %get-tuple-element.73), channel_id=1, source_target_pairs={{0,4},{4,0},{8,12},{12,8},{16,20},{20,16},{24,28},{28,24},{1,5},{5... | collective-permute-start | bytes 786440 | tf_op jit(solution)/shard_map/ppermute | solution.py:428
  77.0 9.1 %collective-permute-start.15 = (f32[256,256]{1,0:T(8,128)S(1)}, f32[256,256]{1,0:T(8,128)S(1)}, u32[]{:S(2)}, u32[]{:S(2)}) collective-permute-start(f32[256,256]{1,0:T(8,128)S(1)} %get-tuple-element.74), channel_id=1, source_target_pairs={{0,8},{4,12},{8,0},{12,4},{16,24},{20,28},{24,16},{28,20},{1,9},{5... | collective-permute-start | bytes 786440 | tf_op jit(solution)/shard_map/ppermute | solution.py:428
  77.0 14.1 %collective-permute-start.13 = (f32[256,256]{1,0:T(8,128)S(1)}, f32[256,256]{1,0:T(8,128)S(1)}, u32[]{:S(2)}, u32[]{:S(2)}) collective-permute-start(f32[256,256]{1,0:T(8,128)S(1)} %get-tuple-element.71), channel_id=1, source_target_pairs={{0,12},{4,8},{8,4},{12,0},{16,28},{20,24},{24,20},{28,16},{1,13},{... | collective-permute-start | bytes 786440 | tf_op jit(solution)/shard_map/ppermute | solution.py:428
